TPU v7x, 512 devices: a whole 4x4x16 slice. The times are simulated.
512 devices in a mesh: pipe: 4 (over y), ctx: 32 (over z, core), tp: 4 (over x).
Axes of the slice: x: 4, y: 4, z: 16, core: 2. Of those that a mesh axis runs over, the one named last changes fastest.
Arguments:
- hidden_in: bfloat16 [4, 4096, 4096], P('pipe', 'ctx', 'tp'), may hold values from -8 to 8
- doc_ids: int32 [4096], P('ctx'), may hold values from 0 to 3, never falling along the last dimension, each value on 1 to 2048 neighbouring positions
- layer_kind: int32 [4], P('pipe'), may hold values from 0 to 1, as said below
- norm_gain: float32 [4, 4096], P('pipe', 'tp'), may hold values from 0.5 to 1.5
- q_weight: bfloat16 [4, 4096, 4096], P('pipe', 'ctx', 'tp'), may hold values from -2 to 2
- k_weight: bfloat16 [4, 4096, 512], P('pipe', 'ctx', 'tp'), may hold values from -1 to 1
- v_weight: bfloat16 [4, 4096, 512], P('pipe', 'ctx', 'tp'), may hold values from -0.09375 to 0.09375
- bc_weight: bfloat16 [4, 4096, 32], P('pipe', 'tp'), may hold values from -0.046875 to 0.046875
- dt_weight: bfloat16 [4, 4096, 64], P('pipe', 'tp'), may hold values from -0.09375 to 0.09375
- dt_bias: float32 [4, 64], P('pipe', 'tp'), may hold values from -1 to 1
- decay_rate: float32 [4, 64], P('pipe', 'tp'), may hold values from 1.2207031e-05 to 0.05
- skip_gain: float32 [4, 64], P('pipe', 'tp'), may hold values from 0.5 to 1.5
Outputs:
- section_out: bfloat16 [4, 4096, 4096], P('pipe', 'ctx', 'tp')
- passed: bfloat16 [4, 4096, 4096], P('pipe', 'ctx', 'tp')
Inputs may be any that keep to these rules, and one draw needn't show every extreme that they name: `layer_kind`: every draw has at least one attention section and at least one state-space section.
All inputs are finite; a program needn't handle non-finite values.
Results may differ from a plain program's by a relative error of at most 0.011.
Values may be sent and summed in bfloat16 or wider, within the bound.
No kernel may reach another device: no remote copies, remote signals or barrier semaphores. Data moves between devices by JAX's collectives and lax.ppermute only.
A program may use at most 64 MiB of HBM per device.

v0:
```python
import jax
import jax.numpy as jnp
from jax import lax
from jax.sharding import PartitionSpec as P

D = 4096
HD = 128


def entering(x, axis, combine, identity):
    devices, index = (lax.axis_size(axis), lax.axis_index(axis))
    everything = jax.tree.map(
        lambda part, kind: lax.all_gather(part.astype(kind), axis), x, (jnp.bfloat16, jnp.bfloat16)
    )
    start = jax.tree.map(
        lambda part, zero: jnp.broadcast_to(jnp.asarray(zero, part.dtype), part.shape), x, identity
    )

    def turn(k, before):
        reached = k < index
        new = combine(
            before, jax.tree.map(lambda part, own: part[k].astype(own.dtype), everything, x)
        )
        return jax.tree.map(lambda a, b: jnp.where(reached, a, b), new, before)

    return lax.fori_loop(0, devices, turn, start)


def passed_along(x, axis, by):
    devices = lax.axis_size(axis)
    pairs = [(i, i + by) for i in range(devices) if 0 <= i + by < devices]
    return lax.ppermute(x, axis, pairs)


def make_fold(q_rows, q_pos, q_ids, ids_all, groups, head_size, active):
    rows = q_rows.shape[0]
    gsize = rows // groups
    q_top = jnp.max(q_pos.reshape(groups, gsize), axis=1)
    scale = head_size ** (-0.5)

    def update(state, piece_k, piece_v, key_pos, key_ids):
        top, denom, total = state
        scores = (
            jnp.einsum("tkjd,skd->kjts", q_rows, piece_k, preferred_element_type=jnp.float32)
            * scale
        )
        allowed = (key_pos[None, :] <= q_pos[:, None]) & (key_ids[None, :] == q_ids[:, None])
        scores = jnp.where(allowed[None, None], scores, -1e30)
        new_top = jnp.maximum(top, jnp.max(scores, axis=-1))
        probs = jnp.where(allowed[None, None], jnp.exp(scores - new_top[..., None]), 0.0)
        factor = jnp.exp(top - new_top)
        denom = denom * factor + jnp.sum(probs, axis=-1)
        total = total * factor[..., None] + jnp.einsum(
            "kjts,skd->kjtd",
            probs.astype(jnp.bfloat16),
            piece_v,
            preferred_element_type=jnp.float32,
        )
        return (new_top, denom, total)

    def fold(carry, piece, start):
        piece_k, piece_v = piece
        count = piece_k.shape[0]
        block = 512
        for offset in range(0, count, block):
            key_start = start + offset
            key_pos = key_start + jnp.arange(block)
            key_ids = lax.dynamic_slice_in_dim(ids_all, key_start, block)
            block_k = piece_k[offset : offset + block]
            block_v = piece_v[offset : offset + block]
            low = 0

            def compute(state, low=low):
                return update(state, block_k, block_v, key_pos, key_ids)

            wanted = jnp.logical_and(active, key_start <= q_top[0])
            updated = [lax.cond(wanted, compute, lambda state: state, carry[0])]
            carry = tuple(updated)
        return carry

    def initial(kv_count, group):
        return tuple(
            (
                (
                    jnp.full((kv_count, group, gsize), -1e30, jnp.float32),
                    jnp.zeros((kv_count, group, gsize), jnp.float32),
                    jnp.zeros((kv_count, group, gsize, head_size), jnp.float32),
                )
                for index in range(groups)
            )
        )

    def finish(carry):
        parts = [
            total / jnp.where(denom > 0.0, denom, 1.0)[..., None] for top, denom, total in carry
        ]
        joined = parts[0]
        kv_count, group = (joined.shape[0], joined.shape[1])
        return (
            jnp.transpose(joined, (2, 0, 1, 3))
            .reshape(rows, kv_count * group * head_size)
            .astype(jnp.bfloat16)
        )

    return (fold, initial, finish)


def shards(
    hidden_in,
    doc_ids,
    layer_kind,
    norm_gain,
    q_weight,
    k_weight,
    v_weight,
    bc_weight,
    dt_weight,
    dt_bias,
    decay_rate,
    skip_gain,
):
    current = hidden_in[0]
    rows, width = current.shape
    ctx_pos = lax.axis_index("ctx")
    tp_pos = lax.axis_index("tp")
    ids_all = lax.all_gather(doc_ids, "ctx", axis=0, tiled=True)
    first = ctx_pos * rows
    prev_id = jnp.where(
        ctx_pos > 0,
        lax.dynamic_index_in_dim(ids_all, jnp.maximum(first - 1, 0), 0, keepdims=False),
        -1,
    )
    gain = norm_gain[0]
    head_size = HD
    q_cols = q_weight.shape[2]
    kv_cols = k_weight.shape[2]
    heads_local = q_cols // head_size
    kv_local = kv_cols // head_size
    group = heads_local // kv_local
    is_attention = layer_kind[0] == 1
    hf = current.astype(jnp.float32)
    squares = lax.psum(jnp.sum(hf * hf, axis=1), "tp")
    xn = (hf * lax.rsqrt(squares / D + 1e-05)[:, None] * gain[None, :]).astype(jnp.bfloat16)
    whole = lax.all_gather(xn, "tp", axis=1, tiled=True)
    empty = (
        jnp.zeros((rows, q_cols), jnp.float32),
        jnp.zeros((rows, kv_cols), jnp.float32),
        jnp.zeros((rows, kv_cols), jnp.float32),
    )
    pieces = (
        lax.all_gather(q_weight[0], "ctx", axis=0, tiled=True),
        lax.all_gather(k_weight[0], "ctx", axis=0, tiled=True),
        lax.all_gather(v_weight[0], "ctx", axis=0, tiled=True),
    )

    def really(values):
        return tuple(
            (jnp.dot(whole, piece, preferred_element_type=jnp.float32) for piece in pieces)
        )

    q_sum, k_sum, v_sum = lax.cond(is_attention, really, lambda values: values, empty)
    query = q_sum.astype(jnp.bfloat16).reshape(rows, kv_local, group, head_size)
    keys = k_sum.astype(jnp.bfloat16).reshape(rows, kv_local, head_size)
    values = v_sum.astype(jnp.bfloat16).reshape(rows, kv_local, head_size)
    q_pos = first + jnp.arange(rows)
    fold, initial, finish = make_fold(query, q_pos, doc_ids, ids_all, 1, head_size, is_attention)
    carry = fold(
        initial(kv_local, group),
        (
            lax.all_gather(keys, "ctx", axis=0, tiled=True),
            lax.all_gather(values, "ctx", axis=0, tiled=True),
        ),
        jnp.int32(0),
    )
    attended = finish(carry)
    attention_result = (current.astype(jnp.float32) + attended.astype(jnp.float32)).astype(
        jnp.bfloat16
    )
    ssm_local = dt_bias.shape[1]
    channels = width // ssm_local
    inputs = xn.astype(jnp.float32).reshape(rows, ssm_local, channels)
    maps, step_all = lax.psum(
        (
            jnp.dot(xn, bc_weight[0], preferred_element_type=jnp.float32),
            jnp.dot(xn, dt_weight[0], preferred_element_type=jnp.float32),
        ),
        "tp",
    )
    step = jax.nn.softplus(
        lax.dynamic_slice_in_dim(step_all, tp_pos * ssm_local, ssm_local, 1) + dt_bias[0][None, :]
    )
    state_size = maps.shape[1] // 2
    in_map = maps[:, :state_size]
    out_map = maps[:, state_size:]
    cumulative = jnp.cumsum(-step * decay_rate[0][None, :], axis=0)
    order = jnp.arange(rows)
    pairs = (doc_ids[:, None] == doc_ids[None, :]) & (order[:, None] >= order[None, :])
    exponent = jnp.where(
        pairs[:, :, None], cumulative[:, None, :] - cumulative[None, :, :], -jnp.inf
    )
    intersection = jnp.dot(out_map, in_map.T, precision=lax.Precision.HIGHEST)
    weighted = inputs * step[:, :, None]
    inner = jnp.einsum(
        "tsh,shp->thp",
        jnp.exp(exponent) * intersection[:, :, None],
        weighted,
        precision=lax.Precision.HIGHEST,
    )
    end_weight = (
        jnp.exp(cumulative[-1][None, :] - cumulative)
        * (doc_ids == doc_ids[-1]).astype(jnp.float32)[:, None]
    )
    end_state = jnp.einsum(
        "sh,sn,shp->hnp", end_weight, in_map, weighted, precision=lax.Precision.HIGHEST
    )
    total_decay = jnp.exp(cumulative[-1]) * (doc_ids[-1] == prev_id).astype(jnp.float32)

    def combine(earlier, later):
        return (earlier[0] * later[0], earlier[1] * later[0][:, None, None] + later[1])

    identity = (jnp.ones_like(total_decay), jnp.zeros_like(end_state))
    incoming = entering((total_decay, end_state), "ctx", combine, identity)[1]
    reach = jnp.exp(cumulative) * (doc_ids == prev_id).astype(jnp.float32)[:, None]
    carried = (
        jnp.einsum("tn,hnp->thp", out_map, incoming, precision=lax.Precision.HIGHEST)
        * reach[:, :, None]
    )
    outputs = inner + carried + skip_gain[0][None, :, None] * inputs
    outputs = outputs * lax.rsqrt(jnp.mean(outputs * outputs, axis=2, keepdims=True) + 1e-05)
    state_result = (current.astype(jnp.float32) + outputs.reshape(rows, width)).astype(jnp.bfloat16)
    produced = jnp.where(is_attention, attention_result, state_result)
    moved = passed_along(produced, "pipe", 1)
    return (produced[None], moved[None])


def solution(mesh):
    in_specs = (
        P("pipe", "ctx", "tp"),
        P("ctx"),
        P("pipe"),
        P("pipe", "tp"),
        P("pipe", "ctx", "tp"),
        P("pipe", "ctx", "tp"),
        P("pipe", "ctx", "tp"),
        P("pipe", "tp", None),
        P("pipe", "tp", None),
        P("pipe", "tp"),
        P("pipe", "tp"),
        P("pipe", "tp"),
    )
    out_specs = (P("pipe", "ctx", "tp"), P("pipe", "ctx", "tp"))
    return jax.shard_map(shards, mesh=mesh, in_specs=in_specs, out_specs=out_specs, check_vma=False)
```

profile of v0, /device:TPU:490, one launch (start us, length us, event | category | flops | bytes accessed | tf_op | source)
XLA Modules:
  0.0 523.1 jit_solution(2879111344124291897)
XLA Ops:
  7.3 1.1 fusion.178
  8.4 8.6 %psum.21 = f32[128]{0:T(128)S(1)} all-reduce(f32[128]{0:T(128)S(1)} %fusion.178), channel_id=1, replica_groups=mesh['pipe'=4,'ctx'=32,'tp'=4] {'tp'}, use_global_device_ids=true, to_apply=%region_2.3 | all-reduce | flops 128 | bytes 1024 | tf_op jit(solution)/shard_map/psum | solution.py:142
  17.1 1.8 fusion.180
  18.9 0.7 all-gather.18.cloned.1.call-update
  19.7 0.7 all-gather.20.cloned.1.call-update
  21.0 1.1 copy.85
  22.7 16.0 %all-reduce = (f32[128,64]{0,1:T(8,128)S(1)}, f32[128,32]{0,1:T(8,128)S(1)}) all-reduce(f32[128,64]{0,1:T(8,128)S(1)} %fusion.192, f32[128,32]{0,1:T(8,128)S(1)} %fusion.195), channel_id=1, replica_groups=mesh['pipe'=4,'ctx'=32,'tp'=4] {'tp'}, use_global_device_ids=true, to_apply=%region_37.38 | all-reduce | flops 12288 | bytes 98304 | tf_op jit(solution)/shard_map/psum | solution.py:182
  39.5 26.3 %all-gather.6 = s32[32,1,128]{2,1,0:T(1,128)S(1)} all-gather(s32[1,1,128]{2,1,0:T(1,128)S(1)} %bitcast.510), channel_id=1, replica_groups=mesh['pipe'=4,'ctx'=32,'tp'=4] {'ctx'}, dimensions={0}, use_global_device_ids=true | all-gather | bytes 16896 | tf_op jit(solution)/shard_map/all_gather | solution.py:126
  67.7 0.6 compare_convert_fusion
  69.0 0.7 reduce.20
  69.8 1.6 convolution_convert_fusion.1
  72.2 48.9 %all-gather.18.cloned.1.call-done = bf16[1,4096,128]{2,1,0:T(8,128)(2,1)} async-done(((bf16[1,128,128]{2,1,0:T(8,128)(2,1)}), bf16[1,4096,128]{2,1,0:T(8,128)(2,1)}) %all-gather.18.cloned.1.call-update) | async-done | bytes 1048592 | tf_op jit(solution)/shard_map/all_gather | solution.py:152
  121.0 70.0 %all-gather.20.cloned.1.call-done = bf16[1,4096,128]{2,1,0:T(8,128)(2,1)} async-done(((bf16[1,128,128]{2,1,0:T(8,128)(2,1)}), bf16[1,4096,128]{2,1,0:T(8,128)(2,1)}) %all-gather.20.cloned.1.call-update) | async-done | bytes 1048592 | tf_op jit(solution)/shard_map/all_gather | solution.py:153
  191.0 78.8 %all-gather.22.cloned.1.call-done = bf16[1,4096,1024]{2,1,0:T(8,128)(2,1)} async-done(((bf16[1,128,1024]{2,1,0:T(8,128)(2,1)}), bf16[1,4096,1024]{2,1,0:T(8,128)(2,1)}) %all-gather.22.cloned.1.call-update) | async-done | bytes 8388624 | tf_op jit(solution)/shard_map/all_gather | solution.py:151
  270.6 0.7 fusion.208
  276.4 26.0 %all-gather.7 = bf16[32,1,16]{2,1,0:T(2,128)(2,1)S(1)} all-gather(bf16[1,1,16]{2,1,0:T(2,128)(2,1)S(1)} %get-tuple-element.767), channel_id=1, replica_groups=mesh['pipe'=4,'ctx'=32,'tp'=4] {'ctx'}, dimensions={0}, use_global_device_ids=true | all-gather | bytes 1056 | tf_op jit(solution)/shard_map/all_gather | solution.py:13
  302.4 0.6 iota_add_fusion.4
  305.3 0.6 fusion.211
  306.3 34.3 %all-gather.28.cloned.1.call-done = bf16[512,16,64]{2,1,0:T(8,128)(2,1)} async-done(((bf16[16,16,64]{2,1,0:T(8,128)(2,1)}), bf16[512,16,64]{2,1,0:T(8,128)(2,1)}) %all-gather.28.cloned.1.call-update) | async-done | bytes 1048592 | tf_op jit(solution)/shard_map/all_gather | solution.py:13
  340.7 31.3 %while.14 = (s32[]{:T(128)}, f32[16,16,64]{2,1,0:T(8,128)S(1)}, s32[]{:T(128)}, bf16[32,16]{1,0:T(8,128)(2,1)S(1)}, bf16[32,16,16,64]{3,2,1,0:T(8,128)(2,1)}, /*index=5*/s32[]{:T(128)}, s32[]{:T(128)}) while((s32[]{:T(128)}, f32[16,16,64]{2,1,0:T(8,128)S(1)}, s32[]{:T(128)}, bf16[32,16]{1,0:T(8,128)(2,1)S(1)}, ...), condition=%wide.region_41.42_spmd.clone, body=%wide.region_40.41_spmd.clone.sunk | while | flops 81940 | bytes 164105 | solution.py:26
  340.7 0.9 fusion.222
  341.6 0.9 fusion.222
  342.6 0.9 fusion.222
  343.6 0.9 fusion.222
  344.6 0.9 fusion.222
  345.6 0.9 fusion.222
  346.5 0.9 fusion.222
  347.5 0.9 fusion.222
  348.5 0.9 fusion.222
  349.5 0.9 fusion.222
  350.4 0.9 fusion.222
  351.4 0.9 fusion.222
  352.4 0.9 fusion.222
  353.4 0.9 fusion.222
  354.4 0.9 fusion.222
  355.3 0.9 fusion.222
  356.3 0.9 fusion.222
  357.3 0.9 fusion.222
  358.3 0.9 fusion.222
  359.2 0.9 fusion.222
  360.2 0.9 fusion.222
  361.2 0.9 fusion.222
  362.2 0.9 fusion.222
  363.2 0.9 fusion.222
  364.1 0.9 fusion.222
  365.1 0.9 fusion.222
  366.1 0.9 fusion.222
  367.1 0.9 fusion.222
  368.0 0.9 fusion.222
  369.0 0.9 fusion.222
  370.0 0.9 fusion.222
  371.0 0.9 fusion.222
  371.9 1.0 convolution_multiply_fusion
  373.0 2.3 multiply_reduce_fusion
  375.7 35.1 %all-gather.26.cloned.1.call-done = bf16[4096,128]{1,0:T(8,128)(2,1)} async-done(((bf16[128,128]{1,0:T(8,128)(2,1)}), bf16[4096,128]{1,0:T(8,128)(2,1)}) %all-gather.26.cloned.1.call-update) | async-done | bytes 1048592 | tf_op jit(solution)/shard_map/all_gather | solution.py:171
  410.8 1.9 slice_bitcast_fusion
  412.7 68.1 %all-gather.24.cloned.1.call-done = bf16[4096,128]{1,0:T(8,128)(2,1)} async-done(((bf16[128,128]{1,0:T(8,128)(2,1)}), bf16[4096,128]{1,0:T(8,128)(2,1)}) %all-gather.24.cloned.1.call-update) | async-done | bytes 1048592 | tf_op jit(solution)/shard_map/all_gather | solution.py:170
  480.8 1.3 slice_bitcast_fusion.1
  483.1 0.7 copy-done.12
  483.7 0.7 copy-done.11
  485.5 3.4 collective-permute-start
  488.9 0.8 fusion.188
  489.7 25.9 %collective-permute-done = bf16[128,1024]{1,0:T(8,128)(2,1)S(1)} collective-permute-done((bf16[128,1024]{1,0:T(8,128)(2,1)S(1)}, bf16[128,1024]{1,0:T(8,128)(2,1)S(1)}, u32[]{:S(2)}, u32[]{:S(2)}) %collective-permute-start) | collective-permute-done | bytes 262176 | tf_op jit(solution)/shard_map/ppermute | solution.py:32
  515.6 0.7 copy.220
  (129 shorter events, 10.0 us)
Async XLA Ops:
  7.2 15.2 %copy-start = (bf16[1,1024,64]{1,2,0:T(8,128)(2,1)S(1)}, bf16[1,1024,64]{1,2,0:T(8,128)(2,1)}, u32[]{:S(2)}) copy-start(bf16[1,1024,64]{1,2,0:T(8,128)(2,1)} %param.40) | copy-start | bytes 393220
  7.2 14.9 %copy-start.2 = (bf16[1,128,1024]{2,1,0:T(8,128)(2,1)S(1)}, bf16[1,128,1024]{2,1,0:T(8,128)(2,1)}, u32[]{:S(2)}) copy-start(bf16[1,128,1024]{2,1,0:T(8,128)(2,1)} %param.32) | copy-start | bytes 786436
  7.2 14.9 %copy-start.10 = (f32[1,1024]{1,0:T(1,128)S(1)}, f32[1,1024]{1,0:T(1,128)}, u32[]{:S(2)}) copy-start(f32[1,1024]{1,0:T(1,128)} %param.35) | copy-start | bytes 12292
  7.2 14.9 %copy-start.19 = (bf16[1,1024,32]{1,2,0:T(8,128)(2,1)S(1)}, bf16[1,1024,32]{1,2,0:T(8,128)(2,1)}, u32[]{:S(2)}) copy-start(bf16[1,1024,32]{1,2,0:T(8,128)(2,1)} %param.39) | copy-start | bytes 196612
  7.2 31.5 %copy-start.18 = (f32[1,16]{1,0:T(1,128)S(1)}, f32[1,16]{1,0:T(1,128)}, u32[]{:S(2)}) copy-start(f32[1,16]{1,0:T(1,128)} %param.41) | copy-start | bytes 196
  7.2 31.5 %copy-start.17 = (f32[1,16]{1,0:T(1,128)S(1)}, f32[1,16]{1,0:T(1,128)}, u32[]{:S(2)}) copy-start(f32[1,16]{1,0:T(1,128)} %param.42) | copy-start | bytes 196
  7.2 31.7 %copy-start.8 = (s32[128]{0:T(128)S(1)}, s32[128]{0:T(128)}, u32[]{:S(2)}) copy-start(s32[128]{0:T(128)} %param.33) | copy-start | bytes 1540
  7.2 64.9 %all-gather.16.cloned.1.call-start = ((), (), s32[]{:S(2)}) async-start(), calls=%async_computation | async-start | bytes 1310720 | tf_op jit(solution)/shard_map/all_gather | solution.py:144
  18.9 102.2 %all-gather.18.cloned.1.call-start = ((), (), s32[]{:S(2)}) async-start(), calls=%async_computation.1 | async-start | bytes 1081344 | tf_op jit(solution)/shard_map/all_gather | solution.py:152
  19.6 171.4 %all-gather.20.cloned.1.call-start = ((), (), s32[]{:S(2)}) async-start(), calls=%async_computation.2 | async-start | bytes 1081344 | tf_op jit(solution)/shard_map/all_gather | solution.py:153
  20.4 249.4 %all-gather.22.cloned.1.call-start = ((), (), s32[]{:S(2)}) async-start(), calls=%async_computation.3 | async-start | bytes 8650752 | tf_op jit(solution)/shard_map/all_gather | solution.py:151
  20.9 319.7 %all-gather.28.cloned.1.call-start = ((), (), s32[]{:S(2)}) async-start(), calls=%async_computation.6 | async-start | bytes 2162688 | tf_op jit(solution)/shard_map/all_gather | solution.py:13
  65.7 239.6 %copy-start.9 = (s32[32,1,128]{2,1,0:T(1,128)}, s32[32,1,128]{2,1,0:T(1,128)S(1)}, u32[]{:S(2)}) copy-start(s32[32,1,128]{2,1,0:T(1,128)S(1)} %all-gather.6) | copy-start | bytes 49156
  71.4 339.4 %all-gather.26.cloned.1.call-start = ((), (), s32[]{:S(2)}) async-start(), calls=%async_computation.5 | async-start | bytes 1081344 | tf_op jit(solution)/shard_map/all_gather | solution.py:171
  269.9 0.6 copy-start.7
  269.9 36.4 %copy-start.6 = (bf16[128,128]{1,0:T(8,128)(2,1)}, bf16[128,128]{1,0:T(8,128)(2,1)S(1)}, u32[]{:S(2)}) copy-start(bf16[128,128]{1,0:T(8,128)(2,1)S(1)} %get-tuple-element.418) | copy-start | bytes 98308
  269.9 103.1 %copy-start.20 = (f32[1,16]{1,0:T(1,128)S(1)}, f32[1,16]{1,0:T(1,128)}, u32[]{:S(2)}) copy-start(f32[1,16]{1,0:T(1,128)} %param.43) | copy-start | bytes 196
  270.5 210.3 %all-gather.24.cloned.1.call-start = ((), (), s32[]{:S(2)}) async-start(), calls=%async_computation.4 | async-start | bytes 1081344 | tf_op jit(solution)/shard_map/all_gather | solution.py:170
  482.4 0.6 copy-start.13
  482.4 0.7 copy-start.16
  483.1 0.7 copy-start.12
  483.1 0.7 copy-start.15
  483.7 0.7 copy-start.11
  483.7 0.7 copy-start.14
  485.5 30.1 %collective-permute-start = (bf16[128,1024]{1,0:T(8,128)(2,1)S(1)}, bf16[128,1024]{1,0:T(8,128)(2,1)S(1)}, u32[]{:S(2)}, u32[]{:S(2)}) collective-permute-start(bf16[128,1024]{1,0:T(8,128)(2,1)S(1)} %fusion.187), channel_id=1, source_target_pairs={{0,128},{128,256},{256,384},{1,129},{129,257},{257,385},{2,130},{1... | collective-permute-start | bytes 786440 | tf_op jit(solution)/shard_map/ppermute | solution.py:32
Sparse Core Ops, SparseCore 0:
  19.0 29.2 all-gather.15
  50.4 70.5 all-gather.17
  123.2 67.8 all-gather.19
  193.0 76.7 all-gather.21
  272.3 68.2 all-gather.27
  343.2 67.5 all-gather.25
  413.0 67.8 all-gather.23
where the time goes:
time: 525 us; the launch traced here: 523 us
  waiting for transfers between devices  363 us (69%)
  blocking collectives  76.8 us (15%)
  other arithmetic  39.7 us (8%)
  between operations  21.6 us (4%)
  local copies, waits for them, and re-layouts  11.1 us (2%)
  matrix products  5.81 us (1%)
    all_gather x1, waiting for transfers between devices, shards(): lax.all_gather(q_weight[0], 'ctx', axis=0, tiled=True)  78.8 us
    all_gather x1, waiting for transfers between devices, shards(): lax.all_gather(v_weight[0], 'ctx', axis=0, tiled=True)  70 us
    all_gather x1, waiting for transfers between devices, shards(): lax.all_gather(keys, 'ctx', axis=0, tiled=True)  68.1 us
    all_gather x1, waiting for transfers between devices, shards(): lax.all_gather(k_weight[0], 'ctx', axis=0, tiled=True)  48.9 us
    all_gather x1, waiting for transfers between devices, shards(): lax.all_gather(values, 'ctx', axis=0, tiled=True)  35.1 us
    all_gather x1, waiting for transfers between devices, entering(): lax.all_gather(part.astype(kind), axis)  34.3 us
    select_n x32, other arithmetic, turn(): return jax.tree.map(lambda a, b: jnp.where(reached, a, b), new, before)  29.9 us
    all_gather x1, blocking collectives, shards(): ids_all = lax.all_gather(doc_ids, 'ctx', axis=0, tiled=True)  26.3 us
  transfers between devices with their start and end apart: 8, of which 7 were waited for; matrix products, arithmetic and copies ran while one was open for 9% of the time, Pallas kernels for 0%

commit v1 on v0

v1 whole, which is shorter than its diff:
```python
import jax
import jax.numpy as jnp
from jax import lax
from jax.experimental import pallas as pl
from jax.experimental.pallas import tpu as pltpu
from jax.sharding import PartitionSpec as P

D = 4096
HD = 128
ROWS = 128
COLS = 1024
CHIPS = 16
STATE = 16
HL = 16
PAY = ROWS + 16
BACK = 8
NEG = -1e30
BF, F32 = jnp.bfloat16, jnp.float32
EXACT = lax.Precision.HIGHEST

W_FIRST = (0, -4, 4, -8)
W_REL = tuple(a + b for b in (0, -1, 1, -2) for a in W_FIRST)
KV_AT = {0: (0, 0), 4: (0, 1), 8: (0, 2), 1: (1, 0), 5: (1, 1), 2: (1, 2), 6: (1, 3), 3: (1, 4), 7: (1, 5)}


def iota(shape, dim):
    return lax.broadcasted_iota(jnp.int32, shape, dim)


def dot(a, b, precision=None):
    return jnp.dot(a, b, preferred_element_type=F32, precision=precision)


def pair(low, j, values):
    return jnp.where(low, values[:, 2 * j : 2 * j + 1], values[:, 2 * j + 1 : 2 * j + 2])


def front(scal, got, idc_ref, idr_ref, bias, rate, skip, xn, pay, yloc, aux):
    attention, place = scal[0], scal[1]
    squares = jnp.zeros((ROWS, 1), F32)
    for s in range(4):
        hf = got[s, :ROWS, :].astype(F32)
        squares += jnp.sum(hf * hf, axis=1, keepdims=True)
    inverse = lax.rsqrt(squares / D + 1e-05)
    for s in range(4):
        gain = got[s, ROWS + 48 :, :].astype(F32)
        gain = gain[0:1] + gain[1:2] + gain[2:3]
        xn[:, s * COLS : (s + 1) * COLS] = (got[s, :ROWS, :].astype(F32) * inverse * gain).astype(BF)
    idc, idr = idc_ref[...], idr_ref[...]
    row = iota((16, 256), 0)
    ids = jnp.concatenate([idr, jnp.zeros((1, ROWS), F32)], axis=1)
    pay[ROWS:, :] = jnp.where(row == 0, ids, 0.0).astype(BF)

    @pl.when(attention == 0)
    def _():
        maps = jnp.zeros((ROWS, 48), F32)
        for s in range(4):
            maps += lax.dot_general(
                xn[:, s * COLS : (s + 1) * COLS],
                got[s, ROWS : ROWS + 48, :],
                (((1,), (1,)), ((), ())),
                preferred_element_type=F32,
            )
        raw = maps[:, :HL] + bias[...]
        step = jnp.maximum(raw, 0.0) + jnp.log1p(jnp.exp(-jnp.abs(raw)))
        in_map, out_map = maps[:, HL : HL + STATE], maps[:, HL + STATE :]
        earlier = iota((ROWS, ROWS), 0) >= iota((ROWS, ROWS), 1)
        cum = dot(earlier.astype(F32), -step * rate[...], EXACT)
        empty = jnp.zeros((ROWS, ROWS - 32), F32)
        turned = jnp.concatenate([cum, in_map, empty], axis=1).T
        cum_t, in_t = turned[:HL], turned[HL : HL + STATE]
        both = dot(out_map, in_t, EXACT)
        mask = earlier & (idc == idr)
        last = cum[ROWS - 1 :, :]
        end = jnp.where(idc == idr[:, ROWS - 1 :], jnp.exp(last - cum), 0.0)
        low = iota((ROWS, ROWS), 1) < 64
        base = pl.multiple_of(place * COLS, COLS)
        for j in range(HL // 2):
            x = xn[:, pl.ds(base + j * 128, 128)].astype(F32)
            wx = x * pair(low, j, step)
            weights = [
                jnp.exp(jnp.where(mask, cum[:, i : i + 1] - cum_t[i : i + 1, :], NEG)) * both
                for i in (2 * j, 2 * j + 1)
            ]
            split = jnp.concatenate([jnp.where(low, wx, 0.0), jnp.where(low, 0.0, wx)], axis=0)
            inner = dot(jnp.concatenate(weights, axis=1), split, EXACT)
            yloc[:, j * 128 : (j + 1) * 128] = inner + pair(low[:1], j, skip[...]) * x
            state = dot(in_t, wx * pair(low, j, end), EXACT)
            at = 16 * (j // 2)
            pay[at : at + 16, 128 * (j % 2) : 128 * (j % 2) + 128] = state.astype(BF)
        wide = jnp.concatenate([last, jnp.zeros((1, 256 - HL), F32)], axis=1)
        first = wide.astype(BF).astype(F32)
        second = (wide - first).astype(BF).astype(F32)
        third = wide - first - second
        extra = jnp.where(row == 1, first, jnp.where(row == 2, second, jnp.where(row == 3, third, 0.0)))
        pay[ROWS:, :] = jnp.where(row == 0, ids, extra).astype(BF)
        aux[...] = jnp.concatenate([cum, out_map, empty], axis=1)


def project(scal, xn, own0, own1, own2, own3, sib, state_pay, pay, weight):
    attention, chip, core = scal[0], scal[2], scal[3]

    @pl.when(attention == 1)
    def _():
        for n, rel in enumerate(W_REL):
            at = lax.rem(chip + rel + CHIPS, CHIPS) * 256
            source = (own0, own1, own2, own3)[n // 4]
            k = n % 4
            weight[pl.ds(pl.multiple_of(at + core * 128, 128), 128), :] = source[k * 128 : k * 128 + 128, :]
            weight[pl.ds(pl.multiple_of(at + (1 - core) * 128, 128), 128), :] = sib[n * 128 : n * 128 + 128, :]
        pay[:ROWS, :] = dot(xn[...], weight[...]).astype(BF)
        pay[ROWS:, :] = state_pay[ROWS:, :]

    @pl.when(attention == 0)
    def _():
        pay[...] = state_pay[...]


def attend(scal, h, xn, wq, blocks, idc_ref, out, wbuf, keys, values, mask, sem):
    chip, core = scal[2], scal[3]
    copies = [
        pltpu.make_async_copy(wq.at[:, pl.ds(j * 256, 256)], wbuf.at[j], sem.at[j]) for j in range(4)
    ]
    for copy in copies:
        copy.start()
    idc = idc_ref[...]
    n = 0
    for r in range(BACK + 1):
        which, k = KV_AT[r]
        for mine in (True, False):
            ref = blocks[which if mine else 2 + which]
            rows = slice(n * ROWS, (n + 1) * ROWS)
            keys[rows, :] = ref[k * PAY : k * PAY + ROWS, :HD]
            values[rows, :] = ref[k * PAY : k * PAY + ROWS, HD:]
            ids = ref[k * PAY + ROWS : (k + 1) * PAY, :HD].astype(F32)[0:1, :]
            allowed = idc == ids
            if r == 0 and mine:
                allowed = allowed & (iota((ROWS, ROWS), 0) >= iota((ROWS, ROWS), 1))
            else:
                valid = core == 1 if r == 0 else chip >= r
                allowed = allowed & (jnp.full((ROWS, ROWS), valid.astype(jnp.int32)) == 1)
            mask[:, rows] = jnp.where(allowed, 0.0, NEG)
            n += 1
    factor = HD ** (-0.5) * 1.4426950408889634
    for j in range(4):
        copies[j].wait()
        q = dot(xn[...], wbuf[j]).astype(BF)
        query = jnp.concatenate([q[:, :HD], q[:, HD:]], axis=0)
        scores = lax.dot_general(
            query, keys[...], (((1,), (1,)), ((), ())), preferred_element_type=F32
        )
        parts, dens = [], []
        for i in range(2):
            s = scores[i * ROWS : (i + 1) * ROWS, :] + mask[...]
            p = jnp.exp2((s - jnp.max(s, axis=1, keepdims=True)) * factor)
            dens.append(jnp.sum(p, axis=1, keepdims=True))
            parts.append(p.astype(BF))
        mixed = dot(jnp.concatenate(parts, axis=0), values[...])
        for i in range(2):
            o = (mixed[i * ROWS : (i + 1) * ROWS, :] / dens[i]).astype(BF).astype(F32)
            cols = slice(j * 256 + i * HD, j * 256 + (i + 1) * HD)
            out[:, cols] = (h[:, cols].astype(F32) + o).astype(BF)


def finish_states(scal, h, blocks, yloc, aux, idc_ref, out):
    core, device = scal[3], scal[4]
    order = []
    for r in range(1, BACK + 1):
        def block(mine, back):
            which, k = KV_AT[back]
            return blocks[which if mine else 2 + which], k * PAY

        order.append((block(False, r - 1), block(False, r)))
        order.append((block(True, r), None))

    def read(entry, lo, hi):
        (ref, at), other = entry
        tile = ref[at + lo : at + hi, :].astype(F32)
        if other is not None:
            ref, at = other
            tile = jnp.where(core == 1, tile, ref[at + lo : at + hi, :].astype(F32))
        return tile

    idc = idc_ref[...]
    before = jnp.zeros((1, HL), F32)
    coefs = []
    previous = None
    for k, entry in enumerate(order, 1):
        extra = read(entry, ROWS, PAY)
        tail = jnp.where(device >= k, extra[0:1, HD - 1 : HD], -1.0)
        if previous is None:
            previous = tail
        fits = (tail == previous) & (tail >= 0.0)
        coefs.append(jnp.where(fits, jnp.exp(before), 0.0))
        before += extra[1:2, :HL] + extra[2:3, :HL] + extra[3:4, :HL]
    spread = (iota((HL, COLS), 1) // 64 == iota((HL, COLS), 0)).astype(F32)
    coef = dot(jnp.concatenate(coefs, axis=0), spread, EXACT)
    cum, out_map = aux[:, :HL], aux[:, HL : HL + STATE]
    reach = jnp.where(idc == previous, jnp.exp(cum), 0.0)
    low = iota((ROWS, ROWS), 1) < 64
    for c in range(4):
        incoming = jnp.zeros((STATE, 256), F32)
        for k, entry in enumerate(order):
            incoming += coef[k : k + 1, c * 256 : (c + 1) * 256] * read(entry, 16 * c, 16 * c + 16)
        for i in range(2):
            j = 2 * c + i
            cols = slice(j * 128, (j + 1) * 128)
            carried = dot(out_map, incoming[:, i * 128 : (i + 1) * 128], EXACT) * pair(low, j, reach)
            y = yloc[:, cols] + carried
            y2 = y * y
            one = jnp.sum(jnp.where(low, y2, 0.0), axis=1, keepdims=True)
            two = jnp.sum(jnp.where(low, 0.0, y2), axis=1, keepdims=True)
            scale = lax.rsqrt(jnp.where(low, one, two) / 64 + 1e-05)
            out[:, cols] = (h[:, cols].astype(F32) + y * scale).astype(BF)


def finish(scal, h, xn, wq, own0, own1, sib0, sib1, yloc, aux, idc, out, wbuf, keys, values, mask, sem):
    blocks = (own0, own1, sib0, sib1)

    @pl.when(scal[0] == 1)
    def _():
        attend(scal, h, xn, wq, blocks, idc, out, wbuf, keys, values, mask, sem)

    @pl.when(scal[0] == 0)
    def _():
        finish_states(scal, h, blocks, yloc, aux, idc, out)


VMEM = pl.BlockSpec(memory_space=pltpu.VMEM)
SMEM = pl.BlockSpec(memory_space=pltpu.SMEM)
ANY = pl.BlockSpec(memory_space=pl.ANY)


def shape(*dims, dtype=BF):
    return jax.ShapeDtypeStruct(dims, dtype)


def by_chips(x, k):
    return lax.ppermute(x, "ctx", [(i, (i + 2 * k) % (2 * CHIPS)) for i in range(2 * CHIPS)])


def swap(x):
    return lax.ppermute(x, "ctx", [(i, i ^ 1) for i in range(2 * CHIPS)])


def shards(
    hidden_in,
    doc_ids,
    layer_kind,
    norm_gain,
    q_weight,
    k_weight,
    v_weight,
    bc_weight,
    dt_weight,
    dt_bias,
    decay_rate,
    skip_gain,
):
    device = lax.axis_index("ctx")
    scal = jnp.stack(
        [layer_kind[0], lax.axis_index("tp"), device // 2, device % 2, device]
    ).astype(jnp.int32)
    params = pltpu.CompilerParams(vmem_limit_bytes=48 << 20)

    wq = lax.all_gather(q_weight[0], "ctx", axis=0, tiled=True)

    wkv = jnp.concatenate([k_weight[0], v_weight[0]], axis=1)
    first = jnp.concatenate([wkv] + [by_chips(wkv, k) for k in (4, -4, 8)], axis=0)
    others = [by_chips(first, k) for k in (1, -1, 2)]
    sibling = swap(jnp.concatenate([first] + others, axis=0))

    gain = norm_gain[0]
    gain1 = lax.reduce_precision(gain, 8, 7)
    gain2 = lax.reduce_precision(gain - gain1, 8, 7)
    gain3 = gain - gain1 - gain2
    gains = jnp.concatenate([jnp.stack([gain1, gain2, gain3]), jnp.zeros((13, COLS), F32)]).astype(BF)
    everyone = lambda x: jnp.broadcast_to(x[None], (4,) + x.shape)
    got = lax.all_to_all(
        jnp.concatenate(
            [
                everyone(hidden_in[0]),
                dt_weight[0].T.reshape(4, HL, COLS),
                everyone(bc_weight[0].T),
                everyone(gains),
            ],
            axis=1,
        ),
        "tp",
        0,
        0,
    )
    ids = doc_ids.astype(F32)
    idc, idr = ids[:, None], ids[None, :]
    xn, state_pay, yloc, aux = pl.pallas_call(
        front,
        name="front",
        out_shape=(shape(ROWS, D), shape(PAY, 256), shape(ROWS, COLS, dtype=F32), shape(ROWS, 128, dtype=F32)),
        in_specs=[SMEM] + [VMEM] * 6,
        out_specs=(VMEM,) * 4,
        compiler_params=params,
        cost_estimate=pl.CostEstimate(flops=2 * 128 * 128 * 4096, bytes_accessed=4 << 20, transcendentals=0),
    )(scal, got, idc, idr, dt_bias, decay_rate, skip_gain)

    pay = pl.pallas_call(
        project,
        name="project",
        out_shape=shape(PAY, 256),
        in_specs=[SMEM] + [VMEM] * 7,
        out_specs=VMEM,
        scratch_shapes=[pltpu.VMEM((D, 256), BF)],
        compiler_params=params,
        cost_estimate=pl.CostEstimate(flops=2 * 128 * 256 * 4096, bytes_accessed=4 << 20, transcendentals=0),
    )(scal, xn, first, *others, sibling, state_pay)

    back4, back8 = by_chips(pay, 4), by_chips(pay, 8)
    near = jnp.concatenate([pay, back4], axis=0)
    far = jnp.concatenate([back4, back8], axis=0)
    own0 = jnp.concatenate([pay, back4, back8], axis=0)
    own1 = jnp.concatenate([by_chips(near, 1), by_chips(near, 2), by_chips(far, -1)], axis=0)
    sib0, sib1 = swap(own0), swap(own1)

    produced = pl.pallas_call(
        finish,
        name="finish",
        out_shape=shape(ROWS, COLS),
        in_specs=[SMEM, VMEM, VMEM, ANY] + [VMEM] * 7,
        out_specs=VMEM,
        scratch_shapes=[
            pltpu.VMEM((4, D, 256), BF),
            pltpu.VMEM((18 * ROWS, HD), BF),
            pltpu.VMEM((18 * ROWS, HD), BF),
            pltpu.VMEM((ROWS, 18 * ROWS), F32),
            pltpu.SemaphoreType.DMA((4,)),
        ],
        compiler_params=params,
        cost_estimate=pl.CostEstimate(flops=2 * 128 * 1024 * 8192, bytes_accessed=12 << 20, transcendentals=0),
    )(scal, hidden_in[0], xn, wq, own0, own1, sib0, sib1, yloc, aux, idc)
    moved = lax.ppermute(produced, "pipe", [(i, i + 1) for i in range(3)])
    return (produced[None], moved[None])


def solution(mesh):
    in_specs = (
        P("pipe", "ctx", "tp"),
        P("ctx"),
        P("pipe"),
        P("pipe", "tp"),
        P("pipe", "ctx", "tp"),
        P("pipe", "ctx", "tp"),
        P("pipe", "ctx", "tp"),
        P("pipe", "tp", None),
        P("pipe", "tp", None),
        P("pipe", "tp"),
        P("pipe", "tp"),
        P("pipe", "tp"),
    )
    out_specs = (P("pipe", "ctx", "tp"), P("pipe", "ctx", "tp"))
    return jax.shard_map(shards, mesh=mesh, in_specs=in_specs, out_specs=out_specs, check_vma=False)
```

time: 525 us -> 167 us (0.32)
  the two profiles are of different devices: /device:TPU:490 before, /device:TPU:60 now
where the time goes in v1:
time: 167 us; the launch traced here: 166 us
  starting transfers between devices  71.7 us (43%)
  waiting for transfers between devices  49.3 us (30%)
  between operations  15 us (9%)
  Pallas kernels  14.6 us (9%)
  local copies, waits for them, and re-layouts  10.5 us (6%)
  other arithmetic  5.06 us (3%)
    ppermute x11, starting transfers between devices, by_chips(): lax.ppermute(x, 'ctx', [(i, (i + 2 * k) % (2 * CHIPS)) for i in range(2 *...  59.2 us
    ppermute x11, waiting for transfers between devices, by_chips(): lax.ppermute(x, 'ctx', [(i, (i + 2 * k) % (2 * CHIPS)) for i in range(2 *...  38.1 us
    pallas_call x1, Pallas kernels, shards(): pl.pallas_call(finish, name='finish', out_shape=shape(ROWS, COLS), in_spe...  11.7 us
    ppermute x1, waiting for transfers between devices, shards(): moved = lax.ppermute(produced, 'pipe', [(i, i + 1) for i in range(3)])  9.41 us
    unnamed x36, local copies, waits for them, and re-layouts  7.51 us
    ppermute x3, starting transfers between devices, swap(): return lax.ppermute(x, 'ctx', [(i, i ^ 1) for i in range(2 * CHIPS)])  6.24 us
    all_to_all x1, starting transfers between devices, shards(): lax.all_to_all(jnp.concatenate([everyone(hidden_in[0]), dt_weight[0].T.re...  4.94 us
  transfers between devices with their start and end apart: 17, of which 8 were waited for; matrix products, arithmetic and copies ran while one was open for 7% of the time, Pallas kernels for 2%

profile of v1, /device:TPU:60, one launch (start us, length us, event | category | flops | bytes accessed | tf_op | source)
XLA Modules:
  0.0 166.2 jit_solution(5175265846587116588)
XLA Ops:
  7.2 0.0 all-gather.3.cloned.1.call-start
  7.2 0.7 all-gather.3.cloned.1.call-update
  7.9 1.4 constant_dynamic-update-slice_fusion.6
  9.3 9.1 %collective-permute-start = (bf16[128,256]{1,0:T(8,128)(2,1)S(1)}, bf16[128,256]{1,0:T(8,128)(2,1)S(1)}, u32[]{:S(2)}, u32[]{:S(2)}) collective-permute-start(bf16[128,256]{1,0:T(8,128)(2,1)S(1)} %get-tuple-element.13), channel_id=1, source_target_pairs={{0,32},{4,36},{8,40},{12,44},{16,48},{20,52},{24,56},{28,60},{32,6... | collective-permute-start | bytes 196616 | tf_op jit(solution)/shard_map/ppermute | solution.py:239
  18.4 4.7 %collective-permute-start.1 = (bf16[128,256]{1,0:T(8,128)(2,1)S(1)}, bf16[128,256]{1,0:T(8,128)(2,1)S(1)}, u32[]{:S(2)}, u32[]{:S(2)}) collective-permute-start(bf16[128,256]{1,0:T(8,128)(2,1)S(1)} %get-tuple-element.13), channel_id=1, source_target_pairs={{0,96},{4,100},{8,104},{12,108},{16,112},{20,116},{24,120},{28,124... | collective-permute-start | bytes 196616 | tf_op jit(solution)/shard_map/ppermute | solution.py:239
  23.1 10.8 %collective-permute-start.2 = (bf16[128,256]{1,0:T(8,128)(2,1)S(1)}, bf16[128,256]{1,0:T(8,128)(2,1)S(1)}, u32[]{:S(2)}, u32[]{:S(2)}) collective-permute-start(bf16[128,256]{1,0:T(8,128)(2,1)S(1)} %get-tuple-element.13), channel_id=1, source_target_pairs={{0,64},{4,68},{8,72},{12,76},{16,80},{20,84},{24,88},{28,92},{32,9... | collective-permute-start | bytes 196616 | tf_op jit(solution)/shard_map/ppermute | solution.py:239
  33.9 0.1 pad.23.clone
  34.0 0.7 reduce-precision_convert_fusion.1
  34.7 0.1 maximum_maximum_fusion
  34.8 1.1 broadcast_in_dim.32
  35.9 0.9 broadcast_in_dim.33
  36.7 0.0 copy-start.11
  36.7 0.0 copy-start.12
  36.7 2.2 %pad_maximum_fusion = bf16[4,192,1024]{2,1,0:T(8,128)(2,1)} fusion(bf16[4,16,1024]{2,1,0:T(8,128)(2,1)S(1)} %broadcast_in_dim.35, bf16[4,32,1024]{2,1,0:T(8,128)(2,1)S(1)} %broadcast_in_dim.33, bf16[4,16,1024]{2,1,0:T(8,128)(2,1)} %bitcast.27, bf16[4,128,1024]{2,1,0:T(8,128)(2,1)S(1)} %broadcast_in_dim.32), kind=kLoop, calls=%fused_computation | loop fusion | flops 6291456 | bytes 3145728 | tf_op jit(solution)/shard_map/concatenate | solution.py:280
  39.0 4.9 %all-to-all-start = ((bf16[4,192,1024]{2,1,0:T(8,128)(2,1)}), bf16[4,192,1024]{2,1,0:T(8,128)(2,1)S(1)}, u32[]{:S(2)}, u32[]{:S(2)}) async-start(bf16[4,192,1024]{2,1,0:T(8,128)(2,1)} %pad_maximum_fusion), calls=%async_computation | async-start | bytes 3145728 | tf_op jit(solution)/shard_map/all_to_all | solution.py:279
  43.9 0.0 collective-permute-done
  43.9 0.0 collective-permute-done.1
  43.9 0.0 collective-permute-done.2
  44.0 3.0 %collective-permute-start.3 = (bf16[512,256]{1,0:T(8,128)(2,1)S(1)}, bf16[512,256]{1,0:T(8,128)(2,1)S(1)}, u32[]{:S(2)}, u32[]{:S(2)}) collective-permute-start(bf16[512,256]{1,0:T(8,128)(2,1)S(1)} %pad_maximum_fusion.1.own0), channel_id=1, source_target_pairs={{0,8},{4,12},{8,16},{12,20},{16,24},{20,28},{24,32},{28,36},{32,40... | collective-permute-start | bytes 786440 | tf_op jit(solution)/shard_map/ppermute | solution.py:239
  47.0 2.9 %collective-permute-start.4 = (bf16[512,256]{1,0:T(8,128)(2,1)S(1)}, bf16[512,256]{1,0:T(8,128)(2,1)S(1)}, u32[]{:S(2)}, u32[]{:S(2)}) collective-permute-start(bf16[512,256]{1,0:T(8,128)(2,1)S(1)} %pad_maximum_fusion.1.own0), channel_id=1, source_target_pairs={{0,120},{4,124},{8,0},{12,4},{16,8},{20,12},{24,16},{28,20},{32,24... | collective-permute-start | bytes 786440 | tf_op jit(solution)/shard_map/ppermute | solution.py:239
  49.8 3.4 %collective-permute-start.5 = (bf16[512,256]{1,0:T(8,128)(2,1)S(1)}, bf16[512,256]{1,0:T(8,128)(2,1)S(1)}, u32[]{:S(2)}, u32[]{:S(2)}) collective-permute-start(bf16[512,256]{1,0:T(8,128)(2,1)S(1)} %pad_maximum_fusion.1.own0), channel_id=1, source_target_pairs={{0,16},{4,20},{8,24},{12,28},{16,32},{20,36},{24,40},{28,44},{32,4... | collective-permute-start | bytes 786440 | tf_op jit(solution)/shard_map/ppermute | solution.py:239
  53.2 0.6 constant_dynamic-update-slice_fusion.5
  53.9 0.6 constant_dynamic-update-slice_fusion.4
  54.5 0.6 constant_dynamic-update-slice_fusion.3
  55.1 5.1 %collective-permute-done.3.own1 = bf16[512,256]{1,0:T(8,128)(2,1)S(1)} collective-permute-done((bf16[512,256]{1,0:T(8,128)(2,1)S(1)}, bf16[512,256]{1,0:T(8,128)(2,1)S(1)}, u32[]{:S(2)}, u32[]{:S(2)}) %collective-permute-start.3) | collective-permute-done | bytes 262176 | tf_op jit(solution)/shard_map/ppermute | solution.py:239
  60.3 0.7 constant_dynamic-update-slice_fusion.2
  61.0 1.0 collective-permute-done.4.own2
  62.0 0.7 constant_dynamic-update-slice_fusion.1
  62.7 15.1 %collective-permute-done.5.own3 = bf16[512,256]{1,0:T(8,128)(2,1)S(1)} collective-permute-done((bf16[512,256]{1,0:T(8,128)(2,1)S(1)}, bf16[512,256]{1,0:T(8,128)(2,1)S(1)}, u32[]{:S(2)}, u32[]{:S(2)}) %collective-permute-start.5) | collective-permute-done | bytes 262176 | tf_op jit(solution)/shard_map/ppermute | solution.py:239
  77.8 0.8 constant_dynamic-update-slice_fusion
  78.6 1.9 %collective-permute-start.6 = (bf16[2048,256]{1,0:T(8,128)(2,1)}, bf16[2048,256]{1,0:T(8,128)(2,1)}, u32[]{:S(2)}, u32[]{:S(2)}) collective-permute-start(bf16[2048,256]{1,0:T(8,128)(2,1)} %constant_dynamic-update-slice_fusion), channel_id=1, source_target_pairs={{0,4},{4,0},{8,12},{12,8},{16,20},{20,16},{24,28},{28,24},{32,36},... | collective-permute-start | bytes 3145736 | tf_op jit(solution)/shard_map/ppermute | solution.py:243
  81.2 0.6 convert_bitcast_fusion
  81.7 0.1 copy.14.idc_ref.idc
  81.9 0.1 stack.22.scal
  82.0 0.0 all-to-all-done.got
  82.0 0.0 copy-done.7
  82.0 0.0 copy-done.8
  82.0 0.0 copy-done.9
  82.0 0.0 copy-start.10
  82.0 0.7 copy-done.10
  82.7 1.0 front.1
  83.7 0.8 copy-done.5
  84.6 0.0 collective-permute-done.6.sib
  84.6 1.0 copy-done.2
  85.5 1.0 copy-done.4
  86.5 1.9 %project.1 = bf16[144,256]{1,0:T(8,128)(2,1)S(1)} custom-call(s32[5]{0:T(128)S(1)} %stack.22.scal, bf16[128,4096]{1,0:T(8,128)(2,1)S(1)} %get-tuple-element.6.xn, bf16[512,256]{1,0:T(8,128)(2,1)S(1)} %pad_maximum_fusion.1.own0, bf16[512,256]{1,0:T(8,128)(2,1)S(1)} %collective-permute-done.3.own1, bf16[512,256]{1,0:T(8,128)(2,1)S(1)} %copy-done.2, ...), custom_call_target="tpu_custom_call" | custom-call | flops 268435456 | bytes 4194304 | tf_op jit(solution)/shard_map/project/pallas_call | solution.py:305
  88.4 4.1 %collective-permute-start.7 = (bf16[144,256]{1,0:T(8,128)(2,1)S(1)}, bf16[144,256]{1,0:T(8,128)(2,1)S(1)}, u32[]{:S(2)}, u32[]{:S(2)}) collective-permute-start(bf16[144,256]{1,0:T(8,128)(2,1)S(1)} %project.1), channel_id=1, source_target_pairs={{0,32},{4,36},{8,40},{12,44},{16,48},{20,52},{24,56},{28,60},{32,6... | collective-permute-start | bytes 221192 | tf_op jit(solution)/shard_map/ppermute | solution.py:239
  92.5 8.4 %collective-permute-start.8 = (bf16[144,256]{1,0:T(8,128)(2,1)S(1)}, bf16[144,256]{1,0:T(8,128)(2,1)S(1)}, u32[]{:S(2)}, u32[]{:S(2)}) collective-permute-start(bf16[144,256]{1,0:T(8,128)(2,1)S(1)} %project.1), channel_id=1, source_target_pairs={{0,64},{4,68},{8,72},{12,76},{16,80},{20,84},{24,88},{28,92},{32,9... | collective-permute-start | bytes 221192 | tf_op jit(solution)/shard_map/ppermute | solution.py:239
  101.0 2.8 %collective-permute-done.7 = bf16[144,256]{1,0:T(8,128)(2,1)S(1)} collective-permute-done((bf16[144,256]{1,0:T(8,128)(2,1)S(1)}, bf16[144,256]{1,0:T(8,128)(2,1)S(1)}, u32[]{:S(2)}, u32[]{:S(2)}) %collective-permute-start.7) | collective-permute-done | bytes 73760 | tf_op jit(solution)/shard_map/ppermute | solution.py:239
  103.7 7.9 %collective-permute-done.8 = bf16[144,256]{1,0:T(8,128)(2,1)S(1)} collective-permute-done((bf16[144,256]{1,0:T(8,128)(2,1)S(1)}, bf16[144,256]{1,0:T(8,128)(2,1)S(1)}, u32[]{:S(2)}, u32[]{:S(2)}) %collective-permute-start.8) | collective-permute-done | bytes 73760 | tf_op jit(solution)/shard_map/ppermute | solution.py:239
  111.6 4.9 %collective-permute-start.9 = (bf16[288,256]{1,0:T(8,128)(2,1)S(1)}, bf16[288,256]{1,0:T(8,128)(2,1)S(1)}, u32[]{:S(2)}, u32[]{:S(2)}) collective-permute-start(bf16[288,256]{1,0:T(8,128)(2,1)S(1)} %get-tuple-element.11), channel_id=1, source_target_pairs={{0,8},{4,12},{8,16},{12,20},{16,24},{20,28},{24,32},{28,36},{32,40... | collective-permute-start | bytes 442376 | tf_op jit(solution)/shard_map/ppermute | solution.py:239
  116.5 6.0 %collective-permute-start.10 = (bf16[288,256]{1,0:T(8,128)(2,1)S(1)}, bf16[288,256]{1,0:T(8,128)(2,1)S(1)}, u32[]{:S(2)}, u32[]{:S(2)}) collective-permute-start(bf16[288,256]{1,0:T(8,128)(2,1)S(1)} %get-tuple-element.11), channel_id=1, source_target_pairs={{0,16},{4,20},{8,24},{12,28},{16,32},{20,36},{24,40},{28,44},{32,4... | collective-permute-start | bytes 442376 | tf_op jit(solution)/shard_map/ppermute | solution.py:239
  122.5 1.9 %collective-permute-start.11 = (bf16[288,256]{1,0:T(8,128)(2,1)S(1)}, bf16[288,256]{1,0:T(8,128)(2,1)S(1)}, u32[]{:S(2)}, u32[]{:S(2)}) collective-permute-start(bf16[288,256]{1,0:T(8,128)(2,1)S(1)} %get-tuple-element.10), channel_id=1, source_target_pairs={{0,120},{4,124},{8,0},{12,4},{16,8},{20,12},{24,16},{28,20},{32,24... | collective-permute-start | bytes 442376 | tf_op jit(solution)/shard_map/ppermute | solution.py:239
  124.5 0.0 collective-permute-done.9
  124.5 6.2 %collective-permute-done.10 = bf16[288,256]{1,0:T(8,128)(2,1)S(1)} collective-permute-done((bf16[288,256]{1,0:T(8,128)(2,1)S(1)}, bf16[288,256]{1,0:T(8,128)(2,1)S(1)}, u32[]{:S(2)}, u32[]{:S(2)}) %collective-permute-start.10) | collective-permute-done | bytes 147488 | tf_op jit(solution)/shard_map/ppermute | solution.py:239
  130.8 0.0 collective-permute-done.11
  130.8 1.9 %collective-permute-start.13 = (bf16[864,256]{1,0:T(8,128)(2,1)S(1)}, bf16[864,256]{1,0:T(8,128)(2,1)S(1)}, u32[]{:S(2)}, u32[]{:S(2)}) collective-permute-start(bf16[864,256]{1,0:T(8,128)(2,1)S(1)} %constant_dynamic-update-slice_fusion.7.own1), channel_id=1, source_target_pairs={{0,4},{4,0},{8,12},{12,8},{16,20},{20,16},{24,28},{28,24},{32,36},... | collective-permute-start | bytes 1327112 | tf_op jit(solution)/shard_map/ppermute | solution.py:243
  132.7 2.4 %collective-permute-start.12 = (bf16[432,256]{1,0:T(8,128)(2,1)S(1)}, bf16[432,256]{1,0:T(8,128)(2,1)S(1)}, u32[]{:S(2)}, u32[]{:S(2)}) collective-permute-start(bf16[432,256]{1,0:T(8,128)(2,1)S(1)} %pad_maximum_fusion.2.own0), channel_id=1, source_target_pairs={{0,4},{4,0},{8,12},{12,8},{16,20},{20,16},{24,28},{28,24},{32,36},... | collective-permute-start | bytes 663560 | tf_op jit(solution)/shard_map/ppermute | solution.py:243
  135.2 1.1 collective-permute-done.12.sib0
  136.2 0.0 collective-permute-done.13.sib1
  136.3 11.7 %finish.1 = bf16[128,1024]{1,0:T(8,128)(2,1)} custom-call(s32[5]{0:T(128)S(1)} %stack.22.scal, bf16[128,1024]{1,0:T(8,128)(2,1)S(1)} %bitcast.23, bf16[128,4096]{1,0:T(8,128)(2,1)S(1)} %get-tuple-element.6.xn, bf16[4096,1024]{1,0:T(8,128)(2,1)} %bitcast.24, bf16[432,256]{1,0:T(8,128)(2,1)S(1)} %pad_maximum_fusion.2.own0, ...), custom_call_target="tpu_custom_call" | custom-call | flops 2147483648 | bytes 12582912 | tf_op jit(solution)/shard_map/finish/pallas_call | solution.py:323
  147.9 1.3 collective-permute-start.14
  149.2 9.4 %collective-permute-done.14 = bf16[128,1024]{1,0:T(8,128)(2,1)S(1)} collective-permute-done((bf16[128,1024]{1,0:T(8,128)(2,1)}, bf16[128,1024]{1,0:T(8,128)(2,1)S(1)}, u32[]{:S(2)}, u32[]{:S(2)}) %collective-permute-start.14) | collective-permute-done | bytes 262176 | tf_op jit(solution)/shard_map/ppermute | solution.py:339
  158.6 0.7 copy.26
  (27 shorter events, 0.1 us)
Async XLA Ops:
  7.2 129.1 %all-gather.3.cloned.1.call-start = ((), (), s32[]{:S(2)}) async-start(), calls=%async_computation.1 | async-start | bytes 8650752 | tf_op jit(solution)/shard_map/all_gather | solution.py:266
  9.3 34.6 %collective-permute-start = (bf16[128,256]{1,0:T(8,128)(2,1)S(1)}, bf16[128,256]{1,0:T(8,128)(2,1)S(1)}, u32[]{:S(2)}, u32[]{:S(2)}) collective-permute-start(bf16[128,256]{1,0:T(8,128)(2,1)S(1)} %get-tuple-element.13), channel_id=1, source_target_pairs={{0,32},{4,36},{8,40},{12,44},{16,48},{20,52},{24,56},{28,60},{32,6... | collective-permute-start | bytes 196616 | tf_op jit(solution)/shard_map/ppermute | solution.py:239
  18.4 25.5 %collective-permute-start.1 = (bf16[128,256]{1,0:T(8,128)(2,1)S(1)}, bf16[128,256]{1,0:T(8,128)(2,1)S(1)}, u32[]{:S(2)}, u32[]{:S(2)}) collective-permute-start(bf16[128,256]{1,0:T(8,128)(2,1)S(1)} %get-tuple-element.13), channel_id=1, source_target_pairs={{0,96},{4,100},{8,104},{12,108},{16,112},{20,116},{24,120},{28,124... | collective-permute-start | bytes 196616 | tf_op jit(solution)/shard_map/ppermute | solution.py:239
  23.1 20.9 %collective-permute-start.2 = (bf16[128,256]{1,0:T(8,128)(2,1)S(1)}, bf16[128,256]{1,0:T(8,128)(2,1)S(1)}, u32[]{:S(2)}, u32[]{:S(2)}) collective-permute-start(bf16[128,256]{1,0:T(8,128)(2,1)S(1)} %get-tuple-element.13), channel_id=1, source_target_pairs={{0,64},{4,68},{8,72},{12,76},{16,80},{20,84},{24,88},{28,92},{32,9... | collective-permute-start | bytes 196616 | tf_op jit(solution)/shard_map/ppermute | solution.py:239
  36.7 7.2 %copy-start.11 = (bf16[1,128,128]{2,1,0:T(8,128)(2,1)S(1)}, bf16[1,128,128]{2,1,0:T(8,128)(2,1)}, u32[]{:S(2)}) copy-start(bf16[1,128,128]{2,1,0:T(8,128)(2,1)} %param.18) | copy-start | bytes 98308
  36.7 7.2 %copy-start.12 = (bf16[1,128,128]{2,1,0:T(8,128)(2,1)S(1)}, bf16[1,128,128]{2,1,0:T(8,128)(2,1)}, u32[]{:S(2)}) copy-start(bf16[1,128,128]{2,1,0:T(8,128)(2,1)} %param.17) | copy-start | bytes 98308
  39.0 42.2 %copy-start.13 = (s32[128]{0:T(128)S(1)}, s32[128]{0:T(128)}, u32[]{:S(2)}) copy-start(s32[128]{0:T(128)} %param.13) | copy-start | bytes 1540
  39.0 43.0 %copy-start.7 = (f32[1,16]{1,0:T(1,128)S(1)}, f32[1,16]{1,0:T(1,128)}, u32[]{:S(2)}) copy-start(f32[1,16]{1,0:T(1,128)} %bias.1) | copy-start | bytes 196
  39.0 43.0 %copy-start.8 = (f32[1,16]{1,0:T(1,128)S(1)}, f32[1,16]{1,0:T(1,128)}, u32[]{:S(2)}) copy-start(f32[1,16]{1,0:T(1,128)} %rate.1) | copy-start | bytes 196
  39.0 43.0 %copy-start.9 = (f32[1,16]{1,0:T(1,128)S(1)}, f32[1,16]{1,0:T(1,128)}, u32[]{:S(2)}) copy-start(f32[1,16]{1,0:T(1,128)} %skip.1) | copy-start | bytes 196
  39.0 43.0 %all-to-all-start = ((bf16[4,192,1024]{2,1,0:T(8,128)(2,1)}), bf16[4,192,1024]{2,1,0:T(8,128)(2,1)S(1)}, u32[]{:S(2)}, u32[]{:S(2)}) async-start(bf16[4,192,1024]{2,1,0:T(8,128)(2,1)} %pad_maximum_fusion), calls=%async_computation | async-start | bytes 3145728 | tf_op jit(solution)/shard_map/all_to_all | solution.py:279
  44.0 16.3 %collective-permute-start.3 = (bf16[512,256]{1,0:T(8,128)(2,1)S(1)}, bf16[512,256]{1,0:T(8,128)(2,1)S(1)}, u32[]{:S(2)}, u32[]{:S(2)}) collective-permute-start(bf16[512,256]{1,0:T(8,128)(2,1)S(1)} %pad_maximum_fusion.1.own0), channel_id=1, source_target_pairs={{0,8},{4,12},{8,16},{12,20},{16,24},{20,28},{24,32},{28,36},{32,40... | collective-permute-start | bytes 786440 | tf_op jit(solution)/shard_map/ppermute | solution.py:239
  47.0 15.0 %collective-permute-start.4 = (bf16[512,256]{1,0:T(8,128)(2,1)S(1)}, bf16[512,256]{1,0:T(8,128)(2,1)S(1)}, u32[]{:S(2)}, u32[]{:S(2)}) collective-permute-start(bf16[512,256]{1,0:T(8,128)(2,1)S(1)} %pad_maximum_fusion.1.own0), channel_id=1, source_target_pairs={{0,120},{4,124},{8,0},{12,4},{16,8},{20,12},{24,16},{28,20},{32,24... | collective-permute-start | bytes 786440 | tf_op jit(solution)/shard_map/ppermute | solution.py:239
  49.8 27.9 %collective-permute-start.5 = (bf16[512,256]{1,0:T(8,128)(2,1)S(1)}, bf16[512,256]{1,0:T(8,128)(2,1)S(1)}, u32[]{:S(2)}, u32[]{:S(2)}) collective-permute-start(bf16[512,256]{1,0:T(8,128)(2,1)S(1)} %pad_maximum_fusion.1.own0), channel_id=1, source_target_pairs={{0,16},{4,20},{8,24},{12,28},{16,32},{20,36},{24,40},{28,44},{32,4... | collective-permute-start | bytes 786440 | tf_op jit(solution)/shard_map/ppermute | solution.py:239
  62.0 20.0 %copy-start.1 = (bf16[512,256]{1,0:T(8,128)(2,1)}, bf16[512,256]{1,0:T(8,128)(2,1)S(1)}, u32[]{:S(2)}) copy-start(bf16[512,256]{1,0:T(8,128)(2,1)S(1)} %collective-permute-done.4.own2) | copy-start | bytes 786436
  77.8 4.2 %copy-start.3 = (bf16[512,256]{1,0:T(8,128)(2,1)}, bf16[512,256]{1,0:T(8,128)(2,1)S(1)}, u32[]{:S(2)}) copy-start(bf16[512,256]{1,0:T(8,128)(2,1)S(1)} %collective-permute-done.5.own3) | copy-start | bytes 786436
  78.6 6.0 %collective-permute-start.6 = (bf16[2048,256]{1,0:T(8,128)(2,1)}, bf16[2048,256]{1,0:T(8,128)(2,1)}, u32[]{:S(2)}, u32[]{:S(2)}) collective-permute-start(bf16[2048,256]{1,0:T(8,128)(2,1)} %constant_dynamic-update-slice_fusion), channel_id=1, source_target_pairs={{0,4},{4,0},{8,12},{12,8},{16,20},{20,16},{24,28},{28,24},{32,36},... | collective-permute-start | bytes 3145736 | tf_op jit(solution)/shard_map/ppermute | solution.py:243
  82.0 0.7 copy-start.10
  82.7 53.6 %copy-start = (bf16[1,128,1024]{2,1,0:T(8,128)(2,1)S(1)}, bf16[1,128,1024]{2,1,0:T(8,128)(2,1)}, u32[]{:S(2)}) copy-start(bf16[1,128,1024]{2,1,0:T(8,128)(2,1)} %param.12) | copy-start | bytes 786436
  83.7 0.8 copy-start.5
  84.6 1.0 copy-start.2
  85.5 1.0 copy-start.4
  86.5 49.8 %copy-start.6 = (f32[128,1024]{1,0:T(8,128)S(1)}, f32[128,1024]{1,0:T(8,128)}, u32[]{:S(2)}) copy-start(f32[128,1024]{1,0:T(8,128)} %copy-done.5) | copy-start | bytes 1572868
  88.4 15.4 %collective-permute-start.7 = (bf16[144,256]{1,0:T(8,128)(2,1)S(1)}, bf16[144,256]{1,0:T(8,128)(2,1)S(1)}, u32[]{:S(2)}, u32[]{:S(2)}) collective-permute-start(bf16[144,256]{1,0:T(8,128)(2,1)S(1)} %project.1), channel_id=1, source_target_pairs={{0,32},{4,36},{8,40},{12,44},{16,48},{20,52},{24,56},{28,60},{32,6... | collective-permute-start | bytes 221192 | tf_op jit(solution)/shard_map/ppermute | solution.py:239
  92.5 19.1 %collective-permute-start.8 = (bf16[144,256]{1,0:T(8,128)(2,1)S(1)}, bf16[144,256]{1,0:T(8,128)(2,1)S(1)}, u32[]{:S(2)}, u32[]{:S(2)}) collective-permute-start(bf16[144,256]{1,0:T(8,128)(2,1)S(1)} %project.1), channel_id=1, source_target_pairs={{0,64},{4,68},{8,72},{12,76},{16,80},{20,84},{24,88},{28,92},{32,9... | collective-permute-start | bytes 221192 | tf_op jit(solution)/shard_map/ppermute | solution.py:239
  111.6 12.8 %collective-permute-start.9 = (bf16[288,256]{1,0:T(8,128)(2,1)S(1)}, bf16[288,256]{1,0:T(8,128)(2,1)S(1)}, u32[]{:S(2)}, u32[]{:S(2)}) collective-permute-start(bf16[288,256]{1,0:T(8,128)(2,1)S(1)} %get-tuple-element.11), channel_id=1, source_target_pairs={{0,8},{4,12},{8,16},{12,20},{16,24},{20,28},{24,32},{28,36},{32,40... | collective-permute-start | bytes 442376 | tf_op jit(solution)/shard_map/ppermute | solution.py:239
  116.5 14.2 %collective-permute-start.10 = (bf16[288,256]{1,0:T(8,128)(2,1)S(1)}, bf16[288,256]{1,0:T(8,128)(2,1)S(1)}, u32[]{:S(2)}, u32[]{:S(2)}) collective-permute-start(bf16[288,256]{1,0:T(8,128)(2,1)S(1)} %get-tuple-element.11), channel_id=1, source_target_pairs={{0,16},{4,20},{8,24},{12,28},{16,32},{20,36},{24,40},{28,44},{32,4... | collective-permute-start | bytes 442376 | tf_op jit(solution)/shard_map/ppermute | solution.py:239
  122.5 8.2 %collective-permute-start.11 = (bf16[288,256]{1,0:T(8,128)(2,1)S(1)}, bf16[288,256]{1,0:T(8,128)(2,1)S(1)}, u32[]{:S(2)}, u32[]{:S(2)}) collective-permute-start(bf16[288,256]{1,0:T(8,128)(2,1)S(1)} %get-tuple-element.10), channel_id=1, source_target_pairs={{0,120},{4,124},{8,0},{12,4},{16,8},{20,12},{24,16},{28,20},{32,24... | collective-permute-start | bytes 442376 | tf_op jit(solution)/shard_map/ppermute | solution.py:239
  130.8 5.5 %collective-permute-start.13 = (bf16[864,256]{1,0:T(8,128)(2,1)S(1)}, bf16[864,256]{1,0:T(8,128)(2,1)S(1)}, u32[]{:S(2)}, u32[]{:S(2)}) collective-permute-start(bf16[864,256]{1,0:T(8,128)(2,1)S(1)} %constant_dynamic-update-slice_fusion.7.own1), channel_id=1, source_target_pairs={{0,4},{4,0},{8,12},{12,8},{16,20},{20,16},{24,28},{28,24},{32,36},... | collective-permute-start | bytes 1327112 | tf_op jit(solution)/shard_map/ppermute | solution.py:243
  132.7 3.5 %collective-permute-start.12 = (bf16[432,256]{1,0:T(8,128)(2,1)S(1)}, bf16[432,256]{1,0:T(8,128)(2,1)S(1)}, u32[]{:S(2)}, u32[]{:S(2)}) collective-permute-start(bf16[432,256]{1,0:T(8,128)(2,1)S(1)} %pad_maximum_fusion.2.own0), channel_id=1, source_target_pairs={{0,4},{4,0},{8,12},{12,8},{16,20},{20,16},{24,28},{28,24},{32,36},... | collective-permute-start | bytes 663560 | tf_op jit(solution)/shard_map/ppermute | solution.py:243
  147.9 10.7 %collective-permute-start.14 = (bf16[128,1024]{1,0:T(8,128)(2,1)}, bf16[128,1024]{1,0:T(8,128)(2,1)S(1)}, u32[]{:S(2)}, u32[]{:S(2)}) collective-permute-start(bf16[128,1024]{1,0:T(8,128)(2,1)} %finish.1), channel_id=1, source_target_pairs={{0,128},{128,256},{256,384},{1,129},{129,257},{257,385},{2,130},{1... | collective-permute-start | bytes 786440 | tf_op jit(solution)/shard_map/ppermute | solution.py:339
Sparse Core Ops, SparseCore 0:
  10.1 107.9 all-gather.2

commit v2 on v1

v2 whole, which is shorter than its diff:
```python
import jax
import jax.numpy as jnp
from jax import lax
from jax.experimental import pallas as pl
from jax.experimental.pallas import tpu as pltpu
from jax.sharding import PartitionSpec as P

D = 4096
HD = 128
ROWS = 128
COLS = 1024
CHIPS = 16
STATE = 16
HL = 16
WROWS = ROWS + 16
BACK = 8
NEG = -1e30
BF, F32 = jnp.bfloat16, jnp.float32
EXACT = lax.Precision.HIGHEST

W_FIRST = (-4, 0, 4, -8)
W_REL = tuple(a + b for b in (0, -1, 1) for a in W_FIRST) + (-6, -2, 2, 6)
KV_AT = {0: (0, 0), 4: (0, 1), 8: (0, 2), 1: (1, 0), 5: (1, 1), 2: (1, 2), 6: (1, 3), 3: (1, 4), 7: (1, 5)}


def iota(shape, dim):
    return lax.broadcasted_iota(jnp.int32, shape, dim)


def dot(a, b, precision=None):
    return jnp.dot(a, b, preferred_element_type=F32, precision=precision)


def pair(low, j, values):
    return jnp.where(low, values[:, 2 * j : 2 * j + 1], values[:, 2 * j + 1 : 2 * j + 2])


def front(scal, got, idc_ref, idr_ref, bias, rate, skip, xn, states, yloc, aux):
    attention, place = scal[0], scal[1]
    squares = jnp.zeros((ROWS, 1), F32)
    for s in range(4):
        hf = got[s, :ROWS, :].astype(F32)
        squares += jnp.sum(hf * hf, axis=1, keepdims=True)
    inverse = lax.rsqrt(squares / D + 1e-05)
    for s in range(4):
        gain = got[s, ROWS + 48 :, :].astype(F32)
        gain = gain[0:1] + gain[1:2] + gain[2:3]
        xn[:, s * COLS : (s + 1) * COLS] = (got[s, :ROWS, :].astype(F32) * inverse * gain).astype(BF)
    idc, idr = idc_ref[...], idr_ref[...]

    @pl.when(attention == 0)
    def _():
        maps = jnp.zeros((ROWS, 48), F32)
        for s in range(4):
            maps += lax.dot_general(
                xn[:, s * COLS : (s + 1) * COLS],
                got[s, ROWS : ROWS + 48, :],
                (((1,), (1,)), ((), ())),
                preferred_element_type=F32,
            )
        raw = maps[:, :HL] + bias[...]
        step = jnp.maximum(raw, 0.0) + jnp.log1p(jnp.exp(-jnp.abs(raw)))
        in_map, out_map = maps[:, HL : HL + STATE], maps[:, HL + STATE :]
        earlier = iota((ROWS, ROWS), 0) >= iota((ROWS, ROWS), 1)
        cum = dot(earlier.astype(F32), -step * rate[...], EXACT)
        empty = jnp.zeros((ROWS, ROWS - 32), F32)
        turned = jnp.concatenate([cum, in_map, empty], axis=1).T
        cum_t, in_t = turned[:HL], turned[HL : HL + STATE]
        both = dot(out_map, in_t, EXACT)
        mask = earlier & (idc == idr)
        last = cum[ROWS - 1 :, :]
        end = jnp.where(idc == idr[:, ROWS - 1 :], jnp.exp(last - cum), 0.0)
        low = iota((ROWS, ROWS), 1) < 64
        base = pl.multiple_of(place * COLS, COLS)
        for j in range(HL // 2):
            x = xn[:, pl.ds(base + j * 128, 128)].astype(F32)
            wx = x * pair(low, j, step)
            weights = [
                jnp.exp(jnp.where(mask, cum[:, i : i + 1] - cum_t[i : i + 1, :], NEG)) * both
                for i in (2 * j, 2 * j + 1)
            ]
            split = jnp.concatenate([jnp.where(low, wx, 0.0), jnp.where(low, 0.0, wx)], axis=0)
            inner = dot(jnp.concatenate(weights, axis=1), split, EXACT)
            yloc[:, j * 128 : (j + 1) * 128] = inner + pair(low[:1], j, skip[...]) * x
            state = dot(in_t, wx * pair(low, j, end), EXACT)
            at = 16 * (j // 2)
            states[at : at + 16, 128 * (j % 2) : 128 * (j % 2) + 128] = state.astype(BF)
        wide = jnp.concatenate([last, jnp.zeros((1, 256 - HL), F32)], axis=1)
        first = wide.astype(BF).astype(F32)
        second = (wide - first).astype(BF).astype(F32)
        third = wide - first - second
        row = iota((64, 256), 0)
        extra = jnp.where(row == 0, first, jnp.where(row == 1, second, jnp.where(row == 2, third, 0.0)))
        states[64:, :] = extra.astype(BF)
        aux[...] = jnp.concatenate([cum, out_map, empty], axis=1)


def project(scal, xn, own, sib, states, pay, kid, weight):
    attention, chip, core = scal[0], scal[2], scal[3]
    n = 0
    for r in range(BACK + 1):
        at = [w % CHIPS for w in W_REL].index(-r % CHIPS) * WROWS + ROWS
        for ref in (own, sib):
            kid[n : n + 1, :] = ref[at : at + 16, :ROWS].astype(F32)[0:1, :]
            n += 1

    @pl.when(attention == 1)
    def _():
        for n, rel in enumerate(W_REL):
            at = lax.rem(chip + rel + CHIPS, CHIPS) * 256
            rows = slice(n * WROWS, n * WROWS + ROWS)
            weight[pl.ds(pl.multiple_of(at + core * 128, 128), 128), :] = own[rows, :]
            weight[pl.ds(pl.multiple_of(at + (1 - core) * 128, 128), 128), :] = sib[rows, :]
        pay[...] = dot(xn[...], weight[...]).astype(BF)

    @pl.when(attention == 0)
    def _():
        pay[...] = states[...]


def query(scal, xn, wq, out, wbuf, sem):
    @pl.when(scal[0] == 1)
    def _():
        copies = [
            pltpu.make_async_copy(wq.at[:, pl.ds(j * 256, 256)], wbuf.at[j], sem.at[j]) for j in range(4)
        ]
        for copy in copies:
            copy.start()
        for j, copy in enumerate(copies):
            copy.wait()
            out[:, j * 256 : (j + 1) * 256] = dot(xn[...], wbuf[j]).astype(BF)


def attend(scal, h, q, blocks, kid, idc_ref, out, keys, values, mask):
    chip, core = scal[2], scal[3]
    idc = idc_ref[...]
    n = 0
    for r in range(BACK + 1):
        which, k = KV_AT[r]
        for mine in (True, False):
            ref = blocks[which if mine else 2 + which]
            rows = slice(n * ROWS, (n + 1) * ROWS)
            keys[rows, :] = ref[k * ROWS : (k + 1) * ROWS, :HD]
            values[rows, :] = ref[k * ROWS : (k + 1) * ROWS, HD:]
            allowed = idc == kid[n : n + 1, :]
            if r == 0 and mine:
                allowed = allowed & (iota((ROWS, ROWS), 0) >= iota((ROWS, ROWS), 1))
            else:
                valid = core == 1 if r == 0 else chip >= r
                allowed = allowed & (jnp.full((ROWS, ROWS), valid.astype(jnp.int32)) == 1)
            mask[:, rows] = jnp.where(allowed, 0.0, NEG)
            n += 1
    factor = HD ** (-0.5) * 1.4426950408889634
    for j in range(4):
        at = 256 * j
        rows = jnp.concatenate([q[:, at : at + HD], q[:, at + HD : at + 256]], axis=0)
        scores = lax.dot_general(
            rows, keys[...], (((1,), (1,)), ((), ())), preferred_element_type=F32
        )
        parts, dens = [], []
        for i in range(2):
            s = scores[i * ROWS : (i + 1) * ROWS, :] + mask[...]
            p = jnp.exp2((s - jnp.max(s, axis=1, keepdims=True)) * factor)
            dens.append(jnp.sum(p, axis=1, keepdims=True))
            parts.append(p.astype(BF))
        mixed = dot(jnp.concatenate(parts, axis=0), values[...])
        for i in range(2):
            o = (mixed[i * ROWS : (i + 1) * ROWS, :] / dens[i]).astype(BF).astype(F32)
            cols = slice(j * 256 + i * HD, j * 256 + (i + 1) * HD)
            out[:, cols] = (h[:, cols].astype(F32) + o).astype(BF)


def finish_states(scal, h, blocks, kid, yloc, aux, idc_ref, out):
    core, device = scal[3], scal[4]
    order = []
    for r in range(1, BACK + 1):
        def block(mine, back):
            which, k = KV_AT[back]
            return blocks[which if mine else 2 + which], k * ROWS, 2 * back + (0 if mine else 1)

        order.append((block(False, r - 1), block(False, r)))
        order.append((block(True, r), None))

    def read(entry, lo, hi):
        (ref, at, _), other = entry
        tile = ref[at + lo : at + hi, :].astype(F32)
        if other is not None:
            ref, at, _ = other
            tile = jnp.where(core == 1, tile, ref[at + lo : at + hi, :].astype(F32))
        return tile

    idc = idc_ref[...]
    before = jnp.zeros((1, HL), F32)
    coefs = []
    previous = None
    for k, entry in enumerate(order, 1):
        n = entry[0][2]
        tail = kid[n : n + 1, ROWS - 1 :]
        if entry[1] is not None:
            n = entry[1][2]
            tail = jnp.where(core == 1, tail, kid[n : n + 1, ROWS - 1 :])
        tail = jnp.where(device >= k, tail, -1.0)
        if previous is None:
            previous = tail
        fits = (tail == previous) & (tail >= 0.0)
        coefs.append(jnp.where(fits, jnp.exp(before), 0.0))
        extra = read(entry, 64, 80)
        before += extra[0:1, :HL] + extra[1:2, :HL] + extra[2:3, :HL]
    spread = (iota((HL, COLS), 1) // 64 == iota((HL, COLS), 0)).astype(F32)
    coef = dot(jnp.concatenate(coefs, axis=0), spread, EXACT)
    cum, out_map = aux[:, :HL], aux[:, HL : HL + STATE]
    reach = jnp.where(idc == previous, jnp.exp(cum), 0.0)
    low = iota((ROWS, ROWS), 1) < 64
    for c in range(4):
        incoming = jnp.zeros((STATE, 256), F32)
        for k, entry in enumerate(order):
            incoming += coef[k : k + 1, c * 256 : (c + 1) * 256] * read(entry, 16 * c, 16 * c + 16)
        for i in range(2):
            j = 2 * c + i
            cols = slice(j * 128, (j + 1) * 128)
            carried = dot(out_map, incoming[:, i * 128 : (i + 1) * 128], EXACT) * pair(low, j, reach)
            y = yloc[:, cols] + carried
            y2 = y * y
            one = jnp.sum(jnp.where(low, y2, 0.0), axis=1, keepdims=True)
            two = jnp.sum(jnp.where(low, 0.0, y2), axis=1, keepdims=True)
            scale = lax.rsqrt(jnp.where(low, one, two) / 64 + 1e-05)
            out[:, cols] = (h[:, cols].astype(F32) + y * scale).astype(BF)


def finish(scal, h, q, own0, own1, sib0, sib1, kid, yloc, aux, idc, out, keys, values, mask):
    blocks = (own0, own1, sib0, sib1)

    @pl.when(scal[0] == 1)
    def _():
        attend(scal, h, q, blocks, kid, idc, out, keys, values, mask)

    @pl.when(scal[0] == 0)
    def _():
        finish_states(scal, h, blocks, kid, yloc, aux, idc, out)


VMEM = pl.BlockSpec(memory_space=pltpu.VMEM)
SMEM = pl.BlockSpec(memory_space=pltpu.SMEM)
ANY = pl.BlockSpec(memory_space=pl.ANY)


def kernel(body, us, mib, outs, ins, scratch=()):
    return pl.pallas_call(
        body,
        name=body.__name__,
        out_shape=outs,
        in_specs=ins,
        out_specs=jax.tree.map(lambda _: VMEM, outs),
        scratch_shapes=scratch,
        compiler_params=pltpu.CompilerParams(vmem_limit_bytes=mib << 20),
        cost_estimate=pl.CostEstimate(flops=int(us * 1.15e9), bytes_accessed=1 << 20, transcendentals=0),
    )


def shape(*dims, dtype=BF):
    return jax.ShapeDtypeStruct(dims, dtype)


def by_chips(x, k):
    return lax.ppermute(x, "ctx", [(i, (i + 2 * k) % (2 * CHIPS)) for i in range(2 * CHIPS)])


def swap(x):
    return lax.ppermute(x, "ctx", [(i, i ^ 1) for i in range(2 * CHIPS)])


def shards(
    hidden_in,
    doc_ids,
    layer_kind,
    norm_gain,
    q_weight,
    k_weight,
    v_weight,
    bc_weight,
    dt_weight,
    dt_bias,
    decay_rate,
    skip_gain,
):
    device = lax.axis_index("ctx")
    scal = jnp.stack(
        [layer_kind[0], lax.axis_index("tp"), device // 2, device % 2, device]
    ).astype(jnp.int32)
    ids = doc_ids.astype(F32)
    idc, idr = ids[:, None], ids[None, :]

    wq = lax.all_gather(q_weight[0], "ctx", axis=0, tiled=True)

    gain = norm_gain[0]
    gain1 = lax.reduce_precision(gain, 8, 7)
    gain2 = lax.reduce_precision(gain - gain1, 8, 7)
    gain3 = gain - gain1 - gain2
    gains = jnp.concatenate([jnp.stack([gain1, gain2, gain3]), jnp.zeros((13, COLS), F32)]).astype(BF)
    everyone = lambda x: jnp.broadcast_to(x[None], (4,) + x.shape)
    parts = jnp.concatenate(
        [
            everyone(hidden_in[0]),
            dt_weight[0].T.reshape(4, HL, COLS),
            everyone(bc_weight[0].T),
            everyone(gains),
        ],
        axis=1,
    )
    wkv = jnp.concatenate([k_weight[0], v_weight[0]], axis=1)
    wkv = jnp.concatenate([wkv, jnp.pad(idr.astype(BF), ((0, 15), (0, 128)))], axis=0)
    a, b, c = [by_chips(wkv, k) for k in (4, -4, 8)]
    first = jnp.concatenate([a, wkv, b, c], axis=0)
    parts, first = lax.optimization_barrier((parts, first))
    got = lax.all_to_all(parts, "tp", 0, 0)
    xn, states, yloc, aux = kernel(
        front,
        4,
        20,
        (shape(ROWS, D), shape(ROWS, 256), shape(ROWS, COLS, dtype=F32), shape(ROWS, 128, dtype=F32)),
        [SMEM] + [VMEM] * 6,
    )(scal, got, idc, idr, dt_bias, decay_rate, skip_gain)

    others = [
        by_chips(first, 1),
        by_chips(first, -1),
        by_chips(first[: 2 * WROWS], 2),
        by_chips(first[WROWS : 3 * WROWS], -2),
    ]
    first, xn = lax.optimization_barrier((first, xn))
    weights = jnp.concatenate([first] + others, axis=0)
    sibling = swap(weights)

    pay, kid = kernel(
        project,
        2,
        12,
        (shape(ROWS, 256), shape(24, ROWS, dtype=F32)),
        [SMEM] + [VMEM] * 4,
        [pltpu.VMEM((D, 256), BF)],
    )(scal, xn, weights, sibling, states)
    q = kernel(
        query,
        5,
        52,
        shape(ROWS, COLS),
        [SMEM, VMEM, ANY],
        [pltpu.VMEM((4, D, 256), BF), pltpu.SemaphoreType.DMA((4,))],
    )(scal, xn, wq)

    back4, back8 = by_chips(pay, 4), by_chips(pay, 8)
    near = jnp.concatenate([pay, back4], axis=0)
    far = jnp.concatenate([back4, back8], axis=0)
    own0 = jnp.concatenate([pay, back4, back8], axis=0)
    own1 = jnp.concatenate([by_chips(near, 1), by_chips(near, 2), by_chips(far, -1)], axis=0)
    sib0, sib1 = swap(own0), swap(own1)

    produced = kernel(
        finish,
        6,
        32,
        shape(ROWS, COLS),
        [SMEM] + [VMEM] * 10,
        [
            pltpu.VMEM((18 * ROWS, HD), BF),
            pltpu.VMEM((18 * ROWS, HD), BF),
            pltpu.VMEM((ROWS, 18 * ROWS), F32),
        ],
    )(scal, hidden_in[0], q, own0, own1, sib0, sib1, kid, yloc, aux, idc)
    moved = lax.ppermute(produced, "pipe", [(i, i + 1) for i in range(3)])
    return (produced[None], moved[None])


def solution(mesh):
    in_specs = (
        P("pipe", "ctx", "tp"),
        P("ctx"),
        P("pipe"),
        P("pipe", "tp"),
        P("pipe", "ctx", "tp"),
        P("pipe", "ctx", "tp"),
        P("pipe", "ctx", "tp"),
        P("pipe", "tp", None),
        P("pipe", "tp", None),
        P("pipe", "tp"),
        P("pipe", "tp"),
        P("pipe", "tp"),
    )
    out_specs = (P("pipe", "ctx", "tp"), P("pipe", "ctx", "tp"))
    return jax.shard_map(shards, mesh=mesh, in_specs=in_specs, out_specs=out_specs, check_vma=False)
```

time: 167 us -> 153 us (0.916)
  the two profiles are of different devices: /device:TPU:60 before, /device:TPU:12 now
where the time goes in v2:
time: 153 us; the launch traced here: 152 us
  starting transfers between devices  80.2 us (52%)
  waiting for transfers between devices  29.1 us (19%)
  between operations  15.1 us (10%)
  Pallas kernels  12.7 us (8%)
  local copies, waits for them, and re-layouts  11.1 us (7%)
  other arithmetic  4.15 us (3%)
    ppermute x12, starting transfers between devices, by_chips(): lax.ppermute(x, 'ctx', [(i, (i + 2 * k) % (2 * CHIPS)) for i in range(2 *...  66.1 us
    ppermute x12, waiting for transfers between devices, by_chips(): lax.ppermute(x, 'ctx', [(i, (i + 2 * k) % (2 * CHIPS)) for i in range(2 *...  18.1 us
    ppermute x1, waiting for transfers between devices, shards(): moved = lax.ppermute(produced, 'pipe', [(i, i + 1) for i in range(3)])  7.44 us
    unnamed x25, local copies, waits for them, and re-layouts  6.5 us
    ppermute x3, starting transfers between devices, swap(): return lax.ppermute(x, 'ctx', [(i, i ^ 1) for i in range(2 * CHIPS)])  5.76 us
    pallas_call x1, Pallas kernels, shards(): kernel(finish, 6, 32, shape(ROWS, COLS), [SMEM] + [VMEM] * 10, [pltpu.VME...  5.51 us
    pallas_call x1, Pallas kernels, shards(): kernel(query, 5, 52, shape(ROWS, COLS), [SMEM, VMEM, ANY], [pltpu.VMEM((4...  4.94 us
    all_to_all x1, starting transfers between devices, shards(): got = lax.all_to_all(parts, 'tp', 0, 0)  4.93 us
  transfers between devices with their start and end apart: 18, of which 8 were waited for; matrix products, arithmetic and copies ran while one was open for 10% of the time, Pallas kernels for 5%

profile of v2, /device:TPU:12, one launch (start us, length us, event | category | flops | bytes accessed | tf_op | source)
XLA Modules:
  0.0 152.3 jit_solution(15753466116621728535)
XLA Ops:
  7.2 0.0 all-gather.3.cloned.1.call-start
  7.2 0.7 all-gather.3.cloned.1.call-update
  7.9 0.7 convert_bitcast_fusion.1
  8.6 0.8 pad_maximum_fusion.2
  9.4 9.1 %collective-permute-start = (bf16[144,256]{1,0:T(8,128)(2,1)S(1)}, bf16[144,256]{1,0:T(8,128)(2,1)S(1)}, u32[]{:S(2)}, u32[]{:S(2)}) collective-permute-start(bf16[144,256]{1,0:T(8,128)(2,1)S(1)} %pad_maximum_fusion.2), channel_id=1, source_target_pairs={{0,32},{4,36},{8,40},{12,44},{16,48},{20,52},{24,56},{28,60},{32,6... | collective-permute-start | bytes 221192 | tf_op jit(solution)/shard_map/ppermute | solution.py:265
  18.5 5.6 %collective-permute-start.1 = (bf16[144,256]{1,0:T(8,128)(2,1)S(1)}, bf16[144,256]{1,0:T(8,128)(2,1)S(1)}, u32[]{:S(2)}, u32[]{:S(2)}) collective-permute-start(bf16[144,256]{1,0:T(8,128)(2,1)S(1)} %pad_maximum_fusion.2), channel_id=1, source_target_pairs={{0,96},{4,100},{8,104},{12,108},{16,112},{20,116},{24,120},{28,124... | collective-permute-start | bytes 221192 | tf_op jit(solution)/shard_map/ppermute | solution.py:265
  24.0 10.8 %collective-permute-start.2 = (bf16[144,256]{1,0:T(8,128)(2,1)S(1)}, bf16[144,256]{1,0:T(8,128)(2,1)S(1)}, u32[]{:S(2)}, u32[]{:S(2)}) collective-permute-start(bf16[144,256]{1,0:T(8,128)(2,1)S(1)} %pad_maximum_fusion.2), channel_id=1, source_target_pairs={{0,64},{4,68},{8,72},{12,76},{16,80},{20,84},{24,88},{28,92},{32,9... | collective-permute-start | bytes 221192 | tf_op jit(solution)/shard_map/ppermute | solution.py:265
  34.9 0.1 pad.19.clone
  34.9 0.7 reduce-precision_convert_fusion.1
  35.6 0.1 maximum_maximum_fusion
  35.7 0.9 broadcast_in_dim.33
  36.6 1.1 broadcast_in_dim.32
  37.7 0.0 copy-start.5
  37.7 0.0 copy-start.6
  37.7 1.3 pad_maximum_fusion
  39.0 0.0 collective-permute-done
  39.0 0.6 constant_dynamic-update-slice_fusion.3
  39.7 0.6 maximum_dynamic-update-slice_fusion
  40.3 0.6 constant_dynamic-update-slice_fusion.2
  40.9 0.0 collective-permute-done.1
  40.9 0.6 constant_dynamic-update-slice_fusion.1
  41.5 0.0 collective-permute-done.2
  41.5 0.6 constant_dynamic-update-slice_fusion
  42.1 4.9 %all-to-all-start = ((bf16[4,192,1024]{2,1,0:T(8,128)(2,1)}), bf16[4,192,1024]{2,1,0:T(8,128)(2,1)S(1)}, u32[]{:S(2)}, u32[]{:S(2)}) async-start(bf16[4,192,1024]{2,1,0:T(8,128)(2,1)} %pad_maximum_fusion), calls=%async_computation | async-start | bytes 3145728 | tf_op jit(solution)/shard_map/all_to_all | solution.py:315
  47.7 0.1 copy.14.idc_ref.idc
  47.9 0.1 stack.22.scal
  47.9 7.6 %collective-permute-start.3 = (bf16[576,256]{1,0:T(8,128)(2,1)}, bf16[576,256]{1,0:T(8,128)(2,1)}, u32[]{:S(2)}, u32[]{:S(2)}) collective-permute-start(bf16[576,256]{1,0:T(8,128)(2,1)} %constant_dynamic-update-slice_fusion), channel_id=1, source_target_pairs={{0,8},{4,12},{8,16},{12,20},{16,24},{20,28},{24,32},{28,36},{32,40... | collective-permute-start | bytes 884744 | tf_op jit(solution)/shard_map/ppermute | solution.py:265
  55.6 4.4 %collective-permute-start.4 = (bf16[576,256]{1,0:T(8,128)(2,1)}, bf16[576,256]{1,0:T(8,128)(2,1)}, u32[]{:S(2)}, u32[]{:S(2)}) collective-permute-start(bf16[576,256]{1,0:T(8,128)(2,1)} %constant_dynamic-update-slice_fusion), channel_id=1, source_target_pairs={{0,120},{4,124},{8,0},{12,4},{16,8},{20,12},{24,16},{28,20},{32,24... | collective-permute-start | bytes 884744 | tf_op jit(solution)/shard_map/ppermute | solution.py:265
  60.0 1.7 %fusion.1 = (bf16[288,256]{1,0:T(8,128)(2,1)}, bf16[288,256]{1,0:T(8,128)(2,1)}) fusion(bf16[576,256]{1,0:T(8,128)(2,1)} %constant_dynamic-update-slice_fusion), kind=kLoop, calls=%fused_computation.30 | loop fusion | bytes 589824 | tf_op jit(solution)/shard_map/slice | solution.py:328
  61.7 1.9 %collective-permute-start.5 = (bf16[288,256]{1,0:T(8,128)(2,1)}, bf16[288,256]{1,0:T(8,128)(2,1)}, u32[]{:S(2)}, u32[]{:S(2)}) collective-permute-start(bf16[288,256]{1,0:T(8,128)(2,1)} %get-tuple-element.23), channel_id=1, source_target_pairs={{0,16},{4,20},{8,24},{12,28},{16,32},{20,36},{24,40},{28,44},{32,4... | collective-permute-start | bytes 442376 | tf_op jit(solution)/shard_map/ppermute | solution.py:265
  63.6 6.0 %collective-permute-start.6 = (bf16[288,256]{1,0:T(8,128)(2,1)}, bf16[288,256]{1,0:T(8,128)(2,1)S(1)}, u32[]{:S(2)}, u32[]{:S(2)}) collective-permute-start(bf16[288,256]{1,0:T(8,128)(2,1)} %get-tuple-element.22), channel_id=1, source_target_pairs={{0,112},{4,116},{8,120},{12,124},{16,0},{20,4},{24,8},{28,12},{32,... | collective-permute-start | bytes 442376 | tf_op jit(solution)/shard_map/ppermute | solution.py:265
  69.6 0.0 all-to-all-done.got
  69.7 1.1 front.1
  70.8 1.0 constant_dynamic-update-slice_fusion.8
  71.7 0.4 collective-permute-done.3
  72.1 1.0 constant_dynamic-update-slice_fusion.7
  73.1 1.8 %collective-permute-done.4 = bf16[576,256]{1,0:T(8,128)(2,1)} collective-permute-done((bf16[576,256]{1,0:T(8,128)(2,1)}, bf16[576,256]{1,0:T(8,128)(2,1)}, u32[]{:S(2)}, u32[]{:S(2)}) %collective-permute-start.4) | collective-permute-done | bytes 294944 | tf_op jit(solution)/shard_map/ppermute | solution.py:265
  74.9 1.0 constant_dynamic-update-slice_fusion.6
  75.9 6.5 %collective-permute-done.5 = bf16[288,256]{1,0:T(8,128)(2,1)} collective-permute-done((bf16[288,256]{1,0:T(8,128)(2,1)}, bf16[288,256]{1,0:T(8,128)(2,1)}, u32[]{:S(2)}, u32[]{:S(2)}) %collective-permute-start.5) | collective-permute-done | bytes 147488 | tf_op jit(solution)/shard_map/ppermute | solution.py:265
  82.3 0.9 constant_dynamic-update-slice_fusion.5
  83.3 1.9 %collective-permute-start.7 = (bf16[2304,256]{1,0:T(8,128)(2,1)S(1)}, bf16[2304,256]{1,0:T(8,128)(2,1)S(1)}, u32[]{:S(2)}, u32[]{:S(2)}) collective-permute-start(bf16[2304,256]{1,0:T(8,128)(2,1)S(1)} %constant_dynamic-update-slice_fusion.4.own), channel_id=1, source_target_pairs={{0,4},{4,0},{8,12},{12,8},{16,20},{20,16},{24,28},{28,24},{32,36},... | collective-permute-start | bytes 3538952 | tf_op jit(solution)/shard_map/ppermute | solution.py:269
  85.2 2.8 %collective-permute-done.7.sib = bf16[2304,256]{1,0:T(8,128)(2,1)S(1)} collective-permute-done((bf16[2304,256]{1,0:T(8,128)(2,1)S(1)}, bf16[2304,256]{1,0:T(8,128)(2,1)S(1)}, u32[]{:S(2)}, u32[]{:S(2)}) %collective-permute-start.7) | collective-permute-done | bytes 1179680 | tf_op jit(solution)/shard_map/ppermute | solution.py:269
  88.0 1.2 project.1
  89.2 2.7 %collective-permute-start.8 = (bf16[128,256]{1,0:T(8,128)(2,1)S(1)}, bf16[128,256]{1,0:T(8,128)(2,1)S(1)}, u32[]{:S(2)}, u32[]{:S(2)}) collective-permute-start(bf16[128,256]{1,0:T(8,128)(2,1)S(1)} %get-tuple-element.18), channel_id=1, source_target_pairs={{0,32},{4,36},{8,40},{12,44},{16,48},{20,52},{24,56},{28,60},{32,6... | collective-permute-start | bytes 196616 | tf_op jit(solution)/shard_map/ppermute | solution.py:265
  91.9 8.6 %collective-permute-start.9 = (bf16[128,256]{1,0:T(8,128)(2,1)S(1)}, bf16[128,256]{1,0:T(8,128)(2,1)S(1)}, u32[]{:S(2)}, u32[]{:S(2)}) collective-permute-start(bf16[128,256]{1,0:T(8,128)(2,1)S(1)} %get-tuple-element.18), channel_id=1, source_target_pairs={{0,64},{4,68},{8,72},{12,76},{16,80},{20,84},{24,88},{28,92},{32,9... | collective-permute-start | bytes 196616 | tf_op jit(solution)/shard_map/ppermute | solution.py:265
  100.5 2.1 %collective-permute-done.8 = bf16[128,256]{1,0:T(8,128)(2,1)S(1)} collective-permute-done((bf16[128,256]{1,0:T(8,128)(2,1)S(1)}, bf16[128,256]{1,0:T(8,128)(2,1)S(1)}, u32[]{:S(2)}, u32[]{:S(2)}) %collective-permute-start.8) | collective-permute-done | bytes 65568 | tf_op jit(solution)/shard_map/ppermute | solution.py:265
  102.7 2.8 %collective-permute-start.10 = (bf16[256,256]{1,0:T(8,128)(2,1)S(1)}, bf16[256,256]{1,0:T(8,128)(2,1)S(1)}, u32[]{:S(2)}, u32[]{:S(2)}) collective-permute-start(bf16[256,256]{1,0:T(8,128)(2,1)S(1)} %get-tuple-element.24), channel_id=1, source_target_pairs={{0,8},{4,12},{8,16},{12,20},{16,24},{20,28},{24,32},{28,36},{32,40... | collective-permute-start | bytes 393224 | tf_op jit(solution)/shard_map/ppermute | solution.py:265
  105.5 4.0 %collective-permute-start.11 = (bf16[256,256]{1,0:T(8,128)(2,1)S(1)}, bf16[256,256]{1,0:T(8,128)(2,1)S(1)}, u32[]{:S(2)}, u32[]{:S(2)}) collective-permute-start(bf16[256,256]{1,0:T(8,128)(2,1)S(1)} %get-tuple-element.24), channel_id=1, source_target_pairs={{0,16},{4,20},{8,24},{12,28},{16,32},{20,36},{24,40},{28,44},{32,4... | collective-permute-start | bytes 393224 | tf_op jit(solution)/shard_map/ppermute | solution.py:265
  109.5 2.5 %collective-permute-done.9 = bf16[128,256]{1,0:T(8,128)(2,1)S(1)} collective-permute-done((bf16[128,256]{1,0:T(8,128)(2,1)S(1)}, bf16[128,256]{1,0:T(8,128)(2,1)S(1)}, u32[]{:S(2)}, u32[]{:S(2)}) %collective-permute-start.9) | collective-permute-done | bytes 65568 | tf_op jit(solution)/shard_map/ppermute | solution.py:265
  112.0 2.6 %collective-permute-start.12 = (bf16[256,256]{1,0:T(8,128)(2,1)S(1)}, bf16[256,256]{1,0:T(8,128)(2,1)S(1)}, u32[]{:S(2)}, u32[]{:S(2)}) collective-permute-start(bf16[256,256]{1,0:T(8,128)(2,1)S(1)} %pad_maximum_fusion.1), channel_id=1, source_target_pairs={{0,120},{4,124},{8,0},{12,4},{16,8},{20,12},{24,16},{28,20},{32,24... | collective-permute-start | bytes 393224 | tf_op jit(solution)/shard_map/ppermute | solution.py:265
  114.6 1.9 %collective-permute-start.13 = (bf16[384,256]{1,0:T(8,128)(2,1)S(1)}, bf16[384,256]{1,0:T(8,128)(2,1)S(1)}, u32[]{:S(2)}, u32[]{:S(2)}) collective-permute-start(bf16[384,256]{1,0:T(8,128)(2,1)S(1)} %constant_dynamic-update-slice_fusion.9.own0), channel_id=1, source_target_pairs={{0,4},{4,0},{8,12},{12,8},{16,20},{20,16},{24,28},{28,24},{32,36},... | collective-permute-start | bytes 589832 | tf_op jit(solution)/shard_map/ppermute | solution.py:269
  116.6 0.0 collective-permute-done.10
  116.6 4.9 %collective-permute-done.11 = bf16[256,256]{1,0:T(8,128)(2,1)S(1)} collective-permute-done((bf16[256,256]{1,0:T(8,128)(2,1)S(1)}, bf16[256,256]{1,0:T(8,128)(2,1)S(1)}, u32[]{:S(2)}, u32[]{:S(2)}) %collective-permute-start.11) | collective-permute-done | bytes 131104 | tf_op jit(solution)/shard_map/ppermute | solution.py:265
  121.5 0.0 collective-permute-done.12
  121.5 1.9 %collective-permute-start.14 = (bf16[768,256]{1,0:T(8,128)(2,1)S(1)}, bf16[768,256]{1,0:T(8,128)(2,1)S(1)}, u32[]{:S(2)}, u32[]{:S(2)}) collective-permute-start(bf16[768,256]{1,0:T(8,128)(2,1)S(1)} %constant_dynamic-update-slice_fusion.14.own1), channel_id=1, source_target_pairs={{0,4},{4,0},{8,12},{12,8},{16,20},{20,16},{24,28},{28,24},{32,36},... | collective-permute-start | bytes 1179656 | tf_op jit(solution)/shard_map/ppermute | solution.py:269
  123.5 0.0 all-gather.3.cloned.1.call-done
  123.5 0.0 copy-start
  123.5 4.9 %query.1.q = bf16[128,1024]{1,0:T(8,128)(2,1)S(1)} custom-call(s32[5]{0:T(128)S(1)} %stack.22.scal, bf16[128,4096]{1,0:T(8,128)(2,1)S(1)} %get-tuple-element.15.xn, bf16[4096,1024]{1,0:T(8,128)(2,1)} %bitcast.33), custom_call_target="tpu_custom_call" | custom-call | flops 5750000128 | bytes 1048576 | tf_op jit(solution)/shard_map/query/pallas_call | solution.py:342
  128.4 0.0 collective-permute-done.13.sib0
  128.5 0.0 collective-permute-done.14.sib1
  128.5 5.5 %finish.1 = bf16[128,1024]{1,0:T(8,128)(2,1)} custom-call(s32[5]{0:T(128)S(1)} %stack.22.scal, bf16[128,1024]{1,0:T(8,128)(2,1)S(1)} %bitcast.25, bf16[128,1024]{1,0:T(8,128)(2,1)S(1)} %query.1.q, bf16[384,256]{1,0:T(8,128)(2,1)S(1)} %constant_dynamic-update-slice_fusion.9.own0, bf16[768,256]{1,0:T(8,128)(2,1)S(1)} %constant_dynamic-update-slice_fusion.14.own1, ...), custom_call_target="tpu_custom_call" | custom-call | flops 6899999744 | bytes 1048576 | tf_op jit(solution)/shard_map/finish/pallas_call | solution.py:358
  134.0 3.4 %collective-permute-start.15 = (bf16[128,1024]{1,0:T(8,128)(2,1)}, bf16[128,1024]{1,0:T(8,128)(2,1)S(1)}, u32[]{:S(2)}, u32[]{:S(2)}) collective-permute-start(bf16[128,1024]{1,0:T(8,128)(2,1)} %finish.1), channel_id=1, source_target_pairs={{0,128},{128,256},{256,384},{1,129},{129,257},{257,385},{2,130},{1... | collective-permute-start | bytes 786440 | tf_op jit(solution)/shard_map/ppermute | solution.py:370
  137.3 7.4 %collective-permute-done.15 = bf16[128,1024]{1,0:T(8,128)(2,1)S(1)} collective-permute-done((bf16[128,1024]{1,0:T(8,128)(2,1)}, bf16[128,1024]{1,0:T(8,128)(2,1)S(1)}, u32[]{:S(2)}, u32[]{:S(2)}) %collective-permute-start.15) | collective-permute-done | bytes 262176 | tf_op jit(solution)/shard_map/ppermute | solution.py:370
  144.8 0.7 copy.31
  (23 shorter events, 0.1 us)
Async XLA Ops:
  7.2 30.5 %copy-start.4 = (bf16[1,1024,64]{1,2,0:T(8,128)(2,1)S(1)}, bf16[1,1024,64]{1,2,0:T(8,128)(2,1)}, u32[]{:S(2)}) copy-start(bf16[1,1024,64]{1,2,0:T(8,128)(2,1)} %param.20) | copy-start | bytes 393220
  7.2 116.3 %all-gather.3.cloned.1.call-start = ((), (), s32[]{:S(2)}) async-start(), calls=%async_computation.1 | async-start | bytes 8650752 | tf_op jit(solution)/shard_map/all_gather | solution.py:293
  9.4 29.6 %collective-permute-start = (bf16[144,256]{1,0:T(8,128)(2,1)S(1)}, bf16[144,256]{1,0:T(8,128)(2,1)S(1)}, u32[]{:S(2)}, u32[]{:S(2)}) collective-permute-start(bf16[144,256]{1,0:T(8,128)(2,1)S(1)} %pad_maximum_fusion.2), channel_id=1, source_target_pairs={{0,32},{4,36},{8,40},{12,44},{16,48},{20,52},{24,56},{28,60},{32,6... | collective-permute-start | bytes 221192 | tf_op jit(solution)/shard_map/ppermute | solution.py:265
  18.5 22.4 %collective-permute-start.1 = (bf16[144,256]{1,0:T(8,128)(2,1)S(1)}, bf16[144,256]{1,0:T(8,128)(2,1)S(1)}, u32[]{:S(2)}, u32[]{:S(2)}) collective-permute-start(bf16[144,256]{1,0:T(8,128)(2,1)S(1)} %pad_maximum_fusion.2), channel_id=1, source_target_pairs={{0,96},{4,100},{8,104},{12,108},{16,112},{20,116},{24,120},{28,124... | collective-permute-start | bytes 221192 | tf_op jit(solution)/shard_map/ppermute | solution.py:265
  24.0 17.5 %collective-permute-start.2 = (bf16[144,256]{1,0:T(8,128)(2,1)S(1)}, bf16[144,256]{1,0:T(8,128)(2,1)S(1)}, u32[]{:S(2)}, u32[]{:S(2)}) collective-permute-start(bf16[144,256]{1,0:T(8,128)(2,1)S(1)} %pad_maximum_fusion.2), channel_id=1, source_target_pairs={{0,64},{4,68},{8,72},{12,76},{16,80},{20,84},{24,88},{28,92},{32,9... | collective-permute-start | bytes 221192 | tf_op jit(solution)/shard_map/ppermute | solution.py:265
  37.7 2.0 %copy-start.5 = (bf16[1,128,128]{2,1,0:T(8,128)(2,1)S(1)}, bf16[1,128,128]{2,1,0:T(8,128)(2,1)}, u32[]{:S(2)}) copy-start(bf16[1,128,128]{2,1,0:T(8,128)(2,1)} %param.18) | copy-start | bytes 98308
  37.7 1.9 %copy-start.6 = (bf16[1,128,128]{2,1,0:T(8,128)(2,1)S(1)}, bf16[1,128,128]{2,1,0:T(8,128)(2,1)}, u32[]{:S(2)}) copy-start(bf16[1,128,128]{2,1,0:T(8,128)(2,1)} %param.17) | copy-start | bytes 98308
  42.1 27.5 %copy-start.1 = (f32[1,16]{1,0:T(1,128)S(1)}, f32[1,16]{1,0:T(1,128)}, u32[]{:S(2)}) copy-start(f32[1,16]{1,0:T(1,128)} %bias.1) | copy-start | bytes 196
  42.1 27.5 %copy-start.2 = (f32[1,16]{1,0:T(1,128)S(1)}, f32[1,16]{1,0:T(1,128)}, u32[]{:S(2)}) copy-start(f32[1,16]{1,0:T(1,128)} %rate.1) | copy-start | bytes 196
  42.1 27.5 %copy-start.3 = (f32[1,16]{1,0:T(1,128)S(1)}, f32[1,16]{1,0:T(1,128)}, u32[]{:S(2)}) copy-start(f32[1,16]{1,0:T(1,128)} %skip.1) | copy-start | bytes 196
  42.1 27.5 %all-to-all-start = ((bf16[4,192,1024]{2,1,0:T(8,128)(2,1)}), bf16[4,192,1024]{2,1,0:T(8,128)(2,1)S(1)}, u32[]{:S(2)}, u32[]{:S(2)}) async-start(bf16[4,192,1024]{2,1,0:T(8,128)(2,1)} %pad_maximum_fusion), calls=%async_computation | async-start | bytes 3145728 | tf_op jit(solution)/shard_map/all_to_all | solution.py:315
  47.9 24.2 %collective-permute-start.3 = (bf16[576,256]{1,0:T(8,128)(2,1)}, bf16[576,256]{1,0:T(8,128)(2,1)}, u32[]{:S(2)}, u32[]{:S(2)}) collective-permute-start(bf16[576,256]{1,0:T(8,128)(2,1)} %constant_dynamic-update-slice_fusion), channel_id=1, source_target_pairs={{0,8},{4,12},{8,16},{12,20},{16,24},{20,28},{24,32},{28,36},{32,40... | collective-permute-start | bytes 884744 | tf_op jit(solution)/shard_map/ppermute | solution.py:265
  55.6 19.3 %collective-permute-start.4 = (bf16[576,256]{1,0:T(8,128)(2,1)}, bf16[576,256]{1,0:T(8,128)(2,1)}, u32[]{:S(2)}, u32[]{:S(2)}) collective-permute-start(bf16[576,256]{1,0:T(8,128)(2,1)} %constant_dynamic-update-slice_fusion), channel_id=1, source_target_pairs={{0,120},{4,124},{8,0},{12,4},{16,8},{20,12},{24,16},{28,20},{32,24... | collective-permute-start | bytes 884744 | tf_op jit(solution)/shard_map/ppermute | solution.py:265
  61.7 20.6 %collective-permute-start.5 = (bf16[288,256]{1,0:T(8,128)(2,1)}, bf16[288,256]{1,0:T(8,128)(2,1)}, u32[]{:S(2)}, u32[]{:S(2)}) collective-permute-start(bf16[288,256]{1,0:T(8,128)(2,1)} %get-tuple-element.23), channel_id=1, source_target_pairs={{0,16},{4,20},{8,24},{12,28},{16,32},{20,36},{24,40},{28,44},{32,4... | collective-permute-start | bytes 442376 | tf_op jit(solution)/shard_map/ppermute | solution.py:265
  63.6 19.6 %collective-permute-start.6 = (bf16[288,256]{1,0:T(8,128)(2,1)}, bf16[288,256]{1,0:T(8,128)(2,1)S(1)}, u32[]{:S(2)}, u32[]{:S(2)}) collective-permute-start(bf16[288,256]{1,0:T(8,128)(2,1)} %get-tuple-element.22), channel_id=1, source_target_pairs={{0,112},{4,116},{8,120},{12,124},{16,0},{20,4},{24,8},{28,12},{32,... | collective-permute-start | bytes 442376 | tf_op jit(solution)/shard_map/ppermute | solution.py:265
  83.3 4.7 %collective-permute-start.7 = (bf16[2304,256]{1,0:T(8,128)(2,1)S(1)}, bf16[2304,256]{1,0:T(8,128)(2,1)S(1)}, u32[]{:S(2)}, u32[]{:S(2)}) collective-permute-start(bf16[2304,256]{1,0:T(8,128)(2,1)S(1)} %constant_dynamic-update-slice_fusion.4.own), channel_id=1, source_target_pairs={{0,4},{4,0},{8,12},{12,8},{16,20},{20,16},{24,28},{28,24},{32,36},... | collective-permute-start | bytes 3538952 | tf_op jit(solution)/shard_map/ppermute | solution.py:269
  89.2 13.5 %collective-permute-start.8 = (bf16[128,256]{1,0:T(8,128)(2,1)S(1)}, bf16[128,256]{1,0:T(8,128)(2,1)S(1)}, u32[]{:S(2)}, u32[]{:S(2)}) collective-permute-start(bf16[128,256]{1,0:T(8,128)(2,1)S(1)} %get-tuple-element.18), channel_id=1, source_target_pairs={{0,32},{4,36},{8,40},{12,44},{16,48},{20,52},{24,56},{28,60},{32,6... | collective-permute-start | bytes 196616 | tf_op jit(solution)/shard_map/ppermute | solution.py:265
  91.9 20.1 %collective-permute-start.9 = (bf16[128,256]{1,0:T(8,128)(2,1)S(1)}, bf16[128,256]{1,0:T(8,128)(2,1)S(1)}, u32[]{:S(2)}, u32[]{:S(2)}) collective-permute-start(bf16[128,256]{1,0:T(8,128)(2,1)S(1)} %get-tuple-element.18), channel_id=1, source_target_pairs={{0,64},{4,68},{8,72},{12,76},{16,80},{20,84},{24,88},{28,92},{32,9... | collective-permute-start | bytes 196616 | tf_op jit(solution)/shard_map/ppermute | solution.py:265
  102.7 13.9 %collective-permute-start.10 = (bf16[256,256]{1,0:T(8,128)(2,1)S(1)}, bf16[256,256]{1,0:T(8,128)(2,1)S(1)}, u32[]{:S(2)}, u32[]{:S(2)}) collective-permute-start(bf16[256,256]{1,0:T(8,128)(2,1)S(1)} %get-tuple-element.24), channel_id=1, source_target_pairs={{0,8},{4,12},{8,16},{12,20},{16,24},{20,28},{24,32},{28,36},{32,40... | collective-permute-start | bytes 393224 | tf_op jit(solution)/shard_map/ppermute | solution.py:265
  105.5 16.0 %collective-permute-start.11 = (bf16[256,256]{1,0:T(8,128)(2,1)S(1)}, bf16[256,256]{1,0:T(8,128)(2,1)S(1)}, u32[]{:S(2)}, u32[]{:S(2)}) collective-permute-start(bf16[256,256]{1,0:T(8,128)(2,1)S(1)} %get-tuple-element.24), channel_id=1, source_target_pairs={{0,16},{4,20},{8,24},{12,28},{16,32},{20,36},{24,40},{28,44},{32,4... | collective-permute-start | bytes 393224 | tf_op jit(solution)/shard_map/ppermute | solution.py:265
  112.0 9.5 %collective-permute-start.12 = (bf16[256,256]{1,0:T(8,128)(2,1)S(1)}, bf16[256,256]{1,0:T(8,128)(2,1)S(1)}, u32[]{:S(2)}, u32[]{:S(2)}) collective-permute-start(bf16[256,256]{1,0:T(8,128)(2,1)S(1)} %pad_maximum_fusion.1), channel_id=1, source_target_pairs={{0,120},{4,124},{8,0},{12,4},{16,8},{20,12},{24,16},{28,20},{32,24... | collective-permute-start | bytes 393224 | tf_op jit(solution)/shard_map/ppermute | solution.py:265
  114.6 13.8 %collective-permute-start.13 = (bf16[384,256]{1,0:T(8,128)(2,1)S(1)}, bf16[384,256]{1,0:T(8,128)(2,1)S(1)}, u32[]{:S(2)}, u32[]{:S(2)}) collective-permute-start(bf16[384,256]{1,0:T(8,128)(2,1)S(1)} %constant_dynamic-update-slice_fusion.9.own0), channel_id=1, source_target_pairs={{0,4},{4,0},{8,12},{12,8},{16,20},{20,16},{24,28},{28,24},{32,36},... | collective-permute-start | bytes 589832 | tf_op jit(solution)/shard_map/ppermute | solution.py:269
  121.5 6.9 %collective-permute-start.14 = (bf16[768,256]{1,0:T(8,128)(2,1)S(1)}, bf16[768,256]{1,0:T(8,128)(2,1)S(1)}, u32[]{:S(2)}, u32[]{:S(2)}) collective-permute-start(bf16[768,256]{1,0:T(8,128)(2,1)S(1)} %constant_dynamic-update-slice_fusion.14.own1), channel_id=1, source_target_pairs={{0,4},{4,0},{8,12},{12,8},{16,20},{20,16},{24,28},{28,24},{32,36},... | collective-permute-start | bytes 1179656 | tf_op jit(solution)/shard_map/ppermute | solution.py:269
  123.5 5.0 %copy-start = (bf16[1,128,1024]{2,1,0:T(8,128)(2,1)S(1)}, bf16[1,128,1024]{2,1,0:T(8,128)(2,1)}, u32[]{:S(2)}) copy-start(bf16[1,128,1024]{2,1,0:T(8,128)(2,1)} %param.12) | copy-start | bytes 786436
  134.0 10.8 %collective-permute-start.15 = (bf16[128,1024]{1,0:T(8,128)(2,1)}, bf16[128,1024]{1,0:T(8,128)(2,1)S(1)}, u32[]{:S(2)}, u32[]{:S(2)}) collective-permute-start(bf16[128,1024]{1,0:T(8,128)(2,1)} %finish.1), channel_id=1, source_target_pairs={{0,128},{128,256},{256,384},{1,129},{129,257},{257,385},{2,130},{1... | collective-permute-start | bytes 786440 | tf_op jit(solution)/shard_map/ppermute | solution.py:370
Sparse Core Ops, SparseCore 0:
  10.1 107.3 all-gather.2

commit v3 on v2

--- a/solution.py
+++ b/solution.py
@@ -19,8 +19,8 @@
 EXACT = lax.Precision.HIGHEST
 
 W_FIRST = (-4, 0, 4, -8)
-W_REL = tuple(a + b for b in (0, -1, 1) for a in W_FIRST) + (-6, -2, 2, 6)
-KV_AT = {0: (0, 0), 4: (0, 1), 8: (0, 2), 1: (1, 0), 5: (1, 1), 2: (1, 2), 6: (1, 3), 3: (1, 4), 7: (1, 5)}
+W_REL = tuple(a + b for b in (0, -1, 1, 2) for a in W_FIRST)
+KV_AT = (0, 3, 5, 7, 1, 4, 6, 8, 2)
 
 
 def iota(shape, dim):
@@ -131,27 +131,9 @@
             out[:, j * 256 : (j + 1) * 256] = dot(xn[...], wbuf[j]).astype(BF)
 
 
-def attend(scal, h, q, blocks, kid, idc_ref, out, keys, values, mask):
-    chip, core = scal[2], scal[3]
-    idc = idc_ref[...]
-    n = 0
-    for r in range(BACK + 1):
-        which, k = KV_AT[r]
-        for mine in (True, False):
-            ref = blocks[which if mine else 2 + which]
-            rows = slice(n * ROWS, (n + 1) * ROWS)
-            keys[rows, :] = ref[k * ROWS : (k + 1) * ROWS, :HD]
-            values[rows, :] = ref[k * ROWS : (k + 1) * ROWS, HD:]
-            allowed = idc == kid[n : n + 1, :]
-            if r == 0 and mine:
-                allowed = allowed & (iota((ROWS, ROWS), 0) >= iota((ROWS, ROWS), 1))
-            else:
-                valid = core == 1 if r == 0 else chip >= r
-                allowed = allowed & (jnp.full((ROWS, ROWS), valid.astype(jnp.int32)) == 1)
-            mask[:, rows] = jnp.where(allowed, 0.0, NEG)
-            n += 1
+def attend(pairs, h, q, keys, values, mask, out):
     factor = HD ** (-0.5) * 1.4426950408889634
-    for j in range(4):
+    for j in pairs:
         at = 256 * j
         rows = jnp.concatenate([q[:, at : at + HD], q[:, at + HD : at + 256]], axis=0)
         scores = lax.dot_general(
@@ -166,77 +148,107 @@
         mixed = dot(jnp.concatenate(parts, axis=0), values[...])
         for i in range(2):
             o = (mixed[i * ROWS : (i + 1) * ROWS, :] / dens[i]).astype(BF).astype(F32)
-            cols = slice(j * 256 + i * HD, j * 256 + (i + 1) * HD)
-            out[:, cols] = (h[:, cols].astype(F32) + o).astype(BF)
-
-
-def finish_states(scal, h, blocks, kid, yloc, aux, idc_ref, out):
-    core, device = scal[3], scal[4]
-    order = []
-    for r in range(1, BACK + 1):
+            cols = slice(at + i * HD, at + (i + 1) * HD)
+            out[:, at - 256 * pairs[0] + i * HD : at - 256 * pairs[0] + (i + 1) * HD] = (h[:, cols].astype(F32) + o).astype(BF)
+
+
+def assemble(scal, own, sib, kid, aux, idc_ref, keys, values, mask, incoming, reach):
+    idc = idc_ref[...]
+    chip, core, device = scal[2], scal[3], scal[4]
+
+    @pl.when(scal[0] == 1)
+    def _():
+        n = 0
+        for r in range(BACK + 1):
+            k = KV_AT[r]
+            for mine in (True, False):
+                ref = own if mine else sib
+                rows = slice(n * ROWS, (n + 1) * ROWS)
+                keys[rows, :] = ref[k * ROWS : (k + 1) * ROWS, :HD]
+                values[rows, :] = ref[k * ROWS : (k + 1) * ROWS, HD:]
+                allowed = idc == kid[n : n + 1, :]
+                if r == 0 and mine:
+                    allowed = allowed & (iota((ROWS, ROWS), 0) >= iota((ROWS, ROWS), 1))
+                else:
+                    valid = core == 1 if r == 0 else chip >= r
+                    allowed = allowed & (jnp.full((ROWS, ROWS), valid.astype(jnp.int32)) == 1)
+                mask[:, rows] = jnp.where(allowed, 0.0, NEG)
+                n += 1
+
+    @pl.when(scal[0] == 0)
+    def _():
         def block(mine, back):
-            which, k = KV_AT[back]
-            return blocks[which if mine else 2 + which], k * ROWS, 2 * back + (0 if mine else 1)
-
-        order.append((block(False, r - 1), block(False, r)))
-        order.append((block(True, r), None))
-
-    def read(entry, lo, hi):
-        (ref, at, _), other = entry
-        tile = ref[at + lo : at + hi, :].astype(F32)
-        if other is not None:
-            ref, at, _ = other
-            tile = jnp.where(core == 1, tile, ref[at + lo : at + hi, :].astype(F32))
-        return tile
-
-    idc = idc_ref[...]
-    before = jnp.zeros((1, HL), F32)
-    coefs = []
-    previous = None
-    for k, entry in enumerate(order, 1):
-        n = entry[0][2]
-        tail = kid[n : n + 1, ROWS - 1 :]
-        if entry[1] is not None:
-            n = entry[1][2]
-            tail = jnp.where(core == 1, tail, kid[n : n + 1, ROWS - 1 :])
-        tail = jnp.where(device >= k, tail, -1.0)
-        if previous is None:
-            previous = tail
-        fits = (tail == previous) & (tail >= 0.0)
-        coefs.append(jnp.where(fits, jnp.exp(before), 0.0))
-        extra = read(entry, 64, 80)
-        before += extra[0:1, :HL] + extra[1:2, :HL] + extra[2:3, :HL]
-    spread = (iota((HL, COLS), 1) // 64 == iota((HL, COLS), 0)).astype(F32)
-    coef = dot(jnp.concatenate(coefs, axis=0), spread, EXACT)
-    cum, out_map = aux[:, :HL], aux[:, HL : HL + STATE]
-    reach = jnp.where(idc == previous, jnp.exp(cum), 0.0)
+            return own if mine else sib, KV_AT[back] * ROWS, 2 * back + (0 if mine else 1)
+
+        order = []
+        for r in range(1, BACK + 1):
+            order.append((block(False, r - 1), block(False, r)))
+            order.append((block(True, r), None))
+
+        def read(entry, lo, hi):
+            (ref, at, _), other = entry
+            tile = ref[at + lo : at + hi, :].astype(F32)
+            if other is not None:
+                ref, at, _ = other
+                tile = jnp.where(core == 1, tile, ref[at + lo : at + hi, :].astype(F32))
+            return tile
+
+        before = jnp.zeros((1, HL), F32)
+        coefs = []
+        previous = None
+        for k, entry in enumerate(order, 1):
+            tails = [kid[e[2] : e[2] + 1, ROWS - 1 :] for e in entry if e is not None]
+            tail = tails[0] if len(tails) == 1 else jnp.where(core == 1, tails[0], tails[1])
+            tail = jnp.where(device >= k, tail, -1.0)
+            if previous is None:
+                previous = tail
+            fits = (tail == previous) & (tail >= 0.0)
+            coefs.append(jnp.where(fits, jnp.exp(before), 0.0))
+            extra = read(entry, 64, 80)
+            before += extra[0:1, :HL] + extra[1:2, :HL] + extra[2:3, :HL]
+        spread = (iota((HL, COLS), 1) // 64 == iota((HL, COLS), 0)).astype(F32)
+        coef = dot(jnp.concatenate(coefs, axis=0), spread, EXACT)
+        for c in range(4):
+            total = jnp.zeros((STATE, 256), F32)
+            for k, entry in enumerate(order):
+                total += coef[k : k + 1, c * 256 : (c + 1) * 256] * read(entry, 16 * c, 16 * c + 16)
+            incoming[:, c * 256 : (c + 1) * 256] = total
+        cum = aux[:, :HL]
+        wide = jnp.where(idc == previous, jnp.exp(cum), 0.0)
+        reach[...] = jnp.concatenate([wide, jnp.zeros((ROWS, ROWS - HL), F32)], axis=1)
+
+
+def finish_states(pairs, h, yloc, aux, incoming, reach_ref, out):
+    out_map, reach = aux[:, HL : HL + STATE], reach_ref[:, :HL]
     low = iota((ROWS, ROWS), 1) < 64
-    for c in range(4):
-        incoming = jnp.zeros((STATE, 256), F32)
-        for k, entry in enumerate(order):
-            incoming += coef[k : k + 1, c * 256 : (c + 1) * 256] * read(entry, 16 * c, 16 * c + 16)
-        for i in range(2):
-            j = 2 * c + i
-            cols = slice(j * 128, (j + 1) * 128)
-            carried = dot(out_map, incoming[:, i * 128 : (i + 1) * 128], EXACT) * pair(low, j, reach)
-            y = yloc[:, cols] + carried
-            y2 = y * y
-            one = jnp.sum(jnp.where(low, y2, 0.0), axis=1, keepdims=True)
-            two = jnp.sum(jnp.where(low, 0.0, y2), axis=1, keepdims=True)
-            scale = lax.rsqrt(jnp.where(low, one, two) / 64 + 1e-05)
-            out[:, cols] = (h[:, cols].astype(F32) + y * scale).astype(BF)
-
-
-def finish(scal, h, q, own0, own1, sib0, sib1, kid, yloc, aux, idc, out, keys, values, mask):
-    blocks = (own0, own1, sib0, sib1)
-
+    for n in range(2 * len(pairs)):
+        j = 2 * pairs[0] + n
+        cols = slice(j * 128, (j + 1) * 128)
+        carried = dot(out_map, incoming[:, cols], EXACT) * pair(low, j, reach)
+        y = yloc[:, cols] + carried
+        y2 = y * y
+        one = jnp.sum(jnp.where(low, y2, 0.0), axis=1, keepdims=True)
+        two = jnp.sum(jnp.where(low, 0.0, y2), axis=1, keepdims=True)
+        scale = lax.rsqrt(jnp.where(low, one, two) / 64 + 1e-05)
+        out[:, n * 128 : (n + 1) * 128] = (h[:, cols].astype(F32) + y * scale).astype(BF)
+
+
+def finish(pairs, scal, h, q, keys, values, mask, yloc, aux, incoming, reach, out):
     @pl.when(scal[0] == 1)
     def _():
-        attend(scal, h, q, blocks, kid, idc, out, keys, values, mask)
+        attend(pairs, h, q, keys, values, mask, out)
 
     @pl.when(scal[0] == 0)
     def _():
-        finish_states(scal, h, blocks, kid, yloc, aux, idc, out)
+        finish_states(pairs, h, yloc, aux, incoming, reach, out)
+
+
+def finish_low(*refs):
+    finish((0, 1, 2), *refs)
+
+
+def finish_high(*refs):
+    finish((3,), *refs)
 
 
 VMEM = pl.BlockSpec(memory_space=pltpu.VMEM)
@@ -321,12 +333,7 @@
         [SMEM] + [VMEM] * 6,
     )(scal, got, idc, idr, dt_bias, decay_rate, skip_gain)
 
-    others = [
-        by_chips(first, 1),
-        by_chips(first, -1),
-        by_chips(first[: 2 * WROWS], 2),
-        by_chips(first[WROWS : 3 * WROWS], -2),
-    ]
+    others = [by_chips(first, k) for k in (1, -1, -2)]
     first, xn = lax.optimization_barrier((first, xn))
     weights = jnp.concatenate([first] + others, axis=0)
     sibling = swap(weights)
@@ -351,23 +358,35 @@
     back4, back8 = by_chips(pay, 4), by_chips(pay, 8)
     near = jnp.concatenate([pay, back4], axis=0)
     far = jnp.concatenate([back4, back8], axis=0)
-    own0 = jnp.concatenate([pay, back4, back8], axis=0)
-    own1 = jnp.concatenate([by_chips(near, 1), by_chips(near, 2), by_chips(far, -1)], axis=0)
-    sib0, sib1 = swap(own0), swap(own1)
-
-    produced = kernel(
-        finish,
-        6,
-        32,
-        shape(ROWS, COLS),
-        [SMEM] + [VMEM] * 10,
-        [
-            pltpu.VMEM((18 * ROWS, HD), BF),
-            pltpu.VMEM((18 * ROWS, HD), BF),
-            pltpu.VMEM((ROWS, 18 * ROWS), F32),
-        ],
-    )(scal, hidden_in[0], q, own0, own1, sib0, sib1, kid, yloc, aux, idc)
-    moved = lax.ppermute(produced, "pipe", [(i, i + 1) for i in range(3)])
+    own = jnp.concatenate(
+        [pay, back4, back8, by_chips(near, 1), by_chips(near, 2), by_chips(far, -1)], axis=0
+    )
+    sib = swap(own)
+    sib, q = lax.optimization_barrier((sib, q))
+
+    gathered = kernel(
+        assemble,
+        1,
+        16,
+        (
+            shape(18 * ROWS, HD),
+            shape(18 * ROWS, HD),
+            shape(ROWS, 18 * ROWS, dtype=F32),
+            shape(STATE, COLS, dtype=F32),
+            shape(ROWS, ROWS, dtype=F32),
+        ),
+        [SMEM] + [VMEM] * 5,
+    )(scal, own, sib, kid, aux, idc)
+    keys, values, mask, incoming, reach = gathered
+    made, moved = [], []
+    for body, us, cols in ((finish_low, 4, 768), (finish_high, 2, 256)):
+        part = kernel(body, us, 20, shape(ROWS, cols), [SMEM] + [VMEM] * 9)(
+            scal, hidden_in[0], q, keys, values, mask, yloc, aux, incoming, reach
+        )
+        made.append(part)
+        q, part = lax.optimization_barrier((q, part))
+        moved.append(lax.ppermute(part, "pipe", [(i, i + 1) for i in range(3)]))
+    produced, moved = jnp.concatenate(made, axis=1), jnp.concatenate(moved, axis=1)
     return (produced[None], moved[None])
 
 

time: 153 us -> 160 us (1.046)
  the two profiles are of different devices: /device:TPU:12 before, /device:TPU:44 now
where the time goes in v3:
time: 160 us; the launch traced here: 159 us
  starting transfers between devices  74.8 us (47%)
  waiting for transfers between devices  42.2 us (26%)
  between operations  15 us (9%)
  Pallas kernels  13.7 us (9%)
  local copies, waits for them, and re-layouts  8.01 us (5%)
  other arithmetic  5.61 us (4%)
    ppermute x11, starting transfers between devices, by_chips(): lax.ppermute(x, 'ctx', [(i, (i + 2 * k) % (2 * CHIPS)) for i in range(2 *...  61.2 us
    ppermute x11, waiting for transfers between devices, by_chips(): lax.ppermute(x, 'ctx', [(i, (i + 2 * k) % (2 * CHIPS)) for i in range(2 *...  32.8 us
    pallas_call x2, Pallas kernels, shards(): kernel(body, us, 20, shape(ROWS, cols), [SMEM] + [VMEM] * 9)  5.75 us
    unnamed x26, local copies, waits for them, and re-layouts  4.96 us
    pallas_call x1, Pallas kernels, shards(): kernel(query, 5, 52, shape(ROWS, COLS), [SMEM, VMEM, ANY], [pltpu.VMEM((4...  4.94 us
    all_to_all x1, starting transfers between devices, shards(): got = lax.all_to_all(parts, 'tp', 0, 0)  4.93 us
    ppermute x2, starting transfers between devices, shards(): moved.append(lax.ppermute(part, 'pipe', [(i, i + 1) for i in range(3)]))  4.81 us
    ppermute x2, starting transfers between devices, swap(): return lax.ppermute(x, 'ctx', [(i, i ^ 1) for i in range(2 * CHIPS)])  3.84 us
  transfers between devices with their start and end apart: 17, of which 10 were waited for; matrix products, arithmetic and copies ran while one was open for 8% of the time, Pallas kernels for 6%

profile of v3, /device:TPU:44, one launch (start us, length us, event | category | flops | bytes accessed | tf_op | source)
XLA Modules:
  0.0 159.5 jit_solution(10745710015507149131)
XLA Ops:
  7.2 0.0 all-gather.3.cloned.1.call-start
  7.2 0.7 all-gather.3.cloned.1.call-update
  7.9 0.7 convert_bitcast_fusion.1
  8.6 0.8 pad_maximum_fusion.2
  9.4 9.1 %collective-permute-start = (bf16[144,256]{1,0:T(8,128)(2,1)S(1)}, bf16[144,256]{1,0:T(8,128)(2,1)S(1)}, u32[]{:S(2)}, u32[]{:S(2)}) collective-permute-start(bf16[144,256]{1,0:T(8,128)(2,1)S(1)} %pad_maximum_fusion.2), channel_id=1, source_target_pairs={{0,32},{4,36},{8,40},{12,44},{16,48},{20,52},{24,56},{28,60},{32,6... | collective-permute-start | bytes 221192 | tf_op jit(solution)/shard_map/ppermute | solution.py:277
  18.5 4.7 %collective-permute-start.1 = (bf16[144,256]{1,0:T(8,128)(2,1)S(1)}, bf16[144,256]{1,0:T(8,128)(2,1)S(1)}, u32[]{:S(2)}, u32[]{:S(2)}) collective-permute-start(bf16[144,256]{1,0:T(8,128)(2,1)S(1)} %pad_maximum_fusion.2), channel_id=1, source_target_pairs={{0,96},{4,100},{8,104},{12,108},{16,112},{20,116},{24,120},{28,124... | collective-permute-start | bytes 221192 | tf_op jit(solution)/shard_map/ppermute | solution.py:277
  23.1 10.8 %collective-permute-start.2 = (bf16[144,256]{1,0:T(8,128)(2,1)S(1)}, bf16[144,256]{1,0:T(8,128)(2,1)S(1)}, u32[]{:S(2)}, u32[]{:S(2)}) collective-permute-start(bf16[144,256]{1,0:T(8,128)(2,1)S(1)} %pad_maximum_fusion.2), channel_id=1, source_target_pairs={{0,64},{4,68},{8,72},{12,76},{16,80},{20,84},{24,88},{28,92},{32,9... | collective-permute-start | bytes 221192 | tf_op jit(solution)/shard_map/ppermute | solution.py:277
  34.0 0.1 pad.23.clone
  34.1 0.7 reduce-precision_convert_fusion.1
  34.8 0.1 maximum_maximum_fusion
  34.9 1.1 broadcast_in_dim.32
  36.0 0.0 copy-start.5
  36.0 0.0 copy-start.6
  36.0 1.3 pad_maximum_fusion
  37.3 0.0 collective-permute-done
  37.3 0.6 constant_dynamic-update-slice_fusion.3
  38.0 0.6 maximum_dynamic-update-slice_fusion
  38.6 0.6 constant_dynamic-update-slice_fusion.2
  39.2 0.0 collective-permute-done.1
  39.2 0.6 constant_dynamic-update-slice_fusion.1
  39.8 5.5 %collective-permute-done.2 = bf16[144,256]{1,0:T(8,128)(2,1)S(1)} collective-permute-done((bf16[144,256]{1,0:T(8,128)(2,1)S(1)}, bf16[144,256]{1,0:T(8,128)(2,1)S(1)}, u32[]{:S(2)}, u32[]{:S(2)}) %collective-permute-start.2) | collective-permute-done | bytes 73760 | tf_op jit(solution)/shard_map/ppermute | solution.py:277
  45.3 0.6 constant_dynamic-update-slice_fusion
  46.0 4.9 %all-to-all-start = ((bf16[4,192,1024]{2,1,0:T(8,128)(2,1)}), bf16[4,192,1024]{2,1,0:T(8,128)(2,1)S(1)}, u32[]{:S(2)}, u32[]{:S(2)}) async-start(bf16[4,192,1024]{2,1,0:T(8,128)(2,1)} %pad_maximum_fusion), calls=%async_computation | async-start | bytes 3145728 | tf_op jit(solution)/shard_map/all_to_all | solution.py:327
  51.6 0.1 copy.14.idc_ref
  51.7 0.1 stack.22.scal.refs_0_
  51.8 1.9 %collective-permute-start.3 = (bf16[576,256]{1,0:T(8,128)(2,1)}, bf16[576,256]{1,0:T(8,128)(2,1)}, u32[]{:S(2)}, u32[]{:S(2)}) collective-permute-start(bf16[576,256]{1,0:T(8,128)(2,1)} %constant_dynamic-update-slice_fusion), channel_id=1, source_target_pairs={{0,8},{4,12},{8,16},{12,20},{16,24},{20,28},{24,32},{28,36},{32,40... | collective-permute-start | bytes 884744 | tf_op jit(solution)/shard_map/ppermute | solution.py:277
  53.7 3.9 %collective-permute-start.4 = (bf16[576,256]{1,0:T(8,128)(2,1)}, bf16[576,256]{1,0:T(8,128)(2,1)}, u32[]{:S(2)}, u32[]{:S(2)}) collective-permute-start(bf16[576,256]{1,0:T(8,128)(2,1)} %constant_dynamic-update-slice_fusion), channel_id=1, source_target_pairs={{0,120},{4,124},{8,0},{12,4},{16,8},{20,12},{24,16},{28,20},{32,24... | collective-permute-start | bytes 884744 | tf_op jit(solution)/shard_map/ppermute | solution.py:277
  57.6 5.8 %collective-permute-start.5 = (bf16[576,256]{1,0:T(8,128)(2,1)}, bf16[576,256]{1,0:T(8,128)(2,1)}, u32[]{:S(2)}, u32[]{:S(2)}) collective-permute-start(bf16[576,256]{1,0:T(8,128)(2,1)} %constant_dynamic-update-slice_fusion), channel_id=1, source_target_pairs={{0,112},{4,116},{8,120},{12,124},{16,0},{20,4},{24,8},{28,12},{32,... | collective-permute-start | bytes 884744 | tf_op jit(solution)/shard_map/ppermute | solution.py:277
  63.5 2.8 %all-to-all-done.got = bf16[4,192,1024]{2,1,0:T(8,128)(2,1)S(1)} async-done(((bf16[4,192,1024]{2,1,0:T(8,128)(2,1)}), bf16[4,192,1024]{2,1,0:T(8,128)(2,1)S(1)}, u32[]{:S(2)}, u32[]{:S(2)}) %all-to-all-start) | async-done | bytes 1572896 | tf_op jit(solution)/shard_map/all_to_all | solution.py:327
  66.2 1.0 front.1
  67.3 1.0 constant_dynamic-update-slice_fusion.7
  68.3 0.4 collective-permute-done.3
  68.7 1.0 constant_dynamic-update-slice_fusion.6
  69.7 3.2 %collective-permute-done.4 = bf16[576,256]{1,0:T(8,128)(2,1)} collective-permute-done((bf16[576,256]{1,0:T(8,128)(2,1)}, bf16[576,256]{1,0:T(8,128)(2,1)}, u32[]{:S(2)}, u32[]{:S(2)}) %collective-permute-start.4) | collective-permute-done | bytes 294944 | tf_op jit(solution)/shard_map/ppermute | solution.py:277
  72.9 1.0 constant_dynamic-update-slice_fusion.5
  73.9 16.0 %collective-permute-done.5 = bf16[576,256]{1,0:T(8,128)(2,1)} collective-permute-done((bf16[576,256]{1,0:T(8,128)(2,1)}, bf16[576,256]{1,0:T(8,128)(2,1)}, u32[]{:S(2)}, u32[]{:S(2)}) %collective-permute-start.5) | collective-permute-done | bytes 294944 | tf_op jit(solution)/shard_map/ppermute | solution.py:277
  89.9 1.0 constant_dynamic-update-slice_fusion.4.own
  90.9 1.9 %collective-permute-start.6 = (bf16[2304,256]{1,0:T(8,128)(2,1)S(1)}, bf16[2304,256]{1,0:T(8,128)(2,1)S(1)}, u32[]{:S(2)}, u32[]{:S(2)}) collective-permute-start(bf16[2304,256]{1,0:T(8,128)(2,1)S(1)} %constant_dynamic-update-slice_fusion.4.own), channel_id=1, source_target_pairs={{0,4},{4,0},{8,12},{12,8},{16,20},{20,16},{24,28},{28,24},{32,36},... | collective-permute-start | bytes 3538952 | tf_op jit(solution)/shard_map/ppermute | solution.py:281
  92.8 2.8 %collective-permute-done.6.sib = bf16[2304,256]{1,0:T(8,128)(2,1)S(1)} collective-permute-done((bf16[2304,256]{1,0:T(8,128)(2,1)S(1)}, bf16[2304,256]{1,0:T(8,128)(2,1)S(1)}, u32[]{:S(2)}, u32[]{:S(2)}) %collective-permute-start.6) | collective-permute-done | bytes 1179680 | tf_op jit(solution)/shard_map/ppermute | solution.py:281
  95.6 1.2 project.1
  96.8 3.9 %collective-permute-start.7 = (bf16[128,256]{1,0:T(8,128)(2,1)S(1)}, bf16[128,256]{1,0:T(8,128)(2,1)S(1)}, u32[]{:S(2)}, u32[]{:S(2)}) collective-permute-start(bf16[128,256]{1,0:T(8,128)(2,1)S(1)} %get-tuple-element.28), channel_id=1, source_target_pairs={{0,32},{4,36},{8,40},{12,44},{16,48},{20,52},{24,56},{28,60},{32,6... | collective-permute-start | bytes 196616 | tf_op jit(solution)/shard_map/ppermute | solution.py:277
  100.7 11.0 %collective-permute-start.8 = (bf16[128,256]{1,0:T(8,128)(2,1)S(1)}, bf16[128,256]{1,0:T(8,128)(2,1)S(1)}, u32[]{:S(2)}, u32[]{:S(2)}) collective-permute-start(bf16[128,256]{1,0:T(8,128)(2,1)S(1)} %get-tuple-element.28), channel_id=1, source_target_pairs={{0,64},{4,68},{8,72},{12,76},{16,80},{20,84},{24,88},{28,92},{32,9... | collective-permute-start | bytes 196616 | tf_op jit(solution)/shard_map/ppermute | solution.py:277
  111.7 0.0 collective-permute-done.7
  111.7 3.7 %collective-permute-start.9 = (bf16[256,256]{1,0:T(8,128)(2,1)S(1)}, bf16[256,256]{1,0:T(8,128)(2,1)S(1)}, u32[]{:S(2)}, u32[]{:S(2)}) collective-permute-start(bf16[256,256]{1,0:T(8,128)(2,1)S(1)} %get-tuple-element.42), channel_id=1, source_target_pairs={{0,8},{4,12},{8,16},{12,20},{16,24},{20,28},{24,32},{28,36},{32,40... | collective-permute-start | bytes 393224 | tf_op jit(solution)/shard_map/ppermute | solution.py:277
  115.4 1.9 %collective-permute-start.10 = (bf16[256,256]{1,0:T(8,128)(2,1)S(1)}, bf16[256,256]{1,0:T(8,128)(2,1)S(1)}, u32[]{:S(2)}, u32[]{:S(2)}) collective-permute-start(bf16[256,256]{1,0:T(8,128)(2,1)S(1)} %get-tuple-element.42), channel_id=1, source_target_pairs={{0,16},{4,20},{8,24},{12,28},{16,32},{20,36},{24,40},{28,44},{32,4... | collective-permute-start | bytes 393224 | tf_op jit(solution)/shard_map/ppermute | solution.py:277
  117.4 0.0 collective-permute-done.8
  117.4 4.5 %collective-permute-start.11 = (bf16[256,256]{1,0:T(8,128)(2,1)S(1)}, bf16[256,256]{1,0:T(8,128)(2,1)S(1)}, u32[]{:S(2)}, u32[]{:S(2)}) collective-permute-start(bf16[256,256]{1,0:T(8,128)(2,1)S(1)} %pad_maximum_fusion.1), channel_id=1, source_target_pairs={{0,120},{4,124},{8,0},{12,4},{16,8},{20,12},{24,16},{28,20},{32,24... | collective-permute-start | bytes 393224 | tf_op jit(solution)/shard_map/ppermute | solution.py:277
  121.9 0.7 collective-permute-done.9
  122.6 6.1 %collective-permute-done.10 = bf16[256,256]{1,0:T(8,128)(2,1)S(1)} collective-permute-done((bf16[256,256]{1,0:T(8,128)(2,1)S(1)}, bf16[256,256]{1,0:T(8,128)(2,1)S(1)}, u32[]{:S(2)}, u32[]{:S(2)}) %collective-permute-start.10) | collective-permute-done | bytes 131104 | tf_op jit(solution)/shard_map/ppermute | solution.py:277
  128.7 0.8 collective-permute-done.11
  129.6 1.9 %collective-permute-start.12 = (bf16[1152,256]{1,0:T(8,128)(2,1)S(1)}, bf16[1152,256]{1,0:T(8,128)(2,1)S(1)}, u32[]{:S(2)}, u32[]{:S(2)}) collective-permute-start(bf16[1152,256]{1,0:T(8,128)(2,1)S(1)} %constant_dynamic-update-slice_fusion.10.own), channel_id=1, source_target_pairs={{0,4},{4,0},{8,12},{12,8},{16,20},{20,16},{24,28},{28,24},{32,36},... | collective-permute-start | bytes 1769480 | tf_op jit(solution)/shard_map/ppermute | solution.py:281
  131.5 0.0 all-gather.3.cloned.1.call-done
  131.5 4.9 %query.1.refs_2_ = bf16[128,1024]{1,0:T(8,128)(2,1)S(1)} custom-call(s32[5]{0:T(128)S(1)} %stack.22.scal.refs_0_, bf16[128,4096]{1,0:T(8,128)(2,1)S(1)} %get-tuple-element.25.xn, bf16[4096,1024]{1,0:T(8,128)(2,1)} %bitcast.35), custom_call_target="tpu_custom_call" | custom-call | flops 5750000128 | bytes 1048576 | tf_op jit(solution)/shard_map/query/pallas_call | solution.py:349
  136.5 0.0 collective-permute-done.12.sib
  136.5 0.0 copy-start
  136.5 0.8 assemble.1
  137.4 0.1 copy-done
  137.4 3.8 %finish_low.1 = bf16[128,768]{1,0:T(8,128)(2,1)S(1)} custom-call(s32[5]{0:T(128)S(1)} %stack.22.scal.refs_0_, bf16[128,1024]{1,0:T(8,128)(2,1)S(1)} %bitcast.27, bf16[128,1024]{1,0:T(8,128)(2,1)S(1)} %query.1.refs_2_, bf16[2304,128]{1,0:T(8,128)(2,1)S(1)} %get-tuple-element.33.refs_3_, bf16[2304,128]{1,0:T(8,128)(2,1)S(1)} %get-tuple-element.34.refs_4_, ...), custom_call_target="tpu_custom_call" | custom-call | flops 4600000000 | bytes 1048576 | tf_op jit(solution)/shard_map/finish_low/pallas_call | solution.py:383
  141.3 1.9 %collective-permute-start.13 = (bf16[128,768]{1,0:T(8,128)(2,1)S(1)}, bf16[128,768]{1,0:T(8,128)(2,1)S(1)}, u32[]{:S(2)}, u32[]{:S(2)}) collective-permute-start(bf16[128,768]{1,0:T(8,128)(2,1)S(1)} %finish_low.1), channel_id=1, source_target_pairs={{0,128},{128,256},{256,384},{1,129},{129,257},{257,385},{2,130},{1... | collective-permute-start | bytes 589832 | tf_op jit(solution)/shard_map/ppermute | solution.py:388
  143.2 1.9 %finish_high.1 = bf16[128,256]{1,0:T(8,128)(2,1)S(1)} custom-call(s32[5]{0:T(128)S(1)} %stack.22.scal.refs_0_, bf16[128,1024]{1,0:T(8,128)(2,1)S(1)} %bitcast.28, bf16[128,1024]{1,0:T(8,128)(2,1)S(1)} %query.1.refs_2_, bf16[2304,128]{1,0:T(8,128)(2,1)S(1)} %get-tuple-element.33.refs_3_, bf16[2304,128]{1,0:T(8,128)(2,1)S(1)} %get-tuple-element.34.refs_4_, ...), custom_call_target="tpu_custom_call" | custom-call | flops 2300000000 | bytes 1048576 | tf_op jit(solution)/shard_map/finish_high/pallas_call | solution.py:383
  145.1 2.9 %collective-permute-start.14 = (bf16[128,256]{1,0:T(8,128)(2,1)S(1)}, bf16[128,256]{1,0:T(8,128)(2,1)S(1)}, u32[]{:S(2)}, u32[]{:S(2)}) collective-permute-start(bf16[128,256]{1,0:T(8,128)(2,1)S(1)} %finish_high.1), channel_id=1, source_target_pairs={{0,128},{128,256},{256,384},{1,129},{129,257},{257,385},{2,130},{1... | collective-permute-start | bytes 196616 | tf_op jit(solution)/shard_map/ppermute | solution.py:388
  148.0 0.7 maximum_bitcast_fusion
  148.8 3.1 %collective-permute-done.14 = bf16[128,256]{1,0:T(8,128)(2,1)S(1)} collective-permute-done((bf16[128,256]{1,0:T(8,128)(2,1)S(1)}, bf16[128,256]{1,0:T(8,128)(2,1)S(1)}, u32[]{:S(2)}, u32[]{:S(2)}) %collective-permute-start.14) | collective-permute-done | bytes 65568 | tf_op jit(solution)/shard_map/ppermute | solution.py:388
  151.9 0.7 maximum_bitcast_fusion.1
  (24 shorter events, 0.1 us)
Async XLA Ops:
  7.2 28.8 %copy-start.7 = (bf16[1,1024,32]{1,2,0:T(8,128)(2,1)S(1)}, bf16[1,1024,32]{1,2,0:T(8,128)(2,1)}, u32[]{:S(2)}) copy-start(bf16[1,1024,32]{1,2,0:T(8,128)(2,1)} %param.19) | copy-start | bytes 196612
  7.2 28.8 %copy-start.4 = (bf16[1,1024,64]{1,2,0:T(8,128)(2,1)S(1)}, bf16[1,1024,64]{1,2,0:T(8,128)(2,1)}, u32[]{:S(2)}) copy-start(bf16[1,1024,64]{1,2,0:T(8,128)(2,1)} %param.20) | copy-start | bytes 393220
  7.2 124.3 %all-gather.3.cloned.1.call-start = ((), (), s32[]{:S(2)}) async-start(), calls=%async_computation.1 | async-start | bytes 8650752 | tf_op jit(solution)/shard_map/all_gather | solution.py:305
  9.4 27.9 %collective-permute-start = (bf16[144,256]{1,0:T(8,128)(2,1)S(1)}, bf16[144,256]{1,0:T(8,128)(2,1)S(1)}, u32[]{:S(2)}, u32[]{:S(2)}) collective-permute-start(bf16[144,256]{1,0:T(8,128)(2,1)S(1)} %pad_maximum_fusion.2), channel_id=1, source_target_pairs={{0,32},{4,36},{8,40},{12,44},{16,48},{20,52},{24,56},{28,60},{32,6... | collective-permute-start | bytes 221192 | tf_op jit(solution)/shard_map/ppermute | solution.py:277
  18.5 20.7 %collective-permute-start.1 = (bf16[144,256]{1,0:T(8,128)(2,1)S(1)}, bf16[144,256]{1,0:T(8,128)(2,1)S(1)}, u32[]{:S(2)}, u32[]{:S(2)}) collective-permute-start(bf16[144,256]{1,0:T(8,128)(2,1)S(1)} %pad_maximum_fusion.2), channel_id=1, source_target_pairs={{0,96},{4,100},{8,104},{12,108},{16,112},{20,116},{24,120},{28,124... | collective-permute-start | bytes 221192 | tf_op jit(solution)/shard_map/ppermute | solution.py:277
  23.1 22.2 %collective-permute-start.2 = (bf16[144,256]{1,0:T(8,128)(2,1)S(1)}, bf16[144,256]{1,0:T(8,128)(2,1)S(1)}, u32[]{:S(2)}, u32[]{:S(2)}) collective-permute-start(bf16[144,256]{1,0:T(8,128)(2,1)S(1)} %pad_maximum_fusion.2), channel_id=1, source_target_pairs={{0,64},{4,68},{8,72},{12,76},{16,80},{20,84},{24,88},{28,92},{32,9... | collective-permute-start | bytes 221192 | tf_op jit(solution)/shard_map/ppermute | solution.py:277
  36.0 2.0 %copy-start.5 = (bf16[1,128,128]{2,1,0:T(8,128)(2,1)S(1)}, bf16[1,128,128]{2,1,0:T(8,128)(2,1)}, u32[]{:S(2)}) copy-start(bf16[1,128,128]{2,1,0:T(8,128)(2,1)} %param.18) | copy-start | bytes 98308
  36.0 2.0 %copy-start.6 = (bf16[1,128,128]{2,1,0:T(8,128)(2,1)S(1)}, bf16[1,128,128]{2,1,0:T(8,128)(2,1)}, u32[]{:S(2)}) copy-start(bf16[1,128,128]{2,1,0:T(8,128)(2,1)} %param.17) | copy-start | bytes 98308
  46.0 20.3 %copy-start.1 = (f32[1,16]{1,0:T(1,128)S(1)}, f32[1,16]{1,0:T(1,128)}, u32[]{:S(2)}) copy-start(f32[1,16]{1,0:T(1,128)} %bias.1) | copy-start | bytes 196
  46.0 20.3 %copy-start.2 = (f32[1,16]{1,0:T(1,128)S(1)}, f32[1,16]{1,0:T(1,128)}, u32[]{:S(2)}) copy-start(f32[1,16]{1,0:T(1,128)} %rate.1) | copy-start | bytes 196
  46.0 20.3 %copy-start.3 = (f32[1,16]{1,0:T(1,128)S(1)}, f32[1,16]{1,0:T(1,128)}, u32[]{:S(2)}) copy-start(f32[1,16]{1,0:T(1,128)} %skip.1) | copy-start | bytes 196
  46.0 20.2 %all-to-all-start = ((bf16[4,192,1024]{2,1,0:T(8,128)(2,1)}), bf16[4,192,1024]{2,1,0:T(8,128)(2,1)S(1)}, u32[]{:S(2)}, u32[]{:S(2)}) async-start(bf16[4,192,1024]{2,1,0:T(8,128)(2,1)} %pad_maximum_fusion), calls=%async_computation | async-start | bytes 3145728 | tf_op jit(solution)/shard_map/all_to_all | solution.py:327
  51.8 16.9 %collective-permute-start.3 = (bf16[576,256]{1,0:T(8,128)(2,1)}, bf16[576,256]{1,0:T(8,128)(2,1)}, u32[]{:S(2)}, u32[]{:S(2)}) collective-permute-start(bf16[576,256]{1,0:T(8,128)(2,1)} %constant_dynamic-update-slice_fusion), channel_id=1, source_target_pairs={{0,8},{4,12},{8,16},{12,20},{16,24},{20,28},{24,32},{28,36},{32,40... | collective-permute-start | bytes 884744 | tf_op jit(solution)/shard_map/ppermute | solution.py:277
  53.7 19.2 %collective-permute-start.4 = (bf16[576,256]{1,0:T(8,128)(2,1)}, bf16[576,256]{1,0:T(8,128)(2,1)}, u32[]{:S(2)}, u32[]{:S(2)}) collective-permute-start(bf16[576,256]{1,0:T(8,128)(2,1)} %constant_dynamic-update-slice_fusion), channel_id=1, source_target_pairs={{0,120},{4,124},{8,0},{12,4},{16,8},{20,12},{24,16},{28,20},{32,24... | collective-permute-start | bytes 884744 | tf_op jit(solution)/shard_map/ppermute | solution.py:277
  57.6 32.3 %collective-permute-start.5 = (bf16[576,256]{1,0:T(8,128)(2,1)}, bf16[576,256]{1,0:T(8,128)(2,1)}, u32[]{:S(2)}, u32[]{:S(2)}) collective-permute-start(bf16[576,256]{1,0:T(8,128)(2,1)} %constant_dynamic-update-slice_fusion), channel_id=1, source_target_pairs={{0,112},{4,116},{8,120},{12,124},{16,0},{20,4},{24,8},{28,12},{32,... | collective-permute-start | bytes 884744 | tf_op jit(solution)/shard_map/ppermute | solution.py:277
  90.9 4.7 %collective-permute-start.6 = (bf16[2304,256]{1,0:T(8,128)(2,1)S(1)}, bf16[2304,256]{1,0:T(8,128)(2,1)S(1)}, u32[]{:S(2)}, u32[]{:S(2)}) collective-permute-start(bf16[2304,256]{1,0:T(8,128)(2,1)S(1)} %constant_dynamic-update-slice_fusion.4.own), channel_id=1, source_target_pairs={{0,4},{4,0},{8,12},{12,8},{16,20},{20,16},{24,28},{28,24},{32,36},... | collective-permute-start | bytes 3538952 | tf_op jit(solution)/shard_map/ppermute | solution.py:281
  96.8 14.9 %collective-permute-start.7 = (bf16[128,256]{1,0:T(8,128)(2,1)S(1)}, bf16[128,256]{1,0:T(8,128)(2,1)S(1)}, u32[]{:S(2)}, u32[]{:S(2)}) collective-permute-start(bf16[128,256]{1,0:T(8,128)(2,1)S(1)} %get-tuple-element.28), channel_id=1, source_target_pairs={{0,32},{4,36},{8,40},{12,44},{16,48},{20,52},{24,56},{28,60},{32,6... | collective-permute-start | bytes 196616 | tf_op jit(solution)/shard_map/ppermute | solution.py:277
  100.7 16.7 %collective-permute-start.8 = (bf16[128,256]{1,0:T(8,128)(2,1)S(1)}, bf16[128,256]{1,0:T(8,128)(2,1)S(1)}, u32[]{:S(2)}, u32[]{:S(2)}) collective-permute-start(bf16[128,256]{1,0:T(8,128)(2,1)S(1)} %get-tuple-element.28), channel_id=1, source_target_pairs={{0,64},{4,68},{8,72},{12,76},{16,80},{20,84},{24,88},{28,92},{32,9... | collective-permute-start | bytes 196616 | tf_op jit(solution)/shard_map/ppermute | solution.py:277
  111.7 10.8 %collective-permute-start.9 = (bf16[256,256]{1,0:T(8,128)(2,1)S(1)}, bf16[256,256]{1,0:T(8,128)(2,1)S(1)}, u32[]{:S(2)}, u32[]{:S(2)}) collective-permute-start(bf16[256,256]{1,0:T(8,128)(2,1)S(1)} %get-tuple-element.42), channel_id=1, source_target_pairs={{0,8},{4,12},{8,16},{12,20},{16,24},{20,28},{24,32},{28,36},{32,40... | collective-permute-start | bytes 393224 | tf_op jit(solution)/shard_map/ppermute | solution.py:277
  115.4 13.3 %collective-permute-start.10 = (bf16[256,256]{1,0:T(8,128)(2,1)S(1)}, bf16[256,256]{1,0:T(8,128)(2,1)S(1)}, u32[]{:S(2)}, u32[]{:S(2)}) collective-permute-start(bf16[256,256]{1,0:T(8,128)(2,1)S(1)} %get-tuple-element.42), channel_id=1, source_target_pairs={{0,16},{4,20},{8,24},{12,28},{16,32},{20,36},{24,40},{28,44},{32,4... | collective-permute-start | bytes 393224 | tf_op jit(solution)/shard_map/ppermute | solution.py:277
  117.4 12.2 %collective-permute-start.11 = (bf16[256,256]{1,0:T(8,128)(2,1)S(1)}, bf16[256,256]{1,0:T(8,128)(2,1)S(1)}, u32[]{:S(2)}, u32[]{:S(2)}) collective-permute-start(bf16[256,256]{1,0:T(8,128)(2,1)S(1)} %pad_maximum_fusion.1), channel_id=1, source_target_pairs={{0,120},{4,124},{8,0},{12,4},{16,8},{20,12},{24,16},{28,20},{32,24... | collective-permute-start | bytes 393224 | tf_op jit(solution)/shard_map/ppermute | solution.py:277
  129.6 6.9 %collective-permute-start.12 = (bf16[1152,256]{1,0:T(8,128)(2,1)S(1)}, bf16[1152,256]{1,0:T(8,128)(2,1)S(1)}, u32[]{:S(2)}, u32[]{:S(2)}) collective-permute-start(bf16[1152,256]{1,0:T(8,128)(2,1)S(1)} %constant_dynamic-update-slice_fusion.10.own), channel_id=1, source_target_pairs={{0,4},{4,0},{8,12},{12,8},{16,20},{20,16},{24,28},{28,24},{32,36},... | collective-permute-start | bytes 1769480 | tf_op jit(solution)/shard_map/ppermute | solution.py:281
  136.5 1.0 copy-start
  141.3 10.6 %collective-permute-start.13 = (bf16[128,768]{1,0:T(8,128)(2,1)S(1)}, bf16[128,768]{1,0:T(8,128)(2,1)S(1)}, u32[]{:S(2)}, u32[]{:S(2)}) collective-permute-start(bf16[128,768]{1,0:T(8,128)(2,1)S(1)} %finish_low.1), channel_id=1, source_target_pairs={{0,128},{128,256},{256,384},{1,129},{129,257},{257,385},{2,130},{1... | collective-permute-start | bytes 589832 | tf_op jit(solution)/shard_map/ppermute | solution.py:388
  145.1 6.8 %collective-permute-start.14 = (bf16[128,256]{1,0:T(8,128)(2,1)S(1)}, bf16[128,256]{1,0:T(8,128)(2,1)S(1)}, u32[]{:S(2)}, u32[]{:S(2)}) collective-permute-start(bf16[128,256]{1,0:T(8,128)(2,1)S(1)} %finish_high.1), channel_id=1, source_target_pairs={{0,128},{128,256},{256,384},{1,129},{129,257},{257,385},{2,130},{1... | collective-permute-start | bytes 196616 | tf_op jit(solution)/shard_map/ppermute | solution.py:388
Sparse Core Ops, SparseCore 0:
  10.1 109.3 all-gather.2

commit v4 on v3

--- a/solution.py
+++ b/solution.py
@@ -19,7 +19,7 @@
 EXACT = lax.Precision.HIGHEST
 
 W_FIRST = (-4, 0, 4, -8)
-W_REL = tuple(a + b for b in (0, -1, 1, 2) for a in W_FIRST)
+W_REL = tuple(a + b for b in (0, -1, 1) for a in W_FIRST) + (-6, -2, 2, 6)
 KV_AT = (0, 3, 5, 7, 1, 4, 6, 8, 2)
 
 
@@ -333,7 +333,12 @@
         [SMEM] + [VMEM] * 6,
     )(scal, got, idc, idr, dt_bias, decay_rate, skip_gain)
 
-    others = [by_chips(first, k) for k in (1, -1, -2)]
+    others = [
+        by_chips(first, 1),
+        by_chips(first, -1),
+        by_chips(first[: 2 * WROWS], 2),
+        by_chips(first[WROWS : 3 * WROWS], -2),
+    ]
     first, xn = lax.optimization_barrier((first, xn))
     weights = jnp.concatenate([first] + others, axis=0)
     sibling = swap(weights)

time: 160 us -> 153 us (0.956)
  the two profiles are of different devices: /device:TPU:44 before, /device:TPU:20 now
where the time goes in v4:
time: 153 us; the launch traced here: 152 us
  starting transfers between devices  80.6 us (53%)
  waiting for transfers between devices  27.2 us (18%)
  between operations  15.1 us (10%)
  Pallas kernels  13.7 us (9%)
  local copies, waits for them, and re-layouts  9.68 us (6%)
  other arithmetic  5.61 us (4%)
    ppermute x12, starting transfers between devices, by_chips(): lax.ppermute(x, 'ctx', [(i, (i + 2 * k) % (2 * CHIPS)) for i in range(2 *...  66.8 us
    ppermute x12, waiting for transfers between devices, by_chips(): lax.ppermute(x, 'ctx', [(i, (i + 2 * k) % (2 * CHIPS)) for i in range(2 *...  20.1 us
    unnamed x27, local copies, waits for them, and re-layouts  5.9 us
    pallas_call x2, Pallas kernels, shards(): kernel(body, us, 20, shape(ROWS, cols), [SMEM] + [VMEM] * 9)  5.75 us
    ppermute x2, starting transfers between devices, shards(): moved.append(lax.ppermute(part, 'pipe', [(i, i + 1) for i in range(3)]))  5.04 us
    pallas_call x1, Pallas kernels, shards(): kernel(query, 5, 52, shape(ROWS, COLS), [SMEM, VMEM, ANY], [pltpu.VMEM((4...  4.94 us
    all_to_all x1, starting transfers between devices, shards(): got = lax.all_to_all(parts, 'tp', 0, 0)  4.93 us
    ppermute x2, starting transfers between devices, swap(): return lax.ppermute(x, 'ctx', [(i, i ^ 1) for i in range(2 * CHIPS)])  3.84 us
  transfers between devices with their start and end apart: 18, of which 9 were waited for; matrix products, arithmetic and copies ran while one was open for 10% of the time, Pallas kernels for 6%

profile of v4, /device:TPU:20, one launch (start us, length us, event | category | flops | bytes accessed | tf_op | source)
XLA Modules:
  0.0 151.9 jit_solution(15812469882530067827)
XLA Ops:
  7.2 0.0 all-gather.3.cloned.1.call-start
  7.2 0.7 all-gather.3.cloned.1.call-update
  7.9 0.7 convert_bitcast_fusion.1
  8.6 0.8 pad_maximum_fusion.2
  9.4 9.1 %collective-permute-start = (bf16[144,256]{1,0:T(8,128)(2,1)S(1)}, bf16[144,256]{1,0:T(8,128)(2,1)S(1)}, u32[]{:S(2)}, u32[]{:S(2)}) collective-permute-start(bf16[144,256]{1,0:T(8,128)(2,1)S(1)} %pad_maximum_fusion.2), channel_id=1, source_target_pairs={{0,32},{4,36},{8,40},{12,44},{16,48},{20,52},{24,56},{28,60},{32,6... | collective-permute-start | bytes 221192 | tf_op jit(solution)/shard_map/ppermute | solution.py:277
  18.5 5.6 %collective-permute-start.1 = (bf16[144,256]{1,0:T(8,128)(2,1)S(1)}, bf16[144,256]{1,0:T(8,128)(2,1)S(1)}, u32[]{:S(2)}, u32[]{:S(2)}) collective-permute-start(bf16[144,256]{1,0:T(8,128)(2,1)S(1)} %pad_maximum_fusion.2), channel_id=1, source_target_pairs={{0,96},{4,100},{8,104},{12,108},{16,112},{20,116},{24,120},{28,124... | collective-permute-start | bytes 221192 | tf_op jit(solution)/shard_map/ppermute | solution.py:277
  24.0 10.8 %collective-permute-start.2 = (bf16[144,256]{1,0:T(8,128)(2,1)S(1)}, bf16[144,256]{1,0:T(8,128)(2,1)S(1)}, u32[]{:S(2)}, u32[]{:S(2)}) collective-permute-start(bf16[144,256]{1,0:T(8,128)(2,1)S(1)} %pad_maximum_fusion.2), channel_id=1, source_target_pairs={{0,64},{4,68},{8,72},{12,76},{16,80},{20,84},{24,88},{28,92},{32,9... | collective-permute-start | bytes 221192 | tf_op jit(solution)/shard_map/ppermute | solution.py:277
  34.9 0.1 pad.23.clone
  35.0 0.7 reduce-precision_convert_fusion.1
  35.7 0.1 maximum_maximum_fusion
  35.8 1.1 broadcast_in_dim.32
  36.9 0.0 copy-start.5
  36.9 0.0 copy-start.6
  36.9 1.3 pad_maximum_fusion
  38.2 0.6 constant_dynamic-update-slice_fusion.3
  38.8 0.6 maximum_dynamic-update-slice_fusion
  39.5 0.6 constant_dynamic-update-slice_fusion.2
  40.1 0.0 collective-permute-done.1
  40.1 0.6 constant_dynamic-update-slice_fusion.1
  40.7 0.0 collective-permute-done.2
  40.7 0.6 constant_dynamic-update-slice_fusion
  41.3 4.9 %all-to-all-start = ((bf16[4,192,1024]{2,1,0:T(8,128)(2,1)}), bf16[4,192,1024]{2,1,0:T(8,128)(2,1)S(1)}, u32[]{:S(2)}, u32[]{:S(2)}) async-start(bf16[4,192,1024]{2,1,0:T(8,128)(2,1)} %pad_maximum_fusion), calls=%async_computation | async-start | bytes 3145728 | tf_op jit(solution)/shard_map/all_to_all | solution.py:327
  46.9 0.1 copy.14.idc_ref
  47.0 0.1 stack.22.scal.refs_0_
  47.1 8.4 %collective-permute-start.3 = (bf16[576,256]{1,0:T(8,128)(2,1)}, bf16[576,256]{1,0:T(8,128)(2,1)}, u32[]{:S(2)}, u32[]{:S(2)}) collective-permute-start(bf16[576,256]{1,0:T(8,128)(2,1)} %constant_dynamic-update-slice_fusion), channel_id=1, source_target_pairs={{0,8},{4,12},{8,16},{12,20},{16,24},{20,28},{24,32},{28,36},{32,40... | collective-permute-start | bytes 884744 | tf_op jit(solution)/shard_map/ppermute | solution.py:277
  55.6 4.4 %collective-permute-start.4 = (bf16[576,256]{1,0:T(8,128)(2,1)}, bf16[576,256]{1,0:T(8,128)(2,1)}, u32[]{:S(2)}, u32[]{:S(2)}) collective-permute-start(bf16[576,256]{1,0:T(8,128)(2,1)} %constant_dynamic-update-slice_fusion), channel_id=1, source_target_pairs={{0,120},{4,124},{8,0},{12,4},{16,8},{20,12},{24,16},{28,20},{32,24... | collective-permute-start | bytes 884744 | tf_op jit(solution)/shard_map/ppermute | solution.py:277
  60.0 1.7 %fusion.1 = (bf16[288,256]{1,0:T(8,128)(2,1)}, bf16[288,256]{1,0:T(8,128)(2,1)}) fusion(bf16[576,256]{1,0:T(8,128)(2,1)} %constant_dynamic-update-slice_fusion), kind=kLoop, calls=%fused_computation.32 | loop fusion | bytes 589824 | tf_op jit(solution)/shard_map/slice | solution.py:340
  61.7 1.9 %collective-permute-start.5 = (bf16[288,256]{1,0:T(8,128)(2,1)}, bf16[288,256]{1,0:T(8,128)(2,1)}, u32[]{:S(2)}, u32[]{:S(2)}) collective-permute-start(bf16[288,256]{1,0:T(8,128)(2,1)} %get-tuple-element.43), channel_id=1, source_target_pairs={{0,16},{4,20},{8,24},{12,28},{16,32},{20,36},{24,40},{28,44},{32,4... | collective-permute-start | bytes 442376 | tf_op jit(solution)/shard_map/ppermute | solution.py:277
  63.6 6.0 %collective-permute-start.6 = (bf16[288,256]{1,0:T(8,128)(2,1)}, bf16[288,256]{1,0:T(8,128)(2,1)S(1)}, u32[]{:S(2)}, u32[]{:S(2)}) collective-permute-start(bf16[288,256]{1,0:T(8,128)(2,1)} %get-tuple-element.42), channel_id=1, source_target_pairs={{0,112},{4,116},{8,120},{12,124},{16,0},{20,4},{24,8},{28,12},{32,... | collective-permute-start | bytes 442376 | tf_op jit(solution)/shard_map/ppermute | solution.py:277
  69.7 1.0 front.1
  70.7 1.0 constant_dynamic-update-slice_fusion.8
  71.7 0.3 collective-permute-done.3
  72.1 1.0 constant_dynamic-update-slice_fusion.7
  73.1 2.0 %collective-permute-done.4 = bf16[576,256]{1,0:T(8,128)(2,1)} collective-permute-done((bf16[576,256]{1,0:T(8,128)(2,1)}, bf16[576,256]{1,0:T(8,128)(2,1)}, u32[]{:S(2)}, u32[]{:S(2)}) %collective-permute-start.4) | collective-permute-done | bytes 294944 | tf_op jit(solution)/shard_map/ppermute | solution.py:277
  75.1 1.0 constant_dynamic-update-slice_fusion.6
  76.1 6.4 %collective-permute-done.5 = bf16[288,256]{1,0:T(8,128)(2,1)} collective-permute-done((bf16[288,256]{1,0:T(8,128)(2,1)}, bf16[288,256]{1,0:T(8,128)(2,1)}, u32[]{:S(2)}, u32[]{:S(2)}) %collective-permute-start.5) | collective-permute-done | bytes 147488 | tf_op jit(solution)/shard_map/ppermute | solution.py:277
  82.5 0.9 constant_dynamic-update-slice_fusion.5
  83.4 1.9 %collective-permute-start.7 = (bf16[2304,256]{1,0:T(8,128)(2,1)S(1)}, bf16[2304,256]{1,0:T(8,128)(2,1)S(1)}, u32[]{:S(2)}, u32[]{:S(2)}) collective-permute-start(bf16[2304,256]{1,0:T(8,128)(2,1)S(1)} %constant_dynamic-update-slice_fusion.4.own), channel_id=1, source_target_pairs={{0,4},{4,0},{8,12},{12,8},{16,20},{20,16},{24,28},{28,24},{32,36},... | collective-permute-start | bytes 3538952 | tf_op jit(solution)/shard_map/ppermute | solution.py:281
  85.4 2.8 %collective-permute-done.7.sib = bf16[2304,256]{1,0:T(8,128)(2,1)S(1)} collective-permute-done((bf16[2304,256]{1,0:T(8,128)(2,1)S(1)}, bf16[2304,256]{1,0:T(8,128)(2,1)S(1)}, u32[]{:S(2)}, u32[]{:S(2)}) %collective-permute-start.7) | collective-permute-done | bytes 1179680 | tf_op jit(solution)/shard_map/ppermute | solution.py:281
  88.2 1.2 project.1
  89.3 2.8 %collective-permute-start.8 = (bf16[128,256]{1,0:T(8,128)(2,1)S(1)}, bf16[128,256]{1,0:T(8,128)(2,1)S(1)}, u32[]{:S(2)}, u32[]{:S(2)}) collective-permute-start(bf16[128,256]{1,0:T(8,128)(2,1)S(1)} %get-tuple-element.28), channel_id=1, source_target_pairs={{0,32},{4,36},{8,40},{12,44},{16,48},{20,52},{24,56},{28,60},{32,6... | collective-permute-start | bytes 196616 | tf_op jit(solution)/shard_map/ppermute | solution.py:277
  92.2 8.4 %collective-permute-start.9 = (bf16[128,256]{1,0:T(8,128)(2,1)S(1)}, bf16[128,256]{1,0:T(8,128)(2,1)S(1)}, u32[]{:S(2)}, u32[]{:S(2)}) collective-permute-start(bf16[128,256]{1,0:T(8,128)(2,1)S(1)} %get-tuple-element.28), channel_id=1, source_target_pairs={{0,64},{4,68},{8,72},{12,76},{16,80},{20,84},{24,88},{28,92},{32,9... | collective-permute-start | bytes 196616 | tf_op jit(solution)/shard_map/ppermute | solution.py:277
  100.6 2.0 %collective-permute-done.8 = bf16[128,256]{1,0:T(8,128)(2,1)S(1)} collective-permute-done((bf16[128,256]{1,0:T(8,128)(2,1)S(1)}, bf16[128,256]{1,0:T(8,128)(2,1)S(1)}, u32[]{:S(2)}, u32[]{:S(2)}) %collective-permute-start.8) | collective-permute-done | bytes 65568 | tf_op jit(solution)/shard_map/ppermute | solution.py:277
  102.7 3.2 %collective-permute-start.10 = (bf16[256,256]{1,0:T(8,128)(2,1)S(1)}, bf16[256,256]{1,0:T(8,128)(2,1)S(1)}, u32[]{:S(2)}, u32[]{:S(2)}) collective-permute-start(bf16[256,256]{1,0:T(8,128)(2,1)S(1)} %get-tuple-element.44), channel_id=1, source_target_pairs={{0,8},{4,12},{8,16},{12,20},{16,24},{20,28},{24,32},{28,36},{32,40... | collective-permute-start | bytes 393224 | tf_op jit(solution)/shard_map/ppermute | solution.py:277
  105.9 3.5 %collective-permute-start.11 = (bf16[256,256]{1,0:T(8,128)(2,1)S(1)}, bf16[256,256]{1,0:T(8,128)(2,1)S(1)}, u32[]{:S(2)}, u32[]{:S(2)}) collective-permute-start(bf16[256,256]{1,0:T(8,128)(2,1)S(1)} %get-tuple-element.44), channel_id=1, source_target_pairs={{0,16},{4,20},{8,24},{12,28},{16,32},{20,36},{24,40},{28,44},{32,4... | collective-permute-start | bytes 393224 | tf_op jit(solution)/shard_map/ppermute | solution.py:277
  109.3 2.5 %collective-permute-done.9 = bf16[128,256]{1,0:T(8,128)(2,1)S(1)} collective-permute-done((bf16[128,256]{1,0:T(8,128)(2,1)S(1)}, bf16[128,256]{1,0:T(8,128)(2,1)S(1)}, u32[]{:S(2)}, u32[]{:S(2)}) %collective-permute-start.9) | collective-permute-done | bytes 65568 | tf_op jit(solution)/shard_map/ppermute | solution.py:277
  111.9 2.6 %collective-permute-start.12 = (bf16[256,256]{1,0:T(8,128)(2,1)S(1)}, bf16[256,256]{1,0:T(8,128)(2,1)S(1)}, u32[]{:S(2)}, u32[]{:S(2)}) collective-permute-start(bf16[256,256]{1,0:T(8,128)(2,1)S(1)} %pad_maximum_fusion.1), channel_id=1, source_target_pairs={{0,120},{4,124},{8,0},{12,4},{16,8},{20,12},{24,16},{28,20},{32,24... | collective-permute-start | bytes 393224 | tf_op jit(solution)/shard_map/ppermute | solution.py:277
  114.5 0.9 collective-permute-done.10
  115.4 5.9 %collective-permute-done.11 = bf16[256,256]{1,0:T(8,128)(2,1)S(1)} collective-permute-done((bf16[256,256]{1,0:T(8,128)(2,1)S(1)}, bf16[256,256]{1,0:T(8,128)(2,1)S(1)}, u32[]{:S(2)}, u32[]{:S(2)}) %collective-permute-start.11) | collective-permute-done | bytes 131104 | tf_op jit(solution)/shard_map/ppermute | solution.py:277
  121.4 1.9 %collective-permute-start.13 = (bf16[1152,256]{1,0:T(8,128)(2,1)S(1)}, bf16[1152,256]{1,0:T(8,128)(2,1)S(1)}, u32[]{:S(2)}, u32[]{:S(2)}) collective-permute-start(bf16[1152,256]{1,0:T(8,128)(2,1)S(1)} %constant_dynamic-update-slice_fusion.11.own), channel_id=1, source_target_pairs={{0,4},{4,0},{8,12},{12,8},{16,20},{20,16},{24,28},{28,24},{32,36},... | collective-permute-start | bytes 1769480 | tf_op jit(solution)/shard_map/ppermute | solution.py:281
  123.3 0.0 all-gather.3.cloned.1.call-done
  123.4 4.9 %query.1.refs_2_ = bf16[128,1024]{1,0:T(8,128)(2,1)S(1)} custom-call(s32[5]{0:T(128)S(1)} %stack.22.scal.refs_0_, bf16[128,4096]{1,0:T(8,128)(2,1)S(1)} %get-tuple-element.25.xn, bf16[4096,1024]{1,0:T(8,128)(2,1)} %bitcast.35), custom_call_target="tpu_custom_call" | custom-call | flops 5750000128 | bytes 1048576 | tf_op jit(solution)/shard_map/query/pallas_call | solution.py:354
  128.3 0.0 collective-permute-done.13.sib
  128.3 0.0 copy-start
  128.3 0.8 assemble.1
  129.2 0.1 copy-done
  129.3 3.8 %finish_low.1 = bf16[128,768]{1,0:T(8,128)(2,1)S(1)} custom-call(s32[5]{0:T(128)S(1)} %stack.22.scal.refs_0_, bf16[128,1024]{1,0:T(8,128)(2,1)S(1)} %bitcast.27, bf16[128,1024]{1,0:T(8,128)(2,1)S(1)} %query.1.refs_2_, bf16[2304,128]{1,0:T(8,128)(2,1)S(1)} %get-tuple-element.33.refs_3_, bf16[2304,128]{1,0:T(8,128)(2,1)S(1)} %get-tuple-element.34.refs_4_, ...), custom_call_target="tpu_custom_call" | custom-call | flops 4600000000 | bytes 1048576 | tf_op jit(solution)/shard_map/finish_low/pallas_call | solution.py:388
  133.1 3.1 %collective-permute-start.14 = (bf16[128,768]{1,0:T(8,128)(2,1)S(1)}, bf16[128,768]{1,0:T(8,128)(2,1)S(1)}, u32[]{:S(2)}, u32[]{:S(2)}) collective-permute-start(bf16[128,768]{1,0:T(8,128)(2,1)S(1)} %finish_low.1), channel_id=1, source_target_pairs={{0,128},{128,256},{256,384},{1,129},{129,257},{257,385},{2,130},{1... | collective-permute-start | bytes 589832 | tf_op jit(solution)/shard_map/ppermute | solution.py:393
  136.2 1.9 %finish_high.1 = bf16[128,256]{1,0:T(8,128)(2,1)S(1)} custom-call(s32[5]{0:T(128)S(1)} %stack.22.scal.refs_0_, bf16[128,1024]{1,0:T(8,128)(2,1)S(1)} %bitcast.28, bf16[128,1024]{1,0:T(8,128)(2,1)S(1)} %query.1.refs_2_, bf16[2304,128]{1,0:T(8,128)(2,1)S(1)} %get-tuple-element.33.refs_3_, bf16[2304,128]{1,0:T(8,128)(2,1)S(1)} %get-tuple-element.34.refs_4_, ...), custom_call_target="tpu_custom_call" | custom-call | flops 2300000000 | bytes 1048576 | tf_op jit(solution)/shard_map/finish_high/pallas_call | solution.py:388
  138.2 1.9 %collective-permute-start.15 = (bf16[128,256]{1,0:T(8,128)(2,1)S(1)}, bf16[128,256]{1,0:T(8,128)(2,1)S(1)}, u32[]{:S(2)}, u32[]{:S(2)}) collective-permute-start(bf16[128,256]{1,0:T(8,128)(2,1)S(1)} %finish_high.1), channel_id=1, source_target_pairs={{0,128},{128,256},{256,384},{1,129},{129,257},{257,385},{2,130},{1... | collective-permute-start | bytes 196616 | tf_op jit(solution)/shard_map/ppermute | solution.py:393
  140.1 0.7 maximum_bitcast_fusion
  140.8 3.5 %collective-permute-done.15 = bf16[128,256]{1,0:T(8,128)(2,1)S(1)} collective-permute-done((bf16[128,256]{1,0:T(8,128)(2,1)S(1)}, bf16[128,256]{1,0:T(8,128)(2,1)S(1)}, u32[]{:S(2)}, u32[]{:S(2)}) %collective-permute-start.15) | collective-permute-done | bytes 65568 | tf_op jit(solution)/shard_map/ppermute | solution.py:393
  144.3 0.0 collective-permute-done.14
  144.3 0.7 maximum_bitcast_fusion.1
  (28 shorter events, 0.2 us)
Async XLA Ops:
  7.2 29.7 %copy-start.7 = (bf16[1,1024,32]{1,2,0:T(8,128)(2,1)S(1)}, bf16[1,1024,32]{1,2,0:T(8,128)(2,1)}, u32[]{:S(2)}) copy-start(bf16[1,1024,32]{1,2,0:T(8,128)(2,1)} %param.19) | copy-start | bytes 196612
  7.2 29.7 %copy-start.4 = (bf16[1,1024,64]{1,2,0:T(8,128)(2,1)S(1)}, bf16[1,1024,64]{1,2,0:T(8,128)(2,1)}, u32[]{:S(2)}) copy-start(bf16[1,1024,64]{1,2,0:T(8,128)(2,1)} %param.20) | copy-start | bytes 393220
  7.2 116.2 %all-gather.3.cloned.1.call-start = ((), (), s32[]{:S(2)}) async-start(), calls=%async_computation.1 | async-start | bytes 8650752 | tf_op jit(solution)/shard_map/all_gather | solution.py:305
  9.4 28.8 %collective-permute-start = (bf16[144,256]{1,0:T(8,128)(2,1)S(1)}, bf16[144,256]{1,0:T(8,128)(2,1)S(1)}, u32[]{:S(2)}, u32[]{:S(2)}) collective-permute-start(bf16[144,256]{1,0:T(8,128)(2,1)S(1)} %pad_maximum_fusion.2), channel_id=1, source_target_pairs={{0,32},{4,36},{8,40},{12,44},{16,48},{20,52},{24,56},{28,60},{32,6... | collective-permute-start | bytes 221192 | tf_op jit(solution)/shard_map/ppermute | solution.py:277
  18.5 21.6 %collective-permute-start.1 = (bf16[144,256]{1,0:T(8,128)(2,1)S(1)}, bf16[144,256]{1,0:T(8,128)(2,1)S(1)}, u32[]{:S(2)}, u32[]{:S(2)}) collective-permute-start(bf16[144,256]{1,0:T(8,128)(2,1)S(1)} %pad_maximum_fusion.2), channel_id=1, source_target_pairs={{0,96},{4,100},{8,104},{12,108},{16,112},{20,116},{24,120},{28,124... | collective-permute-start | bytes 221192 | tf_op jit(solution)/shard_map/ppermute | solution.py:277
  24.0 16.7 %collective-permute-start.2 = (bf16[144,256]{1,0:T(8,128)(2,1)S(1)}, bf16[144,256]{1,0:T(8,128)(2,1)S(1)}, u32[]{:S(2)}, u32[]{:S(2)}) collective-permute-start(bf16[144,256]{1,0:T(8,128)(2,1)S(1)} %pad_maximum_fusion.2), channel_id=1, source_target_pairs={{0,64},{4,68},{8,72},{12,76},{16,80},{20,84},{24,88},{28,92},{32,9... | collective-permute-start | bytes 221192 | tf_op jit(solution)/shard_map/ppermute | solution.py:277
  36.9 2.0 %copy-start.5 = (bf16[1,128,128]{2,1,0:T(8,128)(2,1)S(1)}, bf16[1,128,128]{2,1,0:T(8,128)(2,1)}, u32[]{:S(2)}) copy-start(bf16[1,128,128]{2,1,0:T(8,128)(2,1)} %param.18) | copy-start | bytes 98308
  36.9 1.9 %copy-start.6 = (bf16[1,128,128]{2,1,0:T(8,128)(2,1)S(1)}, bf16[1,128,128]{2,1,0:T(8,128)(2,1)}, u32[]{:S(2)}) copy-start(bf16[1,128,128]{2,1,0:T(8,128)(2,1)} %param.17) | copy-start | bytes 98308
  41.3 28.3 %copy-start.1 = (f32[1,16]{1,0:T(1,128)S(1)}, f32[1,16]{1,0:T(1,128)}, u32[]{:S(2)}) copy-start(f32[1,16]{1,0:T(1,128)} %bias.1) | copy-start | bytes 196
  41.3 28.3 %copy-start.2 = (f32[1,16]{1,0:T(1,128)S(1)}, f32[1,16]{1,0:T(1,128)}, u32[]{:S(2)}) copy-start(f32[1,16]{1,0:T(1,128)} %rate.1) | copy-start | bytes 196
  41.3 28.3 %copy-start.3 = (f32[1,16]{1,0:T(1,128)S(1)}, f32[1,16]{1,0:T(1,128)}, u32[]{:S(2)}) copy-start(f32[1,16]{1,0:T(1,128)} %skip.1) | copy-start | bytes 196
  41.3 28.3 %all-to-all-start = ((bf16[4,192,1024]{2,1,0:T(8,128)(2,1)}), bf16[4,192,1024]{2,1,0:T(8,128)(2,1)S(1)}, u32[]{:S(2)}, u32[]{:S(2)}) async-start(bf16[4,192,1024]{2,1,0:T(8,128)(2,1)} %pad_maximum_fusion), calls=%async_computation | async-start | bytes 3145728 | tf_op jit(solution)/shard_map/all_to_all | solution.py:327
  47.1 25.0 %collective-permute-start.3 = (bf16[576,256]{1,0:T(8,128)(2,1)}, bf16[576,256]{1,0:T(8,128)(2,1)}, u32[]{:S(2)}, u32[]{:S(2)}) collective-permute-start(bf16[576,256]{1,0:T(8,128)(2,1)} %constant_dynamic-update-slice_fusion), channel_id=1, source_target_pairs={{0,8},{4,12},{8,16},{12,20},{16,24},{20,28},{24,32},{28,36},{32,40... | collective-permute-start | bytes 884744 | tf_op jit(solution)/shard_map/ppermute | solution.py:277
  55.6 19.5 %collective-permute-start.4 = (bf16[576,256]{1,0:T(8,128)(2,1)}, bf16[576,256]{1,0:T(8,128)(2,1)}, u32[]{:S(2)}, u32[]{:S(2)}) collective-permute-start(bf16[576,256]{1,0:T(8,128)(2,1)} %constant_dynamic-update-slice_fusion), channel_id=1, source_target_pairs={{0,120},{4,124},{8,0},{12,4},{16,8},{20,12},{24,16},{28,20},{32,24... | collective-permute-start | bytes 884744 | tf_op jit(solution)/shard_map/ppermute | solution.py:277
  61.7 20.8 %collective-permute-start.5 = (bf16[288,256]{1,0:T(8,128)(2,1)}, bf16[288,256]{1,0:T(8,128)(2,1)}, u32[]{:S(2)}, u32[]{:S(2)}) collective-permute-start(bf16[288,256]{1,0:T(8,128)(2,1)} %get-tuple-element.43), channel_id=1, source_target_pairs={{0,16},{4,20},{8,24},{12,28},{16,32},{20,36},{24,40},{28,44},{32,4... | collective-permute-start | bytes 442376 | tf_op jit(solution)/shard_map/ppermute | solution.py:277
  63.6 19.8 %collective-permute-start.6 = (bf16[288,256]{1,0:T(8,128)(2,1)}, bf16[288,256]{1,0:T(8,128)(2,1)S(1)}, u32[]{:S(2)}, u32[]{:S(2)}) collective-permute-start(bf16[288,256]{1,0:T(8,128)(2,1)} %get-tuple-element.42), channel_id=1, source_target_pairs={{0,112},{4,116},{8,120},{12,124},{16,0},{20,4},{24,8},{28,12},{32,... | collective-permute-start | bytes 442376 | tf_op jit(solution)/shard_map/ppermute | solution.py:277
  83.4 4.7 %collective-permute-start.7 = (bf16[2304,256]{1,0:T(8,128)(2,1)S(1)}, bf16[2304,256]{1,0:T(8,128)(2,1)S(1)}, u32[]{:S(2)}, u32[]{:S(2)}) collective-permute-start(bf16[2304,256]{1,0:T(8,128)(2,1)S(1)} %constant_dynamic-update-slice_fusion.4.own), channel_id=1, source_target_pairs={{0,4},{4,0},{8,12},{12,8},{16,20},{20,16},{24,28},{28,24},{32,36},... | collective-permute-start | bytes 3538952 | tf_op jit(solution)/shard_map/ppermute | solution.py:281
  89.3 13.3 %collective-permute-start.8 = (bf16[128,256]{1,0:T(8,128)(2,1)S(1)}, bf16[128,256]{1,0:T(8,128)(2,1)S(1)}, u32[]{:S(2)}, u32[]{:S(2)}) collective-permute-start(bf16[128,256]{1,0:T(8,128)(2,1)S(1)} %get-tuple-element.28), channel_id=1, source_target_pairs={{0,32},{4,36},{8,40},{12,44},{16,48},{20,52},{24,56},{28,60},{32,6... | collective-permute-start | bytes 196616 | tf_op jit(solution)/shard_map/ppermute | solution.py:277
  92.2 19.7 %collective-permute-start.9 = (bf16[128,256]{1,0:T(8,128)(2,1)S(1)}, bf16[128,256]{1,0:T(8,128)(2,1)S(1)}, u32[]{:S(2)}, u32[]{:S(2)}) collective-permute-start(bf16[128,256]{1,0:T(8,128)(2,1)S(1)} %get-tuple-element.28), channel_id=1, source_target_pairs={{0,64},{4,68},{8,72},{12,76},{16,80},{20,84},{24,88},{28,92},{32,9... | collective-permute-start | bytes 196616 | tf_op jit(solution)/shard_map/ppermute | solution.py:277
  102.7 12.7 %collective-permute-start.10 = (bf16[256,256]{1,0:T(8,128)(2,1)S(1)}, bf16[256,256]{1,0:T(8,128)(2,1)S(1)}, u32[]{:S(2)}, u32[]{:S(2)}) collective-permute-start(bf16[256,256]{1,0:T(8,128)(2,1)S(1)} %get-tuple-element.44), channel_id=1, source_target_pairs={{0,8},{4,12},{8,16},{12,20},{16,24},{20,28},{24,32},{28,36},{32,40... | collective-permute-start | bytes 393224 | tf_op jit(solution)/shard_map/ppermute | solution.py:277
  105.9 15.5 %collective-permute-start.11 = (bf16[256,256]{1,0:T(8,128)(2,1)S(1)}, bf16[256,256]{1,0:T(8,128)(2,1)S(1)}, u32[]{:S(2)}, u32[]{:S(2)}) collective-permute-start(bf16[256,256]{1,0:T(8,128)(2,1)S(1)} %get-tuple-element.44), channel_id=1, source_target_pairs={{0,16},{4,20},{8,24},{12,28},{16,32},{20,36},{24,40},{28,44},{32,4... | collective-permute-start | bytes 393224 | tf_op jit(solution)/shard_map/ppermute | solution.py:277
  111.9 9.5 %collective-permute-start.12 = (bf16[256,256]{1,0:T(8,128)(2,1)S(1)}, bf16[256,256]{1,0:T(8,128)(2,1)S(1)}, u32[]{:S(2)}, u32[]{:S(2)}) collective-permute-start(bf16[256,256]{1,0:T(8,128)(2,1)S(1)} %pad_maximum_fusion.1), channel_id=1, source_target_pairs={{0,120},{4,124},{8,0},{12,4},{16,8},{20,12},{24,16},{28,20},{32,24... | collective-permute-start | bytes 393224 | tf_op jit(solution)/shard_map/ppermute | solution.py:277
  121.4 6.9 %collective-permute-start.13 = (bf16[1152,256]{1,0:T(8,128)(2,1)S(1)}, bf16[1152,256]{1,0:T(8,128)(2,1)S(1)}, u32[]{:S(2)}, u32[]{:S(2)}) collective-permute-start(bf16[1152,256]{1,0:T(8,128)(2,1)S(1)} %constant_dynamic-update-slice_fusion.11.own), channel_id=1, source_target_pairs={{0,4},{4,0},{8,12},{12,8},{16,20},{20,16},{24,28},{28,24},{32,36},... | collective-permute-start | bytes 1769480 | tf_op jit(solution)/shard_map/ppermute | solution.py:281
  128.3 1.0 copy-start
  133.1 11.2 %collective-permute-start.14 = (bf16[128,768]{1,0:T(8,128)(2,1)S(1)}, bf16[128,768]{1,0:T(8,128)(2,1)S(1)}, u32[]{:S(2)}, u32[]{:S(2)}) collective-permute-start(bf16[128,768]{1,0:T(8,128)(2,1)S(1)} %finish_low.1), channel_id=1, source_target_pairs={{0,128},{128,256},{256,384},{1,129},{129,257},{257,385},{2,130},{1... | collective-permute-start | bytes 589832 | tf_op jit(solution)/shard_map/ppermute | solution.py:393
  138.2 6.2 %collective-permute-start.15 = (bf16[128,256]{1,0:T(8,128)(2,1)S(1)}, bf16[128,256]{1,0:T(8,128)(2,1)S(1)}, u32[]{:S(2)}, u32[]{:S(2)}) collective-permute-start(bf16[128,256]{1,0:T(8,128)(2,1)S(1)} %finish_high.1), channel_id=1, source_target_pairs={{0,128},{128,256},{256,384},{1,129},{129,257},{257,385},{2,130},{1... | collective-permute-start | bytes 196616 | tf_op jit(solution)/shard_map/ppermute | solution.py:393
Sparse Core Ops, SparseCore 0:
  10.1 107.6 all-gather.2

commit v5 on v4

--- a/solution.py
+++ b/solution.py
@@ -19,8 +19,8 @@
 EXACT = lax.Precision.HIGHEST
 
 W_FIRST = (-4, 0, 4, -8)
-W_REL = tuple(a + b for b in (0, -1, 1) for a in W_FIRST) + (-6, -2, 2, 6)
-KV_AT = (0, 3, 5, 7, 1, 4, 6, 8, 2)
+W_REL = W_FIRST + (-6, -2, 2, 6) + tuple(a + b for b in (-1, 1) for a in W_FIRST)
+KV_AT = (0, 5, 3, 7, 1, 6, 4, 8, 2)
 
 
 def iota(shape, dim):
@@ -323,7 +323,8 @@
     wkv = jnp.concatenate([wkv, jnp.pad(idr.astype(BF), ((0, 15), (0, 128)))], axis=0)
     a, b, c = [by_chips(wkv, k) for k in (4, -4, 8)]
     first = jnp.concatenate([a, wkv, b, c], axis=0)
-    parts, first = lax.optimization_barrier((parts, first))
+    halves = [jnp.concatenate([a, wkv], axis=0), jnp.concatenate([wkv, b], axis=0)]
+    parts, first, halves = lax.optimization_barrier((parts, first, halves))
     got = lax.all_to_all(parts, "tp", 0, 0)
     xn, states, yloc, aux = kernel(
         front,
@@ -334,10 +335,10 @@
     )(scal, got, idc, idr, dt_bias, decay_rate, skip_gain)
 
     others = [
+        by_chips(halves[0], 2),
+        by_chips(halves[1], -2),
         by_chips(first, 1),
         by_chips(first, -1),
-        by_chips(first[: 2 * WROWS], 2),
-        by_chips(first[WROWS : 3 * WROWS], -2),
     ]
     first, xn = lax.optimization_barrier((first, xn))
     weights = jnp.concatenate([first] + others, axis=0)
@@ -351,6 +352,12 @@
         [SMEM] + [VMEM] * 4,
         [pltpu.VMEM((D, 256), BF)],
     )(scal, xn, weights, sibling, states)
+
+    back4, back8 = by_chips(pay, 4), by_chips(pay, 8)
+    near = jnp.concatenate([pay, back4], axis=0)
+    far = jnp.concatenate([back4, back8], axis=0)
+    near2 = by_chips(near, 2)
+    xn, near2 = lax.optimization_barrier((xn, near2))
     q = kernel(
         query,
         5,
@@ -359,15 +366,11 @@
         [SMEM, VMEM, ANY],
         [pltpu.VMEM((4, D, 256), BF), pltpu.SemaphoreType.DMA((4,))],
     )(scal, xn, wq)
-
-    back4, back8 = by_chips(pay, 4), by_chips(pay, 8)
-    near = jnp.concatenate([pay, back4], axis=0)
-    far = jnp.concatenate([back4, back8], axis=0)
+    pay, q = lax.optimization_barrier((pay, q))
     own = jnp.concatenate(
-        [pay, back4, back8, by_chips(near, 1), by_chips(near, 2), by_chips(far, -1)], axis=0
+        [pay, back4, back8, near2, by_chips(near, 1), by_chips(far, -1)], axis=0
     )
     sib = swap(own)
-    sib, q = lax.optimization_barrier((sib, q))
 
     gathered = kernel(
         assemble,

time: 153 us -> 154 us (level)
  starting transfers between devices: 80.6 us -> 88.8 us
  Pallas kernels: 13.7 us -> 8.51 us
  waiting for transfers between devices: 27.2 us -> 25.4 us
    ppermute x2, starting transfers between devices: 5.04 us -> 11.7 us  [shards(): moved.append(lax.ppermute(part, 'pipe', [(i, i + 1) for i in range(3)]))]
    ppermute x12, waiting for transfers between devices: 20.1 us -> 14 us  [by_chips(): lax.ppermute(x, 'ctx', [(i, (i + 2 * k) % (2 * CHIPS)) for i in range(2 *...]
    pallas_call x1, Pallas kernels: 4.94 us -> 0.58 us  [shards(): kernel(query, 5, 52, shape(ROWS, COLS), [SMEM, VMEM, ANY], [pltpu.VMEM((4...]
    pallas_call x2, Pallas kernels: 5.75 us -> 2.43 us  [shards(): kernel(body, us, 20, shape(ROWS, cols), [SMEM] + [VMEM] * 9)]
    pallas_call x1, Pallas kernels: 1.05 us -> 4.03 us  [shards(): kernel(front, 4, 20, (shape(ROWS, D), shape(ROWS, 256), shape(ROWS, COLS,...]
    all_gather x1, waiting for transfers between devices: 0.02 us -> 2.57 us  [shards(): wq = lax.all_gather(q_weight[0], 'ctx', axis=0, tiled=True)]
    ppermute x2, waiting for transfers between devices: 2.82 us -> 4.84 us  [swap(): return lax.ppermute(x, 'ctx', [(i, i ^ 1) for i in range(2 * CHIPS)])]
    slice x1 -> x0, local copies, waits for them, and re-layouts: 1.72 us -> none  [shards(): first[WROWS:3 * WROWS]]
  transfers between devices with their start and end apart: 18 -> 18, of which waited for: 9 -> 9; matrix products, arithmetic and copies ran while one was open for 10% -> 9% of each run, Pallas kernels for 6% -> 4%
where the time goes in v5:
time: 154 us; the launch traced here: 153 us
  starting transfers between devices  88.8 us (58%)
  waiting for transfers between devices  25.4 us (16%)
  between operations  15.1 us (10%)
  local copies, waits for them, and re-layouts  8.72 us (6%)
  Pallas kernels  8.51 us (6%)
  other arithmetic  6.35 us (4%)
    ppermute x12, starting transfers between devices, by_chips(): lax.ppermute(x, 'ctx', [(i, (i + 2 * k) % (2 * CHIPS)) for i in range(2 *...  68.3 us
    ppermute x12, waiting for transfers between devices, by_chips(): lax.ppermute(x, 'ctx', [(i, (i + 2 * k) % (2 * CHIPS)) for i in range(2 *...  14 us
    ppermute x2, starting transfers between devices, shards(): moved.append(lax.ppermute(part, 'pipe', [(i, i + 1) for i in range(3)]))  11.7 us
    all_to_all x1, starting transfers between devices, shards(): got = lax.all_to_all(parts, 'tp', 0, 0)  4.94 us
    unnamed x27, local copies, waits for them, and re-layouts  4.87 us
    ppermute x2, waiting for transfers between devices, swap(): return lax.ppermute(x, 'ctx', [(i, i ^ 1) for i in range(2 * CHIPS)])  4.84 us
    pallas_call x1, Pallas kernels, shards(): kernel(front, 4, 20, (shape(ROWS, D), shape(ROWS, 256), shape(ROWS, COLS,...  4.03 us
    ppermute x2, starting transfers between devices, swap(): return lax.ppermute(x, 'ctx', [(i, i ^ 1) for i in range(2 * CHIPS)])  3.87 us
  transfers between devices with their start and end apart: 18, of which 9 were waited for; matrix products, arithmetic and copies ran while one was open for 9% of the time, Pallas kernels for 4%

profile of v5, /device:TPU:20, one launch (start us, length us, event | category | flops | bytes accessed | tf_op | source)
XLA Modules:
  0.0 152.8 jit_solution(4023641421255623564)
XLA Ops:
  7.2 0.0 all-gather.3.cloned.1.call-start
  7.2 0.7 all-gather.3.cloned.1.call-update
  7.9 0.7 convert_bitcast_fusion.1
  8.6 0.8 pad_maximum_fusion.4
  9.4 9.1 %collective-permute-start = (bf16[144,256]{1,0:T(8,128)(2,1)S(1)}, bf16[144,256]{1,0:T(8,128)(2,1)S(1)}, u32[]{:S(2)}, u32[]{:S(2)}) collective-permute-start(bf16[144,256]{1,0:T(8,128)(2,1)S(1)} %pad_maximum_fusion.4), channel_id=1, source_target_pairs={{0,32},{4,36},{8,40},{12,44},{16,48},{20,52},{24,56},{28,60},{32,6... | collective-permute-start | bytes 221192 | tf_op jit(solution)/shard_map/ppermute | solution.py:277
  18.5 5.6 %collective-permute-start.1 = (bf16[144,256]{1,0:T(8,128)(2,1)S(1)}, bf16[144,256]{1,0:T(8,128)(2,1)S(1)}, u32[]{:S(2)}, u32[]{:S(2)}) collective-permute-start(bf16[144,256]{1,0:T(8,128)(2,1)S(1)} %pad_maximum_fusion.4), channel_id=1, source_target_pairs={{0,96},{4,100},{8,104},{12,108},{16,112},{20,116},{24,120},{28,124... | collective-permute-start | bytes 221192 | tf_op jit(solution)/shard_map/ppermute | solution.py:277
  24.0 10.8 %collective-permute-start.2 = (bf16[144,256]{1,0:T(8,128)(2,1)S(1)}, bf16[144,256]{1,0:T(8,128)(2,1)S(1)}, u32[]{:S(2)}, u32[]{:S(2)}) collective-permute-start(bf16[144,256]{1,0:T(8,128)(2,1)S(1)} %pad_maximum_fusion.4), channel_id=1, source_target_pairs={{0,64},{4,68},{8,72},{12,76},{16,80},{20,84},{24,88},{28,92},{32,9... | collective-permute-start | bytes 221192 | tf_op jit(solution)/shard_map/ppermute | solution.py:277
  34.9 0.1 pad.31.clone
  34.9 0.7 reduce-precision_convert_fusion.1
  35.6 0.1 maximum_maximum_fusion
  35.7 0.9 broadcast_in_dim.33
  36.6 1.1 broadcast_in_dim.32
  37.7 0.0 copy-start.4
  37.7 0.0 copy-start.5
  37.7 1.3 pad_maximum_fusion
  39.0 0.0 collective-permute-done
  39.0 0.6 constant_dynamic-update-slice_fusion.3
  39.7 0.6 maximum_dynamic-update-slice_fusion
  40.3 0.6 constant_dynamic-update-slice_fusion.2
  40.9 0.0 collective-permute-done.1
  40.9 0.6 constant_dynamic-update-slice_fusion.1
  41.5 0.0 collective-permute-done.2
  41.5 0.6 constant_dynamic-update-slice_fusion
  42.2 0.7 pad_maximum_fusion.2
  42.9 4.9 %all-to-all-start = ((bf16[4,192,1024]{2,1,0:T(8,128)(2,1)}), bf16[4,192,1024]{2,1,0:T(8,128)(2,1)S(1)}, u32[]{:S(2)}, u32[]{:S(2)}) async-start(bf16[4,192,1024]{2,1,0:T(8,128)(2,1)} %pad_maximum_fusion), calls=%async_computation | async-start | bytes 3145728 | tf_op jit(solution)/shard_map/all_to_all | solution.py:328
  48.5 0.1 copy.14.idc_ref
  48.6 0.1 stack.22.scal.refs_0_
  48.7 7.6 %collective-permute-start.5 = (bf16[576,256]{1,0:T(8,128)(2,1)}, bf16[576,256]{1,0:T(8,128)(2,1)}, u32[]{:S(2)}, u32[]{:S(2)}) collective-permute-start(bf16[576,256]{1,0:T(8,128)(2,1)} %constant_dynamic-update-slice_fusion), channel_id=1, source_target_pairs={{0,8},{4,12},{8,16},{12,20},{16,24},{20,28},{24,32},{28,36},{32,40... | collective-permute-start | bytes 884744 | tf_op jit(solution)/shard_map/ppermute | solution.py:277
  56.3 4.4 %collective-permute-start.6 = (bf16[576,256]{1,0:T(8,128)(2,1)}, bf16[576,256]{1,0:T(8,128)(2,1)}, u32[]{:S(2)}, u32[]{:S(2)}) collective-permute-start(bf16[576,256]{1,0:T(8,128)(2,1)} %constant_dynamic-update-slice_fusion), channel_id=1, source_target_pairs={{0,120},{4,124},{8,0},{12,4},{16,8},{20,12},{24,16},{28,20},{32,24... | collective-permute-start | bytes 884744 | tf_op jit(solution)/shard_map/ppermute | solution.py:277
  60.7 1.9 %collective-permute-start.3 = (bf16[288,256]{1,0:T(8,128)(2,1)}, bf16[288,256]{1,0:T(8,128)(2,1)}, u32[]{:S(2)}, u32[]{:S(2)}) collective-permute-start(bf16[288,256]{1,0:T(8,128)(2,1)} %get-tuple-element.31), channel_id=1, source_target_pairs={{0,16},{4,20},{8,24},{12,28},{16,32},{20,36},{24,40},{28,44},{32,4... | collective-permute-start | bytes 442376 | tf_op jit(solution)/shard_map/ppermute | solution.py:277
  62.6 6.0 %collective-permute-start.4 = (bf16[288,256]{1,0:T(8,128)(2,1)}, bf16[288,256]{1,0:T(8,128)(2,1)S(1)}, u32[]{:S(2)}, u32[]{:S(2)}) collective-permute-start(bf16[288,256]{1,0:T(8,128)(2,1)} %get-tuple-element.32), channel_id=1, source_target_pairs={{0,112},{4,116},{8,120},{12,124},{16,0},{20,4},{24,8},{28,12},{32,... | collective-permute-start | bytes 442376 | tf_op jit(solution)/shard_map/ppermute | solution.py:277
  68.7 4.0 %front.1 = (bf16[128,4096]{1,0:T(8,128)(2,1)S(1)}, bf16[128,256]{1,0:T(8,128)(2,1)S(1)}, f32[128,1024]{1,0:T(8,128)S(1)}, f32[128,128]{1,0:T(8,128)S(1)}) custom-call(s32[5]{0:T(128)S(1)} %stack.22.scal.refs_0_, bf16[4,192,1024]{2,1,0:T(8,128)(2,1)S(1)} %all-to-all-done.got, f32[128,1]{1,0:T(8,128)S(1)} %copy.14.idc_ref, ...), custom_call_target="tpu_custom_call" | custom-call | flops 4600000000 | bytes 1048576 | tf_op jit(solution)/shard_map/front/pallas_call | solution.py:329
  72.7 1.0 constant_dynamic-update-slice_fusion.8
  73.7 9.2 %collective-permute-done.3 = bf16[288,256]{1,0:T(8,128)(2,1)} collective-permute-done((bf16[288,256]{1,0:T(8,128)(2,1)}, bf16[288,256]{1,0:T(8,128)(2,1)}, u32[]{:S(2)}, u32[]{:S(2)}) %collective-permute-start.3) | collective-permute-done | bytes 147488 | tf_op jit(solution)/shard_map/ppermute | solution.py:277
  83.0 0.9 constant_dynamic-update-slice_fusion.7
  83.9 0.0 collective-permute-done.4
  83.9 1.0 constant_dynamic-update-slice_fusion.5
  84.9 1.0 constant_dynamic-update-slice_fusion.4.own
  85.9 1.9 %collective-permute-start.7 = (bf16[2304,256]{1,0:T(8,128)(2,1)S(1)}, bf16[2304,256]{1,0:T(8,128)(2,1)S(1)}, u32[]{:S(2)}, u32[]{:S(2)}) collective-permute-start(bf16[2304,256]{1,0:T(8,128)(2,1)S(1)} %constant_dynamic-update-slice_fusion.4.own), channel_id=1, source_target_pairs={{0,4},{4,0},{8,12},{12,8},{16,20},{20,16},{24,28},{28,24},{32,36},... | collective-permute-start | bytes 3538952 | tf_op jit(solution)/shard_map/ppermute | solution.py:281
  87.8 2.9 %collective-permute-done.7.sib = bf16[2304,256]{1,0:T(8,128)(2,1)S(1)} collective-permute-done((bf16[2304,256]{1,0:T(8,128)(2,1)S(1)}, bf16[2304,256]{1,0:T(8,128)(2,1)S(1)}, u32[]{:S(2)}, u32[]{:S(2)}) %collective-permute-start.7) | collective-permute-done | bytes 1179680 | tf_op jit(solution)/shard_map/ppermute | solution.py:281
  90.8 0.6 project.1
  91.3 3.0 %collective-permute-start.8 = (bf16[128,256]{1,0:T(8,128)(2,1)S(1)}, bf16[128,256]{1,0:T(8,128)(2,1)S(1)}, u32[]{:S(2)}, u32[]{:S(2)}) collective-permute-start(bf16[128,256]{1,0:T(8,128)(2,1)S(1)} %get-tuple-element.37), channel_id=1, source_target_pairs={{0,32},{4,36},{8,40},{12,44},{16,48},{20,52},{24,56},{28,60},{32,6... | collective-permute-start | bytes 196616 | tf_op jit(solution)/shard_map/ppermute | solution.py:277
  94.3 8.8 %collective-permute-start.10 = (bf16[128,256]{1,0:T(8,128)(2,1)S(1)}, bf16[128,256]{1,0:T(8,128)(2,1)S(1)}, u32[]{:S(2)}, u32[]{:S(2)}) collective-permute-start(bf16[128,256]{1,0:T(8,128)(2,1)S(1)} %get-tuple-element.37), channel_id=1, source_target_pairs={{0,64},{4,68},{8,72},{12,76},{16,80},{20,84},{24,88},{28,92},{32,9... | collective-permute-start | bytes 196616 | tf_op jit(solution)/shard_map/ppermute | solution.py:277
  103.1 1.3 collective-permute-done.8
  104.5 5.0 %collective-permute-start.9 = (bf16[256,256]{1,0:T(8,128)(2,1)S(1)}, bf16[256,256]{1,0:T(8,128)(2,1)S(1)}, u32[]{:S(2)}, u32[]{:S(2)}) collective-permute-start(bf16[256,256]{1,0:T(8,128)(2,1)S(1)} %constant_dynamic-update-slice_fusion.9), channel_id=1, source_target_pairs={{0,16},{4,20},{8,24},{12,28},{16,32},{20,36},{24,40},{28,44},{32,4... | collective-permute-start | bytes 393224 | tf_op jit(solution)/shard_map/ppermute | solution.py:277
  109.5 1.9 %collective-permute-start.11 = (bf16[256,256]{1,0:T(8,128)(2,1)S(1)}, bf16[256,256]{1,0:T(8,128)(2,1)S(1)}, u32[]{:S(2)}, u32[]{:S(2)}) collective-permute-start(bf16[256,256]{1,0:T(8,128)(2,1)S(1)} %constant_dynamic-update-slice_fusion.9), channel_id=1, source_target_pairs={{0,8},{4,12},{8,16},{12,20},{16,24},{20,28},{24,32},{28,36},{32,40... | collective-permute-start | bytes 393224 | tf_op jit(solution)/shard_map/ppermute | solution.py:277
  111.4 1.0 collective-permute-done.10
  112.4 4.2 %collective-permute-start.12 = (bf16[256,256]{1,0:T(8,128)(2,1)S(1)}, bf16[256,256]{1,0:T(8,128)(2,1)S(1)}, u32[]{:S(2)}, u32[]{:S(2)}) collective-permute-start(bf16[256,256]{1,0:T(8,128)(2,1)S(1)} %pad_maximum_fusion.3), channel_id=1, source_target_pairs={{0,120},{4,124},{8,0},{12,4},{16,8},{20,12},{24,16},{28,20},{32,24... | collective-permute-start | bytes 393224 | tf_op jit(solution)/shard_map/ppermute | solution.py:277
  116.6 1.6 %collective-permute-done.9 = bf16[256,256]{1,0:T(8,128)(2,1)S(1)} collective-permute-done((bf16[256,256]{1,0:T(8,128)(2,1)S(1)}, bf16[256,256]{1,0:T(8,128)(2,1)S(1)}, u32[]{:S(2)}, u32[]{:S(2)}) %collective-permute-start.9) | collective-permute-done | bytes 131104 | tf_op jit(solution)/shard_map/ppermute | solution.py:277
  118.2 2.6 %all-gather.3.cloned.1.call-done = bf16[1,4096,1024]{2,1,0:T(8,128)(2,1)} async-done(((bf16[1,128,1024]{2,1,0:T(8,128)(2,1)}), bf16[1,4096,1024]{2,1,0:T(8,128)(2,1)}) %all-gather.3.cloned.1.call-update) | async-done | bytes 8388624 | tf_op jit(solution)/shard_map/all_gather | solution.py:305
  120.8 0.6 query.1.refs_2_
  121.5 0.8 collective-permute-done.11
  122.3 2.0 %collective-permute-start.13 = (bf16[1152,256]{1,0:T(8,128)(2,1)S(1)}, bf16[1152,256]{1,0:T(8,128)(2,1)S(1)}, u32[]{:S(2)}, u32[]{:S(2)}) collective-permute-start(bf16[1152,256]{1,0:T(8,128)(2,1)S(1)} %constant_dynamic-update-slice_fusion.11.own), channel_id=1, source_target_pairs={{0,4},{4,0},{8,12},{12,8},{16,20},{20,16},{24,28},{28,24},{32,36},... | collective-permute-start | bytes 1769480 | tf_op jit(solution)/shard_map/ppermute | solution.py:281
  124.3 1.9 %collective-permute-done.13.sib = bf16[1152,256]{1,0:T(8,128)(2,1)S(1)} collective-permute-done((bf16[1152,256]{1,0:T(8,128)(2,1)S(1)}, bf16[1152,256]{1,0:T(8,128)(2,1)S(1)}, u32[]{:S(2)}, u32[]{:S(2)}) %collective-permute-start.13) | collective-permute-done | bytes 589856 | tf_op jit(solution)/shard_map/ppermute | solution.py:281
  126.2 0.9 assemble.1
  127.2 0.0 copy-done
  127.2 1.4 finish_low.1
  128.6 9.5 %collective-permute-start.14 = (bf16[128,768]{1,0:T(8,128)(2,1)S(1)}, bf16[128,768]{1,0:T(8,128)(2,1)S(1)}, u32[]{:S(2)}, u32[]{:S(2)}) collective-permute-start(bf16[128,768]{1,0:T(8,128)(2,1)S(1)} %finish_low.1), channel_id=1, source_target_pairs={{0,128},{128,256},{256,384},{1,129},{129,257},{257,385},{2,130},{1... | collective-permute-start | bytes 589832 | tf_op jit(solution)/shard_map/ppermute | solution.py:396
  138.1 1.0 finish_high.1
  139.1 2.2 %collective-permute-start.15 = (bf16[128,256]{1,0:T(8,128)(2,1)S(1)}, bf16[128,256]{1,0:T(8,128)(2,1)S(1)}, u32[]{:S(2)}, u32[]{:S(2)}) collective-permute-start(bf16[128,256]{1,0:T(8,128)(2,1)S(1)} %finish_high.1), channel_id=1, source_target_pairs={{0,128},{128,256},{256,384},{1,129},{129,257},{257,385},{2,130},{1... | collective-permute-start | bytes 196616 | tf_op jit(solution)/shard_map/ppermute | solution.py:396
  141.3 0.7 maximum_bitcast_fusion
  142.0 3.2 %collective-permute-done.15 = bf16[128,256]{1,0:T(8,128)(2,1)S(1)} collective-permute-done((bf16[128,256]{1,0:T(8,128)(2,1)S(1)}, bf16[128,256]{1,0:T(8,128)(2,1)S(1)}, u32[]{:S(2)}, u32[]{:S(2)}) %collective-permute-start.15) | collective-permute-done | bytes 65568 | tf_op jit(solution)/shard_map/ppermute | solution.py:396
  145.3 0.0 collective-permute-done.14
  145.3 0.7 maximum_bitcast_fusion.1
  (28 shorter events, 0.1 us)
Async XLA Ops:
  7.2 30.5 %copy-start.6 = (bf16[1,1024,64]{1,2,0:T(8,128)(2,1)S(1)}, bf16[1,1024,64]{1,2,0:T(8,128)(2,1)}, u32[]{:S(2)}) copy-start(bf16[1,1024,64]{1,2,0:T(8,128)(2,1)} %param.20) | copy-start | bytes 393220
  7.2 113.6 %all-gather.3.cloned.1.call-start = ((), (), s32[]{:S(2)}) async-start(), calls=%async_computation.1 | async-start | bytes 8650752 | tf_op jit(solution)/shard_map/all_gather | solution.py:305
  9.4 29.7 %collective-permute-start = (bf16[144,256]{1,0:T(8,128)(2,1)S(1)}, bf16[144,256]{1,0:T(8,128)(2,1)S(1)}, u32[]{:S(2)}, u32[]{:S(2)}) collective-permute-start(bf16[144,256]{1,0:T(8,128)(2,1)S(1)} %pad_maximum_fusion.4), channel_id=1, source_target_pairs={{0,32},{4,36},{8,40},{12,44},{16,48},{20,52},{24,56},{28,60},{32,6... | collective-permute-start | bytes 221192 | tf_op jit(solution)/shard_map/ppermute | solution.py:277
  18.5 22.4 %collective-permute-start.1 = (bf16[144,256]{1,0:T(8,128)(2,1)S(1)}, bf16[144,256]{1,0:T(8,128)(2,1)S(1)}, u32[]{:S(2)}, u32[]{:S(2)}) collective-permute-start(bf16[144,256]{1,0:T(8,128)(2,1)S(1)} %pad_maximum_fusion.4), channel_id=1, source_target_pairs={{0,96},{4,100},{8,104},{12,108},{16,112},{20,116},{24,120},{28,124... | collective-permute-start | bytes 221192 | tf_op jit(solution)/shard_map/ppermute | solution.py:277
  24.0 17.5 %collective-permute-start.2 = (bf16[144,256]{1,0:T(8,128)(2,1)S(1)}, bf16[144,256]{1,0:T(8,128)(2,1)S(1)}, u32[]{:S(2)}, u32[]{:S(2)}) collective-permute-start(bf16[144,256]{1,0:T(8,128)(2,1)S(1)} %pad_maximum_fusion.4), channel_id=1, source_target_pairs={{0,64},{4,68},{8,72},{12,76},{16,80},{20,84},{24,88},{28,92},{32,9... | collective-permute-start | bytes 221192 | tf_op jit(solution)/shard_map/ppermute | solution.py:277
  37.7 2.0 %copy-start.4 = (bf16[1,128,128]{2,1,0:T(8,128)(2,1)S(1)}, bf16[1,128,128]{2,1,0:T(8,128)(2,1)}, u32[]{:S(2)}) copy-start(bf16[1,128,128]{2,1,0:T(8,128)(2,1)} %param.18) | copy-start | bytes 98308
  37.7 2.0 %copy-start.5 = (bf16[1,128,128]{2,1,0:T(8,128)(2,1)S(1)}, bf16[1,128,128]{2,1,0:T(8,128)(2,1)}, u32[]{:S(2)}) copy-start(bf16[1,128,128]{2,1,0:T(8,128)(2,1)} %param.17) | copy-start | bytes 98308
  42.9 25.8 %copy-start.1 = (f32[1,16]{1,0:T(1,128)S(1)}, f32[1,16]{1,0:T(1,128)}, u32[]{:S(2)}) copy-start(f32[1,16]{1,0:T(1,128)} %bias.1) | copy-start | bytes 196
  42.9 25.8 %copy-start.2 = (f32[1,16]{1,0:T(1,128)S(1)}, f32[1,16]{1,0:T(1,128)}, u32[]{:S(2)}) copy-start(f32[1,16]{1,0:T(1,128)} %rate.1) | copy-start | bytes 196
  42.9 25.8 %copy-start.3 = (f32[1,16]{1,0:T(1,128)S(1)}, f32[1,16]{1,0:T(1,128)}, u32[]{:S(2)}) copy-start(f32[1,16]{1,0:T(1,128)} %skip.1) | copy-start | bytes 196
  42.9 25.8 %all-to-all-start = ((bf16[4,192,1024]{2,1,0:T(8,128)(2,1)}), bf16[4,192,1024]{2,1,0:T(8,128)(2,1)S(1)}, u32[]{:S(2)}, u32[]{:S(2)}) async-start(bf16[4,192,1024]{2,1,0:T(8,128)(2,1)} %pad_maximum_fusion), calls=%async_computation | async-start | bytes 3145728 | tf_op jit(solution)/shard_map/all_to_all | solution.py:328
  48.7 35.2 %collective-permute-start.5 = (bf16[576,256]{1,0:T(8,128)(2,1)}, bf16[576,256]{1,0:T(8,128)(2,1)}, u32[]{:S(2)}, u32[]{:S(2)}) collective-permute-start(bf16[576,256]{1,0:T(8,128)(2,1)} %constant_dynamic-update-slice_fusion), channel_id=1, source_target_pairs={{0,8},{4,12},{8,16},{12,20},{16,24},{20,28},{24,32},{28,36},{32,40... | collective-permute-start | bytes 884744 | tf_op jit(solution)/shard_map/ppermute | solution.py:277
  56.3 28.6 %collective-permute-start.6 = (bf16[576,256]{1,0:T(8,128)(2,1)}, bf16[576,256]{1,0:T(8,128)(2,1)}, u32[]{:S(2)}, u32[]{:S(2)}) collective-permute-start(bf16[576,256]{1,0:T(8,128)(2,1)} %constant_dynamic-update-slice_fusion), channel_id=1, source_target_pairs={{0,120},{4,124},{8,0},{12,4},{16,8},{20,12},{24,16},{28,20},{32,24... | collective-permute-start | bytes 884744 | tf_op jit(solution)/shard_map/ppermute | solution.py:277
  60.7 22.3 %collective-permute-start.3 = (bf16[288,256]{1,0:T(8,128)(2,1)}, bf16[288,256]{1,0:T(8,128)(2,1)}, u32[]{:S(2)}, u32[]{:S(2)}) collective-permute-start(bf16[288,256]{1,0:T(8,128)(2,1)} %get-tuple-element.31), channel_id=1, source_target_pairs={{0,16},{4,20},{8,24},{12,28},{16,32},{20,36},{24,40},{28,44},{32,4... | collective-permute-start | bytes 442376 | tf_op jit(solution)/shard_map/ppermute | solution.py:277
  62.6 21.3 %collective-permute-start.4 = (bf16[288,256]{1,0:T(8,128)(2,1)}, bf16[288,256]{1,0:T(8,128)(2,1)S(1)}, u32[]{:S(2)}, u32[]{:S(2)}) collective-permute-start(bf16[288,256]{1,0:T(8,128)(2,1)} %get-tuple-element.32), channel_id=1, source_target_pairs={{0,112},{4,116},{8,120},{12,124},{16,0},{20,4},{24,8},{28,12},{32,... | collective-permute-start | bytes 442376 | tf_op jit(solution)/shard_map/ppermute | solution.py:277
  85.9 4.8 %collective-permute-start.7 = (bf16[2304,256]{1,0:T(8,128)(2,1)S(1)}, bf16[2304,256]{1,0:T(8,128)(2,1)S(1)}, u32[]{:S(2)}, u32[]{:S(2)}) collective-permute-start(bf16[2304,256]{1,0:T(8,128)(2,1)S(1)} %constant_dynamic-update-slice_fusion.4.own), channel_id=1, source_target_pairs={{0,4},{4,0},{8,12},{12,8},{16,20},{20,16},{24,28},{28,24},{32,36},... | collective-permute-start | bytes 3538952 | tf_op jit(solution)/shard_map/ppermute | solution.py:281
  91.3 13.2 %collective-permute-start.8 = (bf16[128,256]{1,0:T(8,128)(2,1)S(1)}, bf16[128,256]{1,0:T(8,128)(2,1)S(1)}, u32[]{:S(2)}, u32[]{:S(2)}) collective-permute-start(bf16[128,256]{1,0:T(8,128)(2,1)S(1)} %get-tuple-element.37), channel_id=1, source_target_pairs={{0,32},{4,36},{8,40},{12,44},{16,48},{20,52},{24,56},{28,60},{32,6... | collective-permute-start | bytes 196616 | tf_op jit(solution)/shard_map/ppermute | solution.py:277
  94.3 18.1 %collective-permute-start.10 = (bf16[128,256]{1,0:T(8,128)(2,1)S(1)}, bf16[128,256]{1,0:T(8,128)(2,1)S(1)}, u32[]{:S(2)}, u32[]{:S(2)}) collective-permute-start(bf16[128,256]{1,0:T(8,128)(2,1)S(1)} %get-tuple-element.37), channel_id=1, source_target_pairs={{0,64},{4,68},{8,72},{12,76},{16,80},{20,84},{24,88},{28,92},{32,9... | collective-permute-start | bytes 196616 | tf_op jit(solution)/shard_map/ppermute | solution.py:277
  104.5 13.7 %collective-permute-start.9 = (bf16[256,256]{1,0:T(8,128)(2,1)S(1)}, bf16[256,256]{1,0:T(8,128)(2,1)S(1)}, u32[]{:S(2)}, u32[]{:S(2)}) collective-permute-start(bf16[256,256]{1,0:T(8,128)(2,1)S(1)} %constant_dynamic-update-slice_fusion.9), channel_id=1, source_target_pairs={{0,16},{4,20},{8,24},{12,28},{16,32},{20,36},{24,40},{28,44},{32,4... | collective-permute-start | bytes 393224 | tf_op jit(solution)/shard_map/ppermute | solution.py:277
  109.5 12.8 %collective-permute-start.11 = (bf16[256,256]{1,0:T(8,128)(2,1)S(1)}, bf16[256,256]{1,0:T(8,128)(2,1)S(1)}, u32[]{:S(2)}, u32[]{:S(2)}) collective-permute-start(bf16[256,256]{1,0:T(8,128)(2,1)S(1)} %constant_dynamic-update-slice_fusion.9), channel_id=1, source_target_pairs={{0,8},{4,12},{8,16},{12,20},{16,24},{20,28},{24,32},{28,36},{32,40... | collective-permute-start | bytes 393224 | tf_op jit(solution)/shard_map/ppermute | solution.py:277
  112.4 9.9 %collective-permute-start.12 = (bf16[256,256]{1,0:T(8,128)(2,1)S(1)}, bf16[256,256]{1,0:T(8,128)(2,1)S(1)}, u32[]{:S(2)}, u32[]{:S(2)}) collective-permute-start(bf16[256,256]{1,0:T(8,128)(2,1)S(1)} %pad_maximum_fusion.3), channel_id=1, source_target_pairs={{0,120},{4,124},{8,0},{12,4},{16,8},{20,12},{24,16},{28,20},{32,24... | collective-permute-start | bytes 393224 | tf_op jit(solution)/shard_map/ppermute | solution.py:277
  122.3 3.9 %collective-permute-start.13 = (bf16[1152,256]{1,0:T(8,128)(2,1)S(1)}, bf16[1152,256]{1,0:T(8,128)(2,1)S(1)}, u32[]{:S(2)}, u32[]{:S(2)}) collective-permute-start(bf16[1152,256]{1,0:T(8,128)(2,1)S(1)} %constant_dynamic-update-slice_fusion.11.own), channel_id=1, source_target_pairs={{0,4},{4,0},{8,12},{12,8},{16,20},{20,16},{24,28},{28,24},{32,36},... | collective-permute-start | bytes 1769480 | tf_op jit(solution)/shard_map/ppermute | solution.py:281
  126.2 1.0 copy-start
  128.6 16.7 %collective-permute-start.14 = (bf16[128,768]{1,0:T(8,128)(2,1)S(1)}, bf16[128,768]{1,0:T(8,128)(2,1)S(1)}, u32[]{:S(2)}, u32[]{:S(2)}) collective-permute-start(bf16[128,768]{1,0:T(8,128)(2,1)S(1)} %finish_low.1), channel_id=1, source_target_pairs={{0,128},{128,256},{256,384},{1,129},{129,257},{257,385},{2,130},{1... | collective-permute-start | bytes 589832 | tf_op jit(solution)/shard_map/ppermute | solution.py:396
  139.1 6.2 %collective-permute-start.15 = (bf16[128,256]{1,0:T(8,128)(2,1)S(1)}, bf16[128,256]{1,0:T(8,128)(2,1)S(1)}, u32[]{:S(2)}, u32[]{:S(2)}) collective-permute-start(bf16[128,256]{1,0:T(8,128)(2,1)S(1)} %finish_high.1), channel_id=1, source_target_pairs={{0,128},{128,256},{256,384},{1,129},{129,257},{257,385},{2,130},{1... | collective-permute-start | bytes 196616 | tf_op jit(solution)/shard_map/ppermute | solution.py:396
Sparse Core Ops, SparseCore 0:
  10.1 110.6 all-gather.2

commit v6 on v4

--- a/solution.py
+++ b/solution.py
@@ -20,7 +20,7 @@
 
 W_FIRST = (-4, 0, 4, -8)
 W_REL = tuple(a + b for b in (0, -1, 1) for a in W_FIRST) + (-6, -2, 2, 6)
-KV_AT = (0, 3, 5, 7, 1, 4, 6, 8, 2)
+KV_AT = (0, 5, 3, 7, 1, 6, 4, 8, 2)
 
 
 def iota(shape, dim):
@@ -118,17 +118,20 @@
         pay[...] = states[...]
 
 
-def query(scal, xn, wq, out, wbuf, sem):
+def query(scal, xn, wq, out, wbuf, total, sem):
     @pl.when(scal[0] == 1)
     def _():
+        parts = [slice(j * 512, (j + 1) * 512) for j in range(8)]
         copies = [
-            pltpu.make_async_copy(wq.at[:, pl.ds(j * 256, 256)], wbuf.at[j], sem.at[j]) for j in range(4)
+            pltpu.make_async_copy(wq.at[part, :], wbuf.at[part, :], sem.at[j]) for j, part in enumerate(parts)
         ]
         for copy in copies:
             copy.start()
-        for j, copy in enumerate(copies):
+        for j, (copy, part) in enumerate(zip(copies, parts)):
             copy.wait()
-            out[:, j * 256 : (j + 1) * 256] = dot(xn[...], wbuf[j]).astype(BF)
+            product = dot(xn[:, part], wbuf[part, :])
+            total[...] = product if j == 0 else total[...] + product
+        out[...] = total[...].astype(BF)
 
 
 def attend(pairs, h, q, keys, values, mask, out):
@@ -323,7 +326,8 @@
     wkv = jnp.concatenate([wkv, jnp.pad(idr.astype(BF), ((0, 15), (0, 128)))], axis=0)
     a, b, c = [by_chips(wkv, k) for k in (4, -4, 8)]
     first = jnp.concatenate([a, wkv, b, c], axis=0)
-    parts, first = lax.optimization_barrier((parts, first))
+    halves = [jnp.concatenate([a, wkv], axis=0), jnp.concatenate([wkv, b], axis=0)]
+    parts, first, halves = lax.optimization_barrier((parts, first, halves))
     got = lax.all_to_all(parts, "tp", 0, 0)
     xn, states, yloc, aux = kernel(
         front,
@@ -336,8 +340,8 @@
     others = [
         by_chips(first, 1),
         by_chips(first, -1),
-        by_chips(first[: 2 * WROWS], 2),
-        by_chips(first[WROWS : 3 * WROWS], -2),
+        by_chips(halves[0], 2),
+        by_chips(halves[1], -2),
     ]
     first, xn = lax.optimization_barrier((first, xn))
     weights = jnp.concatenate([first] + others, axis=0)
@@ -357,14 +361,18 @@
         52,
         shape(ROWS, COLS),
         [SMEM, VMEM, ANY],
-        [pltpu.VMEM((4, D, 256), BF), pltpu.SemaphoreType.DMA((4,))],
+        [
+            pltpu.VMEM((D, COLS), BF),
+            pltpu.VMEM((ROWS, COLS), F32),
+            pltpu.SemaphoreType.DMA((8,)),
+        ],
     )(scal, xn, wq)
 
     back4, back8 = by_chips(pay, 4), by_chips(pay, 8)
     near = jnp.concatenate([pay, back4], axis=0)
     far = jnp.concatenate([back4, back8], axis=0)
     own = jnp.concatenate(
-        [pay, back4, back8, by_chips(near, 1), by_chips(near, 2), by_chips(far, -1)], axis=0
+        [pay, back4, back8, by_chips(near, 2), by_chips(near, 1), by_chips(far, -1)], axis=0
     )
     sib = swap(own)
     sib, q = lax.optimization_barrier((sib, q))

time: 153 us -> 152 us (level)
  the two profiles are of different devices: /device:TPU:20 before, /device:TPU:12 now
where the time goes in v6:
time: 152 us
  starting transfers between devices  82.8 us (54%)
  waiting for transfers between devices  26.6 us (18%)
  between operations  15.1 us (10%)
  Pallas kernels  13.1 us (9%)
  local copies, waits for them, and re-layouts  7.94 us (5%)
  other arithmetic  6.33 us (4%)
    ppermute x12, starting transfers between devices, by_chips(): lax.ppermute(x, 'ctx', [(i, (i + 2 * k) % (2 * CHIPS)) for i in range(2 *...  68.4 us
    ppermute x12, waiting for transfers between devices, by_chips(): lax.ppermute(x, 'ctx', [(i, (i + 2 * k) % (2 * CHIPS)) for i in range(2 *...  19.6 us
    unnamed x27, local copies, waits for them, and re-layouts  5.89 us
    pallas_call x2, Pallas kernels, shards(): kernel(body, us, 20, shape(ROWS, cols), [SMEM] + [VMEM] * 9)  5.75 us
    ppermute x2, starting transfers between devices, shards(): moved.append(lax.ppermute(part, 'pipe', [(i, i + 1) for i in range(3)]))  5.5 us
    all_to_all x1, starting transfers between devices, shards(): got = lax.all_to_all(parts, 'tp', 0, 0)  4.94 us
    pallas_call x1, Pallas kernels, shards(): kernel(query, 5, 52, shape(ROWS, COLS), [SMEM, VMEM, ANY], [pltpu.VMEM((D...  4.34 us
    ppermute x2, starting transfers between devices, swap(): return lax.ppermute(x, 'ctx', [(i, i ^ 1) for i in range(2 * CHIPS)])  3.84 us
  transfers between devices with their start and end apart: 18, of which 9 were waited for; matrix products, arithmetic and copies ran while one was open for 9% of the time, Pallas kernels for 6%

profile of v6, /device:TPU:12, one launch (start us, length us, event | category | flops | bytes accessed | tf_op | source)
XLA Modules:
  0.0 151.8 jit_solution(4957688785656783548)
XLA Ops:
  7.2 0.0 all-gather.3.cloned.1.call-start
  7.2 0.7 all-gather.3.cloned.1.call-update
  7.9 0.7 convert_bitcast_fusion.1
  8.6 0.8 pad_maximum_fusion.4
  9.4 9.1 %collective-permute-start = (bf16[144,256]{1,0:T(8,128)(2,1)S(1)}, bf16[144,256]{1,0:T(8,128)(2,1)S(1)}, u32[]{:S(2)}, u32[]{:S(2)}) collective-permute-start(bf16[144,256]{1,0:T(8,128)(2,1)S(1)} %pad_maximum_fusion.4), channel_id=1, source_target_pairs={{0,32},{4,36},{8,40},{12,44},{16,48},{20,52},{24,56},{28,60},{32,6... | collective-permute-start | bytes 221192 | tf_op jit(solution)/shard_map/ppermute | solution.py:280
  18.5 5.6 %collective-permute-start.1 = (bf16[144,256]{1,0:T(8,128)(2,1)S(1)}, bf16[144,256]{1,0:T(8,128)(2,1)S(1)}, u32[]{:S(2)}, u32[]{:S(2)}) collective-permute-start(bf16[144,256]{1,0:T(8,128)(2,1)S(1)} %pad_maximum_fusion.4), channel_id=1, source_target_pairs={{0,96},{4,100},{8,104},{12,108},{16,112},{20,116},{24,120},{28,124... | collective-permute-start | bytes 221192 | tf_op jit(solution)/shard_map/ppermute | solution.py:280
  24.0 10.8 %collective-permute-start.2 = (bf16[144,256]{1,0:T(8,128)(2,1)S(1)}, bf16[144,256]{1,0:T(8,128)(2,1)S(1)}, u32[]{:S(2)}, u32[]{:S(2)}) collective-permute-start(bf16[144,256]{1,0:T(8,128)(2,1)S(1)} %pad_maximum_fusion.4), channel_id=1, source_target_pairs={{0,64},{4,68},{8,72},{12,76},{16,80},{20,84},{24,88},{28,92},{32,9... | collective-permute-start | bytes 221192 | tf_op jit(solution)/shard_map/ppermute | solution.py:280
  34.9 0.1 pad.31.clone
  35.0 0.7 reduce-precision_convert_fusion.1
  35.7 0.1 maximum_maximum_fusion
  35.8 1.1 broadcast_in_dim.32
  36.9 0.0 copy-start.4
  36.9 0.0 copy-start.5
  36.9 1.3 pad_maximum_fusion
  38.2 0.6 constant_dynamic-update-slice_fusion.3
  38.8 0.6 maximum_dynamic-update-slice_fusion
  39.5 0.6 constant_dynamic-update-slice_fusion.2
  40.1 0.0 collective-permute-done.1
  40.1 0.6 constant_dynamic-update-slice_fusion.1
  40.7 0.0 collective-permute-done.2
  40.7 0.6 constant_dynamic-update-slice_fusion
  41.3 0.7 pad_maximum_fusion.2
  42.1 4.9 %all-to-all-start = ((bf16[4,192,1024]{2,1,0:T(8,128)(2,1)}), bf16[4,192,1024]{2,1,0:T(8,128)(2,1)S(1)}, u32[]{:S(2)}, u32[]{:S(2)}) async-start(bf16[4,192,1024]{2,1,0:T(8,128)(2,1)} %pad_maximum_fusion), calls=%async_computation | async-start | bytes 3145728 | tf_op jit(solution)/shard_map/all_to_all | solution.py:331
  47.7 0.1 copy.14.idc_ref
  47.8 0.1 stack.22.scal.refs_0_
  47.9 8.5 %collective-permute-start.3 = (bf16[576,256]{1,0:T(8,128)(2,1)}, bf16[576,256]{1,0:T(8,128)(2,1)}, u32[]{:S(2)}, u32[]{:S(2)}) collective-permute-start(bf16[576,256]{1,0:T(8,128)(2,1)} %constant_dynamic-update-slice_fusion), channel_id=1, source_target_pairs={{0,8},{4,12},{8,16},{12,20},{16,24},{20,28},{24,32},{28,36},{32,40... | collective-permute-start | bytes 884744 | tf_op jit(solution)/shard_map/ppermute | solution.py:280
  56.3 4.4 %collective-permute-start.4 = (bf16[576,256]{1,0:T(8,128)(2,1)}, bf16[576,256]{1,0:T(8,128)(2,1)}, u32[]{:S(2)}, u32[]{:S(2)}) collective-permute-start(bf16[576,256]{1,0:T(8,128)(2,1)} %constant_dynamic-update-slice_fusion), channel_id=1, source_target_pairs={{0,120},{4,124},{8,0},{12,4},{16,8},{20,12},{24,16},{28,20},{32,24... | collective-permute-start | bytes 884744 | tf_op jit(solution)/shard_map/ppermute | solution.py:280
  60.7 1.9 %collective-permute-start.5 = (bf16[288,256]{1,0:T(8,128)(2,1)}, bf16[288,256]{1,0:T(8,128)(2,1)}, u32[]{:S(2)}, u32[]{:S(2)}) collective-permute-start(bf16[288,256]{1,0:T(8,128)(2,1)} %get-tuple-element.29), channel_id=1, source_target_pairs={{0,16},{4,20},{8,24},{12,28},{16,32},{20,36},{24,40},{28,44},{32,4... | collective-permute-start | bytes 442376 | tf_op jit(solution)/shard_map/ppermute | solution.py:280
  62.7 6.0 %collective-permute-start.6 = (bf16[288,256]{1,0:T(8,128)(2,1)}, bf16[288,256]{1,0:T(8,128)(2,1)S(1)}, u32[]{:S(2)}, u32[]{:S(2)}) collective-permute-start(bf16[288,256]{1,0:T(8,128)(2,1)} %get-tuple-element.30), channel_id=1, source_target_pairs={{0,112},{4,116},{8,120},{12,124},{16,0},{20,4},{24,8},{28,12},{32,... | collective-permute-start | bytes 442376 | tf_op jit(solution)/shard_map/ppermute | solution.py:280
  68.7 1.0 front.1
  69.8 1.0 constant_dynamic-update-slice_fusion.8
  70.8 2.3 %collective-permute-done.3 = bf16[576,256]{1,0:T(8,128)(2,1)} collective-permute-done((bf16[576,256]{1,0:T(8,128)(2,1)}, bf16[576,256]{1,0:T(8,128)(2,1)}, u32[]{:S(2)}, u32[]{:S(2)}) %collective-permute-start.3) | collective-permute-done | bytes 294944 | tf_op jit(solution)/shard_map/ppermute | solution.py:280
  73.1 1.0 constant_dynamic-update-slice_fusion.7
  74.0 2.6 %collective-permute-done.4 = bf16[576,256]{1,0:T(8,128)(2,1)} collective-permute-done((bf16[576,256]{1,0:T(8,128)(2,1)}, bf16[576,256]{1,0:T(8,128)(2,1)}, u32[]{:S(2)}, u32[]{:S(2)}) %collective-permute-start.4) | collective-permute-done | bytes 294944 | tf_op jit(solution)/shard_map/ppermute | solution.py:280
  76.6 1.0 constant_dynamic-update-slice_fusion.6
  77.6 5.1 %collective-permute-done.5 = bf16[288,256]{1,0:T(8,128)(2,1)} collective-permute-done((bf16[288,256]{1,0:T(8,128)(2,1)}, bf16[288,256]{1,0:T(8,128)(2,1)}, u32[]{:S(2)}, u32[]{:S(2)}) %collective-permute-start.5) | collective-permute-done | bytes 147488 | tf_op jit(solution)/shard_map/ppermute | solution.py:280
  82.7 0.9 constant_dynamic-update-slice_fusion.5
  83.6 0.0 collective-permute-done.6
  83.7 1.9 %collective-permute-start.7 = (bf16[2304,256]{1,0:T(8,128)(2,1)S(1)}, bf16[2304,256]{1,0:T(8,128)(2,1)S(1)}, u32[]{:S(2)}, u32[]{:S(2)}) collective-permute-start(bf16[2304,256]{1,0:T(8,128)(2,1)S(1)} %constant_dynamic-update-slice_fusion.4.own), channel_id=1, source_target_pairs={{0,4},{4,0},{8,12},{12,8},{16,20},{20,16},{24,28},{28,24},{32,36},... | collective-permute-start | bytes 3538952 | tf_op jit(solution)/shard_map/ppermute | solution.py:284
  85.6 2.8 %collective-permute-done.7.sib = bf16[2304,256]{1,0:T(8,128)(2,1)S(1)} collective-permute-done((bf16[2304,256]{1,0:T(8,128)(2,1)S(1)}, bf16[2304,256]{1,0:T(8,128)(2,1)S(1)}, u32[]{:S(2)}, u32[]{:S(2)}) %collective-permute-start.7) | collective-permute-done | bytes 1179680 | tf_op jit(solution)/shard_map/ppermute | solution.py:284
  88.4 1.2 project.1
  89.6 3.3 %collective-permute-start.8 = (bf16[128,256]{1,0:T(8,128)(2,1)S(1)}, bf16[128,256]{1,0:T(8,128)(2,1)S(1)}, u32[]{:S(2)}, u32[]{:S(2)}) collective-permute-start(bf16[128,256]{1,0:T(8,128)(2,1)S(1)} %get-tuple-element.32), channel_id=1, source_target_pairs={{0,32},{4,36},{8,40},{12,44},{16,48},{20,52},{24,56},{28,60},{32,6... | collective-permute-start | bytes 196616 | tf_op jit(solution)/shard_map/ppermute | solution.py:280
  92.9 8.8 %collective-permute-start.9 = (bf16[128,256]{1,0:T(8,128)(2,1)S(1)}, bf16[128,256]{1,0:T(8,128)(2,1)S(1)}, u32[]{:S(2)}, u32[]{:S(2)}) collective-permute-start(bf16[128,256]{1,0:T(8,128)(2,1)S(1)} %get-tuple-element.32), channel_id=1, source_target_pairs={{0,64},{4,68},{8,72},{12,76},{16,80},{20,84},{24,88},{28,92},{32,9... | collective-permute-start | bytes 196616 | tf_op jit(solution)/shard_map/ppermute | solution.py:280
  101.7 1.2 collective-permute-done.8
  102.9 5.4 %collective-permute-start.10 = (bf16[256,256]{1,0:T(8,128)(2,1)S(1)}, bf16[256,256]{1,0:T(8,128)(2,1)S(1)}, u32[]{:S(2)}, u32[]{:S(2)}) collective-permute-start(bf16[256,256]{1,0:T(8,128)(2,1)S(1)} %get-tuple-element.48), channel_id=1, source_target_pairs={{0,16},{4,20},{8,24},{12,28},{16,32},{20,36},{24,40},{28,44},{32,4... | collective-permute-start | bytes 393224 | tf_op jit(solution)/shard_map/ppermute | solution.py:280
  108.3 1.9 %collective-permute-start.11 = (bf16[256,256]{1,0:T(8,128)(2,1)S(1)}, bf16[256,256]{1,0:T(8,128)(2,1)S(1)}, u32[]{:S(2)}, u32[]{:S(2)}) collective-permute-start(bf16[256,256]{1,0:T(8,128)(2,1)S(1)} %get-tuple-element.48), channel_id=1, source_target_pairs={{0,8},{4,12},{8,16},{12,20},{16,24},{20,28},{24,32},{28,36},{32,40... | collective-permute-start | bytes 393224 | tf_op jit(solution)/shard_map/ppermute | solution.py:280
  110.2 2.3 %collective-permute-done.9 = bf16[128,256]{1,0:T(8,128)(2,1)S(1)} collective-permute-done((bf16[128,256]{1,0:T(8,128)(2,1)S(1)}, bf16[128,256]{1,0:T(8,128)(2,1)S(1)}, u32[]{:S(2)}, u32[]{:S(2)}) %collective-permute-start.9) | collective-permute-done | bytes 65568 | tf_op jit(solution)/shard_map/ppermute | solution.py:280
  112.6 2.8 %collective-permute-start.12 = (bf16[256,256]{1,0:T(8,128)(2,1)S(1)}, bf16[256,256]{1,0:T(8,128)(2,1)S(1)}, u32[]{:S(2)}, u32[]{:S(2)}) collective-permute-start(bf16[256,256]{1,0:T(8,128)(2,1)S(1)} %pad_maximum_fusion.3), channel_id=1, source_target_pairs={{0,120},{4,124},{8,0},{12,4},{16,8},{20,12},{24,16},{28,20},{32,24... | collective-permute-start | bytes 393224 | tf_op jit(solution)/shard_map/ppermute | solution.py:280
  115.4 2.8 %collective-permute-done.10 = bf16[256,256]{1,0:T(8,128)(2,1)S(1)} collective-permute-done((bf16[256,256]{1,0:T(8,128)(2,1)S(1)}, bf16[256,256]{1,0:T(8,128)(2,1)S(1)}, u32[]{:S(2)}, u32[]{:S(2)}) %collective-permute-start.10) | collective-permute-done | bytes 131104 | tf_op jit(solution)/shard_map/ppermute | solution.py:280
  118.2 3.2 %collective-permute-done.11 = bf16[256,256]{1,0:T(8,128)(2,1)S(1)} collective-permute-done((bf16[256,256]{1,0:T(8,128)(2,1)S(1)}, bf16[256,256]{1,0:T(8,128)(2,1)S(1)}, u32[]{:S(2)}, u32[]{:S(2)}) %collective-permute-start.11) | collective-permute-done | bytes 131104 | tf_op jit(solution)/shard_map/ppermute | solution.py:280
  121.5 1.9 %collective-permute-start.13 = (bf16[1152,256]{1,0:T(8,128)(2,1)S(1)}, bf16[1152,256]{1,0:T(8,128)(2,1)S(1)}, u32[]{:S(2)}, u32[]{:S(2)}) collective-permute-start(bf16[1152,256]{1,0:T(8,128)(2,1)S(1)} %constant_dynamic-update-slice_fusion.11.own), channel_id=1, source_target_pairs={{0,4},{4,0},{8,12},{12,8},{16,20},{20,16},{24,28},{28,24},{32,36},... | collective-permute-start | bytes 1769480 | tf_op jit(solution)/shard_map/ppermute | solution.py:284
  123.4 0.0 all-gather.3.cloned.1.call-done
  123.4 4.3 %query.1.refs_2_ = bf16[128,1024]{1,0:T(8,128)(2,1)S(1)} custom-call(s32[5]{0:T(128)S(1)} %stack.22.scal.refs_0_, bf16[128,4096]{1,0:T(8,128)(2,1)S(1)} %get-tuple-element.27.xn, bf16[4096,1024]{1,0:T(8,128)(2,1)} %bitcast.37), custom_call_target="tpu_custom_call" | custom-call | flops 5750000128 | bytes 1048576 | tf_op jit(solution)/shard_map/query/pallas_call | solution.py:358
  127.8 0.0 collective-permute-done.13.sib
  127.8 0.0 copy-start
  127.8 0.8 assemble.1
  128.7 0.1 copy-done
  128.8 3.8 %finish_low.1 = bf16[128,768]{1,0:T(8,128)(2,1)S(1)} custom-call(s32[5]{0:T(128)S(1)} %stack.22.scal.refs_0_, bf16[128,1024]{1,0:T(8,128)(2,1)S(1)} %bitcast.27, bf16[128,1024]{1,0:T(8,128)(2,1)S(1)} %query.1.refs_2_, bf16[2304,128]{1,0:T(8,128)(2,1)S(1)} %get-tuple-element.37.refs_3_, bf16[2304,128]{1,0:T(8,128)(2,1)S(1)} %get-tuple-element.38.refs_4_, ...), custom_call_target="tpu_custom_call" | custom-call | flops 4600000000 | bytes 1048576 | tf_op jit(solution)/shard_map/finish_low/pallas_call | solution.py:396
  132.6 3.6 %collective-permute-start.14 = (bf16[128,768]{1,0:T(8,128)(2,1)S(1)}, bf16[128,768]{1,0:T(8,128)(2,1)S(1)}, u32[]{:S(2)}, u32[]{:S(2)}) collective-permute-start(bf16[128,768]{1,0:T(8,128)(2,1)S(1)} %finish_low.1), channel_id=1, source_target_pairs={{0,128},{128,256},{256,384},{1,129},{129,257},{257,385},{2,130},{1... | collective-permute-start | bytes 589832 | tf_op jit(solution)/shard_map/ppermute | solution.py:401
  136.2 1.9 %finish_high.1 = bf16[128,256]{1,0:T(8,128)(2,1)S(1)} custom-call(s32[5]{0:T(128)S(1)} %stack.22.scal.refs_0_, bf16[128,1024]{1,0:T(8,128)(2,1)S(1)} %bitcast.28, bf16[128,1024]{1,0:T(8,128)(2,1)S(1)} %query.1.refs_2_, bf16[2304,128]{1,0:T(8,128)(2,1)S(1)} %get-tuple-element.37.refs_3_, bf16[2304,128]{1,0:T(8,128)(2,1)S(1)} %get-tuple-element.38.refs_4_, ...), custom_call_target="tpu_custom_call" | custom-call | flops 2300000000 | bytes 1048576 | tf_op jit(solution)/shard_map/finish_high/pallas_call | solution.py:396
  138.1 1.9 %collective-permute-start.15 = (bf16[128,256]{1,0:T(8,128)(2,1)S(1)}, bf16[128,256]{1,0:T(8,128)(2,1)S(1)}, u32[]{:S(2)}, u32[]{:S(2)}) collective-permute-start(bf16[128,256]{1,0:T(8,128)(2,1)S(1)} %finish_high.1), channel_id=1, source_target_pairs={{0,128},{128,256},{256,384},{1,129},{129,257},{257,385},{2,130},{1... | collective-permute-start | bytes 196616 | tf_op jit(solution)/shard_map/ppermute | solution.py:401
  140.0 0.7 maximum_bitcast_fusion
  140.8 3.5 %collective-permute-done.15 = bf16[128,256]{1,0:T(8,128)(2,1)S(1)} collective-permute-done((bf16[128,256]{1,0:T(8,128)(2,1)S(1)}, bf16[128,256]{1,0:T(8,128)(2,1)S(1)}, u32[]{:S(2)}, u32[]{:S(2)}) %collective-permute-start.15) | collective-permute-done | bytes 65568 | tf_op jit(solution)/shard_map/ppermute | solution.py:401
  144.3 0.7 maximum_bitcast_fusion.1
  (28 shorter events, 0.2 us)
Async XLA Ops:
  7.2 29.7 %copy-start.7 = (bf16[1,1024,32]{1,2,0:T(8,128)(2,1)S(1)}, bf16[1,1024,32]{1,2,0:T(8,128)(2,1)}, u32[]{:S(2)}) copy-start(bf16[1,1024,32]{1,2,0:T(8,128)(2,1)} %param.19) | copy-start | bytes 196612
  7.2 29.7 %copy-start.6 = (bf16[1,1024,64]{1,2,0:T(8,128)(2,1)S(1)}, bf16[1,1024,64]{1,2,0:T(8,128)(2,1)}, u32[]{:S(2)}) copy-start(bf16[1,1024,64]{1,2,0:T(8,128)(2,1)} %param.20) | copy-start | bytes 393220
  7.2 116.3 %all-gather.3.cloned.1.call-start = ((), (), s32[]{:S(2)}) async-start(), calls=%async_computation.1 | async-start | bytes 8650752 | tf_op jit(solution)/shard_map/all_gather | solution.py:308
  9.4 28.8 %collective-permute-start = (bf16[144,256]{1,0:T(8,128)(2,1)S(1)}, bf16[144,256]{1,0:T(8,128)(2,1)S(1)}, u32[]{:S(2)}, u32[]{:S(2)}) collective-permute-start(bf16[144,256]{1,0:T(8,128)(2,1)S(1)} %pad_maximum_fusion.4), channel_id=1, source_target_pairs={{0,32},{4,36},{8,40},{12,44},{16,48},{20,52},{24,56},{28,60},{32,6... | collective-permute-start | bytes 221192 | tf_op jit(solution)/shard_map/ppermute | solution.py:280
  18.5 21.6 %collective-permute-start.1 = (bf16[144,256]{1,0:T(8,128)(2,1)S(1)}, bf16[144,256]{1,0:T(8,128)(2,1)S(1)}, u32[]{:S(2)}, u32[]{:S(2)}) collective-permute-start(bf16[144,256]{1,0:T(8,128)(2,1)S(1)} %pad_maximum_fusion.4), channel_id=1, source_target_pairs={{0,96},{4,100},{8,104},{12,108},{16,112},{20,116},{24,120},{28,124... | collective-permute-start | bytes 221192 | tf_op jit(solution)/shard_map/ppermute | solution.py:280
  24.0 16.7 %collective-permute-start.2 = (bf16[144,256]{1,0:T(8,128)(2,1)S(1)}, bf16[144,256]{1,0:T(8,128)(2,1)S(1)}, u32[]{:S(2)}, u32[]{:S(2)}) collective-permute-start(bf16[144,256]{1,0:T(8,128)(2,1)S(1)} %pad_maximum_fusion.4), channel_id=1, source_target_pairs={{0,64},{4,68},{8,72},{12,76},{16,80},{20,84},{24,88},{28,92},{32,9... | collective-permute-start | bytes 221192 | tf_op jit(solution)/shard_map/ppermute | solution.py:280
  36.9 2.0 %copy-start.4 = (bf16[1,128,128]{2,1,0:T(8,128)(2,1)S(1)}, bf16[1,128,128]{2,1,0:T(8,128)(2,1)}, u32[]{:S(2)}) copy-start(bf16[1,128,128]{2,1,0:T(8,128)(2,1)} %param.18) | copy-start | bytes 98308
  36.9 1.9 %copy-start.5 = (bf16[1,128,128]{2,1,0:T(8,128)(2,1)S(1)}, bf16[1,128,128]{2,1,0:T(8,128)(2,1)}, u32[]{:S(2)}) copy-start(bf16[1,128,128]{2,1,0:T(8,128)(2,1)} %param.17) | copy-start | bytes 98308
  42.1 26.6 %copy-start.1 = (f32[1,16]{1,0:T(1,128)S(1)}, f32[1,16]{1,0:T(1,128)}, u32[]{:S(2)}) copy-start(f32[1,16]{1,0:T(1,128)} %bias.1) | copy-start | bytes 196
  42.1 26.6 %copy-start.2 = (f32[1,16]{1,0:T(1,128)S(1)}, f32[1,16]{1,0:T(1,128)}, u32[]{:S(2)}) copy-start(f32[1,16]{1,0:T(1,128)} %rate.1) | copy-start | bytes 196
  42.1 26.7 %copy-start.3 = (f32[1,16]{1,0:T(1,128)S(1)}, f32[1,16]{1,0:T(1,128)}, u32[]{:S(2)}) copy-start(f32[1,16]{1,0:T(1,128)} %skip.1) | copy-start | bytes 196
  42.1 26.6 %all-to-all-start = ((bf16[4,192,1024]{2,1,0:T(8,128)(2,1)}), bf16[4,192,1024]{2,1,0:T(8,128)(2,1)S(1)}, u32[]{:S(2)}, u32[]{:S(2)}) async-start(bf16[4,192,1024]{2,1,0:T(8,128)(2,1)} %pad_maximum_fusion), calls=%async_computation | async-start | bytes 3145728 | tf_op jit(solution)/shard_map/all_to_all | solution.py:331
  47.9 25.2 %collective-permute-start.3 = (bf16[576,256]{1,0:T(8,128)(2,1)}, bf16[576,256]{1,0:T(8,128)(2,1)}, u32[]{:S(2)}, u32[]{:S(2)}) collective-permute-start(bf16[576,256]{1,0:T(8,128)(2,1)} %constant_dynamic-update-slice_fusion), channel_id=1, source_target_pairs={{0,8},{4,12},{8,16},{12,20},{16,24},{20,28},{24,32},{28,36},{32,40... | collective-permute-start | bytes 884744 | tf_op jit(solution)/shard_map/ppermute | solution.py:280
  56.3 20.3 %collective-permute-start.4 = (bf16[576,256]{1,0:T(8,128)(2,1)}, bf16[576,256]{1,0:T(8,128)(2,1)}, u32[]{:S(2)}, u32[]{:S(2)}) collective-permute-start(bf16[576,256]{1,0:T(8,128)(2,1)} %constant_dynamic-update-slice_fusion), channel_id=1, source_target_pairs={{0,120},{4,124},{8,0},{12,4},{16,8},{20,12},{24,16},{28,20},{32,24... | collective-permute-start | bytes 884744 | tf_op jit(solution)/shard_map/ppermute | solution.py:280
  60.7 22.0 %collective-permute-start.5 = (bf16[288,256]{1,0:T(8,128)(2,1)}, bf16[288,256]{1,0:T(8,128)(2,1)}, u32[]{:S(2)}, u32[]{:S(2)}) collective-permute-start(bf16[288,256]{1,0:T(8,128)(2,1)} %get-tuple-element.29), channel_id=1, source_target_pairs={{0,16},{4,20},{8,24},{12,28},{16,32},{20,36},{24,40},{28,44},{32,4... | collective-permute-start | bytes 442376 | tf_op jit(solution)/shard_map/ppermute | solution.py:280
  62.7 21.0 %collective-permute-start.6 = (bf16[288,256]{1,0:T(8,128)(2,1)}, bf16[288,256]{1,0:T(8,128)(2,1)S(1)}, u32[]{:S(2)}, u32[]{:S(2)}) collective-permute-start(bf16[288,256]{1,0:T(8,128)(2,1)} %get-tuple-element.30), channel_id=1, source_target_pairs={{0,112},{4,116},{8,120},{12,124},{16,0},{20,4},{24,8},{28,12},{32,... | collective-permute-start | bytes 442376 | tf_op jit(solution)/shard_map/ppermute | solution.py:280
  83.7 4.7 %collective-permute-start.7 = (bf16[2304,256]{1,0:T(8,128)(2,1)S(1)}, bf16[2304,256]{1,0:T(8,128)(2,1)S(1)}, u32[]{:S(2)}, u32[]{:S(2)}) collective-permute-start(bf16[2304,256]{1,0:T(8,128)(2,1)S(1)} %constant_dynamic-update-slice_fusion.4.own), channel_id=1, source_target_pairs={{0,4},{4,0},{8,12},{12,8},{16,20},{20,16},{24,28},{28,24},{32,36},... | collective-permute-start | bytes 3538952 | tf_op jit(solution)/shard_map/ppermute | solution.py:284
  89.6 13.3 %collective-permute-start.8 = (bf16[128,256]{1,0:T(8,128)(2,1)S(1)}, bf16[128,256]{1,0:T(8,128)(2,1)S(1)}, u32[]{:S(2)}, u32[]{:S(2)}) collective-permute-start(bf16[128,256]{1,0:T(8,128)(2,1)S(1)} %get-tuple-element.32), channel_id=1, source_target_pairs={{0,32},{4,36},{8,40},{12,44},{16,48},{20,52},{24,56},{28,60},{32,6... | collective-permute-start | bytes 196616 | tf_op jit(solution)/shard_map/ppermute | solution.py:280
  92.9 19.7 %collective-permute-start.9 = (bf16[128,256]{1,0:T(8,128)(2,1)S(1)}, bf16[128,256]{1,0:T(8,128)(2,1)S(1)}, u32[]{:S(2)}, u32[]{:S(2)}) collective-permute-start(bf16[128,256]{1,0:T(8,128)(2,1)S(1)} %get-tuple-element.32), channel_id=1, source_target_pairs={{0,64},{4,68},{8,72},{12,76},{16,80},{20,84},{24,88},{28,92},{32,9... | collective-permute-start | bytes 196616 | tf_op jit(solution)/shard_map/ppermute | solution.py:280
  102.9 15.3 %collective-permute-start.10 = (bf16[256,256]{1,0:T(8,128)(2,1)S(1)}, bf16[256,256]{1,0:T(8,128)(2,1)S(1)}, u32[]{:S(2)}, u32[]{:S(2)}) collective-permute-start(bf16[256,256]{1,0:T(8,128)(2,1)S(1)} %get-tuple-element.48), channel_id=1, source_target_pairs={{0,16},{4,20},{8,24},{12,28},{16,32},{20,36},{24,40},{28,44},{32,4... | collective-permute-start | bytes 393224 | tf_op jit(solution)/shard_map/ppermute | solution.py:280
  108.3 13.2 %collective-permute-start.11 = (bf16[256,256]{1,0:T(8,128)(2,1)S(1)}, bf16[256,256]{1,0:T(8,128)(2,1)S(1)}, u32[]{:S(2)}, u32[]{:S(2)}) collective-permute-start(bf16[256,256]{1,0:T(8,128)(2,1)S(1)} %get-tuple-element.48), channel_id=1, source_target_pairs={{0,8},{4,12},{8,16},{12,20},{16,24},{20,28},{24,32},{28,36},{32,40... | collective-permute-start | bytes 393224 | tf_op jit(solution)/shard_map/ppermute | solution.py:280
  112.6 8.9 %collective-permute-start.12 = (bf16[256,256]{1,0:T(8,128)(2,1)S(1)}, bf16[256,256]{1,0:T(8,128)(2,1)S(1)}, u32[]{:S(2)}, u32[]{:S(2)}) collective-permute-start(bf16[256,256]{1,0:T(8,128)(2,1)S(1)} %pad_maximum_fusion.3), channel_id=1, source_target_pairs={{0,120},{4,124},{8,0},{12,4},{16,8},{20,12},{24,16},{28,20},{32,24... | collective-permute-start | bytes 393224 | tf_op jit(solution)/shard_map/ppermute | solution.py:280
  121.5 6.3 %collective-permute-start.13 = (bf16[1152,256]{1,0:T(8,128)(2,1)S(1)}, bf16[1152,256]{1,0:T(8,128)(2,1)S(1)}, u32[]{:S(2)}, u32[]{:S(2)}) collective-permute-start(bf16[1152,256]{1,0:T(8,128)(2,1)S(1)} %constant_dynamic-update-slice_fusion.11.own), channel_id=1, source_target_pairs={{0,4},{4,0},{8,12},{12,8},{16,20},{20,16},{24,28},{28,24},{32,36},... | collective-permute-start | bytes 1769480 | tf_op jit(solution)/shard_map/ppermute | solution.py:284
  127.8 1.0 copy-start
  132.6 11.7 %collective-permute-start.14 = (bf16[128,768]{1,0:T(8,128)(2,1)S(1)}, bf16[128,768]{1,0:T(8,128)(2,1)S(1)}, u32[]{:S(2)}, u32[]{:S(2)}) collective-permute-start(bf16[128,768]{1,0:T(8,128)(2,1)S(1)} %finish_low.1), channel_id=1, source_target_pairs={{0,128},{128,256},{256,384},{1,129},{129,257},{257,385},{2,130},{1... | collective-permute-start | bytes 589832 | tf_op jit(solution)/shard_map/ppermute | solution.py:401
  138.1 6.2 %collective-permute-start.15 = (bf16[128,256]{1,0:T(8,128)(2,1)S(1)}, bf16[128,256]{1,0:T(8,128)(2,1)S(1)}, u32[]{:S(2)}, u32[]{:S(2)}) collective-permute-start(bf16[128,256]{1,0:T(8,128)(2,1)S(1)} %finish_high.1), channel_id=1, source_target_pairs={{0,128},{128,256},{256,384},{1,129},{129,257},{257,385},{2,130},{1... | collective-permute-start | bytes 196616 | tf_op jit(solution)/shard_map/ppermute | solution.py:401
Sparse Core Ops, SparseCore 0:
  10.1 110.3 all-gather.2

commit v7 on v6

--- a/solution.py
+++ b/solution.py
@@ -19,7 +19,7 @@
 EXACT = lax.Precision.HIGHEST
 
 W_FIRST = (-4, 0, 4, -8)
-W_REL = tuple(a + b for b in (0, -1, 1) for a in W_FIRST) + (-6, -2, 2, 6)
+W_REL = W_FIRST + (-6, -2, 2, 6) + tuple(a + b for b in (-1, 1) for a in W_FIRST)
 KV_AT = (0, 5, 3, 7, 1, 6, 4, 8, 2)
 
 
@@ -95,12 +95,13 @@
         aux[...] = jnp.concatenate([cum, out_map, empty], axis=1)
 
 
-def project(scal, xn, own, sib, states, pay, kid, weight):
+def project(scal, xn, own_a, own_b, sib_a, sib_b, states, pay, kid, weight):
     attention, chip, core = scal[0], scal[2], scal[3]
     n = 0
     for r in range(BACK + 1):
-        at = [w % CHIPS for w in W_REL].index(-r % CHIPS) * WROWS + ROWS
-        for ref in (own, sib):
+        k = [w % CHIPS for w in W_REL].index(-r % CHIPS)
+        for ref in (own_a, sib_a) if k < 8 else (own_b, sib_b):
+            at = (k % 8) * WROWS + ROWS
             kid[n : n + 1, :] = ref[at : at + 16, :ROWS].astype(F32)[0:1, :]
             n += 1
 
@@ -108,7 +109,8 @@
     def _():
         for n, rel in enumerate(W_REL):
             at = lax.rem(chip + rel + CHIPS, CHIPS) * 256
-            rows = slice(n * WROWS, n * WROWS + ROWS)
+            own, sib = (own_a, sib_a) if n < 8 else (own_b, sib_b)
+            rows = slice(n % 8 * WROWS, n % 8 * WROWS + ROWS)
             weight[pl.ds(pl.multiple_of(at + core * 128, 128), 128), :] = own[rows, :]
             weight[pl.ds(pl.multiple_of(at + (1 - core) * 128, 128), 128), :] = sib[rows, :]
         pay[...] = dot(xn[...], weight[...]).astype(BF)
@@ -338,23 +340,23 @@
     )(scal, got, idc, idr, dt_bias, decay_rate, skip_gain)
 
     others = [
+        by_chips(halves[0], 2),
+        by_chips(halves[1], -2),
         by_chips(first, 1),
         by_chips(first, -1),
-        by_chips(halves[0], 2),
-        by_chips(halves[1], -2),
     ]
     first, xn = lax.optimization_barrier((first, xn))
-    weights = jnp.concatenate([first] + others, axis=0)
-    sibling = swap(weights)
+    weights = [jnp.concatenate([first] + others[:2], axis=0), jnp.concatenate(others[2:], axis=0)]
+    siblings = [swap(x) for x in weights]
 
     pay, kid = kernel(
         project,
         2,
         12,
         (shape(ROWS, 256), shape(24, ROWS, dtype=F32)),
-        [SMEM] + [VMEM] * 4,
+        [SMEM] + [VMEM] * 6,
         [pltpu.VMEM((D, 256), BF)],
-    )(scal, xn, weights, sibling, states)
+    )(scal, xn, *weights, *siblings, states)
     q = kernel(
         query,
         5,

time: 152 us -> 156 us (1.026)
  starting transfers between devices: 82.8 us -> 91.1 us
  Pallas kernels: 13.1 us -> 8.57 us
  local copies, waits for them, and re-layouts: 7.94 us -> 5.48 us
    ppermute x2, starting transfers between devices: 5.5 us -> 12.5 us  [shards(): moved.append(lax.ppermute(part, 'pipe', [(i, i + 1) for i in range(3)]))]
    ppermute x12, waiting for transfers between devices: 19.6 us -> 23.5 us  [by_chips(): lax.ppermute(x, 'ctx', [(i, (i + 2 * k) % (2 * CHIPS)) for i in range(2 *...]
    pallas_call x1, Pallas kernels: 4.34 us -> 0.62 us  [shards(): kernel(query, 5, 52, shape(ROWS, COLS), [SMEM, VMEM, ANY], [pltpu.VMEM((D...]
    unnamed x27 -> x30, local copies, waits for them, and re-layouts: 5.89 us -> 2.28 us
    pallas_call x2, Pallas kernels: 5.75 us -> 2.44 us  [shards(): kernel(body, us, 20, shape(ROWS, cols), [SMEM] + [VMEM] * 9)]
    pallas_call x1, Pallas kernels: 1.05 us -> 4.04 us  [shards(): kernel(front, 4, 20, (shape(ROWS, D), shape(ROWS, 256), shape(ROWS, COLS,...]
    ppermute x2, waiting for transfers between devices: 3.5 us -> 1.16 us  [shards(): moved.append(lax.ppermute(part, 'pipe', [(i, i + 1) for i in range(3)]))]
    ppermute x2 -> x3, starting transfers between devices: 3.84 us -> 5.77 us  [swap(): return lax.ppermute(x, 'ctx', [(i, i ^ 1) for i in range(2 * CHIPS)])]
  transfers between devices with their start and end apart: 18 -> 19, of which waited for: 9 -> 8; matrix products, arithmetic and copies ran while one was open for 9% -> 7% of each run, Pallas kernels for 6% -> 4%
where the time goes in v7:
time: 156 us; the launch traced here: 155 us
  starting transfers between devices  91.1 us (58%)
  waiting for transfers between devices  27.4 us (18%)
  between operations  15.2 us (10%)
  Pallas kernels  8.57 us (5%)
  other arithmetic  6.71 us (4%)
  local copies, waits for them, and re-layouts  5.48 us (4%)
    ppermute x12, starting transfers between devices, by_chips(): lax.ppermute(x, 'ctx', [(i, (i + 2 * k) % (2 * CHIPS)) for i in range(2 *...  68 us
    ppermute x12, waiting for transfers between devices, by_chips(): lax.ppermute(x, 'ctx', [(i, (i + 2 * k) % (2 * CHIPS)) for i in range(2 *...  23.5 us
    ppermute x2, starting transfers between devices, shards(): moved.append(lax.ppermute(part, 'pipe', [(i, i + 1) for i in range(3)]))  12.5 us
    ppermute x3, starting transfers between devices, swap(): return lax.ppermute(x, 'ctx', [(i, i ^ 1) for i in range(2 * CHIPS)])  5.77 us
    all_to_all x1, starting transfers between devices, shards(): got = lax.all_to_all(parts, 'tp', 0, 0)  4.8 us
    pallas_call x1, Pallas kernels, shards(): kernel(front, 4, 20, (shape(ROWS, D), shape(ROWS, 256), shape(ROWS, COLS,...  4.04 us
  transfers between devices with their start and end apart: 19, of which 8 were waited for; matrix products, arithmetic and copies ran while one was open for 7% of the time, Pallas kernels for 4%

profile of v7, /device:TPU:12, one launch (start us, length us, event | category | flops | bytes accessed | tf_op | source)
XLA Modules:
  0.0 154.5 jit_solution(2920672687129636861)
XLA Ops:
  7.2 0.0 copy-start.9
  7.2 0.0 copy-start.8
  7.2 0.0 all-gather.3.cloned.1.call-start
  7.2 0.7 all-gather.3.cloned.1.call-update
  7.9 0.7 convert_bitcast_fusion.1
  8.6 0.8 pad_maximum_fusion.4
  9.4 9.1 %collective-permute-start = (bf16[144,256]{1,0:T(8,128)(2,1)S(1)}, bf16[144,256]{1,0:T(8,128)(2,1)S(1)}, u32[]{:S(2)}, u32[]{:S(2)}) collective-permute-start(bf16[144,256]{1,0:T(8,128)(2,1)S(1)} %pad_maximum_fusion.4), channel_id=1, source_target_pairs={{0,32},{4,36},{8,40},{12,44},{16,48},{20,52},{24,56},{28,60},{32,6... | collective-permute-start | bytes 221192 | tf_op jit(solution)/shard_map/ppermute | solution.py:282
  18.5 5.6 %collective-permute-start.1 = (bf16[144,256]{1,0:T(8,128)(2,1)S(1)}, bf16[144,256]{1,0:T(8,128)(2,1)S(1)}, u32[]{:S(2)}, u32[]{:S(2)}) collective-permute-start(bf16[144,256]{1,0:T(8,128)(2,1)S(1)} %pad_maximum_fusion.4), channel_id=1, source_target_pairs={{0,96},{4,100},{8,104},{12,108},{16,112},{20,116},{24,120},{28,124... | collective-permute-start | bytes 221192 | tf_op jit(solution)/shard_map/ppermute | solution.py:282
  24.0 10.8 %collective-permute-start.2 = (bf16[144,256]{1,0:T(8,128)(2,1)S(1)}, bf16[144,256]{1,0:T(8,128)(2,1)S(1)}, u32[]{:S(2)}, u32[]{:S(2)}) collective-permute-start(bf16[144,256]{1,0:T(8,128)(2,1)S(1)} %pad_maximum_fusion.4), channel_id=1, source_target_pairs={{0,64},{4,68},{8,72},{12,76},{16,80},{20,84},{24,88},{28,92},{32,9... | collective-permute-start | bytes 221192 | tf_op jit(solution)/shard_map/ppermute | solution.py:282
  34.9 0.1 pad.31.clone
  35.0 0.7 reduce-precision_convert_fusion.1
  35.7 0.1 maximum_maximum_fusion
  35.8 1.1 broadcast_in_dim.32
  36.8 0.9 broadcast_in_dim.33
  37.7 2.2 %pad_maximum_fusion = bf16[4,192,1024]{2,1,0:T(8,128)(2,1)} fusion(bf16[4,16,1024]{2,1,0:T(8,128)(2,1)S(1)} %broadcast_in_dim.35, bf16[4,32,1024]{2,1,0:T(8,128)(2,1)S(1)} %broadcast_in_dim.33, bf16[4,16,1024]{2,1,0:T(8,128)(2,1)} %bitcast.35, bf16[4,128,1024]{2,1,0:T(8,128)(2,1)S(1)} %broadcast_in_dim.32), kind=kLoop, calls=%fused_computation | loop fusion | flops 6291456 | bytes 3145728 | tf_op jit(solution)/shard_map/concatenate | solution.py:318
  39.9 0.0 collective-permute-done
  40.0 0.0 collective-permute-done.1
  40.0 0.0 collective-permute-done.2
  40.0 0.8 pad_maximum_fusion.2
  40.8 4.8 %all-to-all-start = ((bf16[4,192,1024]{2,1,0:T(8,128)(2,1)}), bf16[4,192,1024]{2,1,0:T(8,128)(2,1)S(1)}, u32[]{:S(2)}, u32[]{:S(2)}) async-start(bf16[4,192,1024]{2,1,0:T(8,128)(2,1)} %pad_maximum_fusion), calls=%async_computation | async-start | bytes 3145728 | tf_op jit(solution)/shard_map/all_to_all | solution.py:333
  45.6 9.1 %collective-permute-start.5 = (bf16[576,256]{1,0:T(8,128)(2,1)S(1)}, bf16[576,256]{1,0:T(8,128)(2,1)S(1)}, u32[]{:S(2)}, u32[]{:S(2)}) collective-permute-start(bf16[576,256]{1,0:T(8,128)(2,1)S(1)} %constant_dynamic-update-slice_fusion), channel_id=1, source_target_pairs={{0,8},{4,12},{8,16},{12,20},{16,24},{20,28},{24,32},{28,36},{32,40... | collective-permute-start | bytes 884744 | tf_op jit(solution)/shard_map/ppermute | solution.py:282
  54.8 4.4 %collective-permute-start.6 = (bf16[576,256]{1,0:T(8,128)(2,1)S(1)}, bf16[576,256]{1,0:T(8,128)(2,1)S(1)}, u32[]{:S(2)}, u32[]{:S(2)}) collective-permute-start(bf16[576,256]{1,0:T(8,128)(2,1)S(1)} %constant_dynamic-update-slice_fusion), channel_id=1, source_target_pairs={{0,120},{4,124},{8,0},{12,4},{16,8},{20,12},{24,16},{28,20},{32,24... | collective-permute-start | bytes 884744 | tf_op jit(solution)/shard_map/ppermute | solution.py:282
  59.8 0.1 copy.14.idc_ref
  59.9 0.1 stack.22.scal.refs_0_
  60.0 1.9 %collective-permute-start.3 = (bf16[288,256]{1,0:T(8,128)(2,1)}, bf16[288,256]{1,0:T(8,128)(2,1)}, u32[]{:S(2)}, u32[]{:S(2)}) collective-permute-start(bf16[288,256]{1,0:T(8,128)(2,1)} %get-tuple-element.29), channel_id=1, source_target_pairs={{0,16},{4,20},{8,24},{12,28},{16,32},{20,36},{24,40},{28,44},{32,4... | collective-permute-start | bytes 442376 | tf_op jit(solution)/shard_map/ppermute | solution.py:282
  62.0 6.0 %collective-permute-start.4 = (bf16[288,256]{1,0:T(8,128)(2,1)}, bf16[288,256]{1,0:T(8,128)(2,1)}, u32[]{:S(2)}, u32[]{:S(2)}) collective-permute-start(bf16[288,256]{1,0:T(8,128)(2,1)} %get-tuple-element.30), channel_id=1, source_target_pairs={{0,112},{4,116},{8,120},{12,124},{16,0},{20,4},{24,8},{28,12},{32,... | collective-permute-start | bytes 442376 | tf_op jit(solution)/shard_map/ppermute | solution.py:282
  68.0 3.5 %collective-permute-done.5 = bf16[576,256]{1,0:T(8,128)(2,1)S(1)} collective-permute-done((bf16[576,256]{1,0:T(8,128)(2,1)S(1)}, bf16[576,256]{1,0:T(8,128)(2,1)S(1)}, u32[]{:S(2)}, u32[]{:S(2)}) %collective-permute-start.5) | collective-permute-done | bytes 294944 | tf_op jit(solution)/shard_map/ppermute | solution.py:282
  71.5 2.2 %collective-permute-done.6 = bf16[576,256]{1,0:T(8,128)(2,1)S(1)} collective-permute-done((bf16[576,256]{1,0:T(8,128)(2,1)S(1)}, bf16[576,256]{1,0:T(8,128)(2,1)S(1)}, u32[]{:S(2)}, u32[]{:S(2)}) %collective-permute-start.6) | collective-permute-done | bytes 294944 | tf_op jit(solution)/shard_map/ppermute | solution.py:282
  73.7 1.9 %collective-permute-start.8 = (bf16[1152,256]{1,0:T(8,128)(2,1)S(1)}, bf16[1152,256]{1,0:T(8,128)(2,1)S(1)}, u32[]{:S(2)}, u32[]{:S(2)}) collective-permute-start(bf16[1152,256]{1,0:T(8,128)(2,1)S(1)} %constant_dynamic-update-slice_fusion.7.own_b), channel_id=1, source_target_pairs={{0,4},{4,0},{8,12},{12,8},{16,20},{20,16},{24,28},{28,24},{32,36},... | collective-permute-start | bytes 1769480 | tf_op jit(solution)/shard_map/ppermute | solution.py:286
  75.7 0.0 all-to-all-done.got
  75.7 4.0 %front.1 = (bf16[128,4096]{1,0:T(8,128)(2,1)S(1)}, bf16[128,256]{1,0:T(8,128)(2,1)S(1)}, f32[128,1024]{1,0:T(8,128)S(1)}, f32[128,128]{1,0:T(8,128)S(1)}) custom-call(s32[5]{0:T(128)S(1)} %stack.22.scal.refs_0_, bf16[4,192,1024]{2,1,0:T(8,128)(2,1)S(1)} %all-to-all-done.got, f32[128,1]{1,0:T(8,128)S(1)} %copy.14.idc_ref, ...), custom_call_target="tpu_custom_call" | custom-call | flops 4600000000 | bytes 1048576 | tf_op jit(solution)/shard_map/front/pallas_call | solution.py:334
  79.8 1.5 %collective-permute-done.3 = bf16[288,256]{1,0:T(8,128)(2,1)} collective-permute-done((bf16[288,256]{1,0:T(8,128)(2,1)}, bf16[288,256]{1,0:T(8,128)(2,1)}, u32[]{:S(2)}, u32[]{:S(2)}) %collective-permute-start.3) | collective-permute-done | bytes 147488 | tf_op jit(solution)/shard_map/ppermute | solution.py:282
  81.4 0.9 constant_dynamic-update-slice_fusion.5
  82.3 0.0 collective-permute-done.4
  82.3 0.9 constant_dynamic-update-slice_fusion.4.own_a
  83.2 1.9 %collective-permute-start.7 = (bf16[1152,256]{1,0:T(8,128)(2,1)S(1)}, bf16[1152,256]{1,0:T(8,128)(2,1)S(1)}, u32[]{:S(2)}, u32[]{:S(2)}) collective-permute-start(bf16[1152,256]{1,0:T(8,128)(2,1)S(1)} %constant_dynamic-update-slice_fusion.4.own_a), channel_id=1, source_target_pairs={{0,4},{4,0},{8,12},{12,8},{16,20},{20,16},{24,28},{28,24},{32,36},... | collective-permute-start | bytes 1769480 | tf_op jit(solution)/shard_map/ppermute | solution.py:286
  85.1 0.0 collective-permute-done.8.sib_b
  85.1 2.0 %collective-permute-done.7.sib_a = bf16[1152,256]{1,0:T(8,128)(2,1)S(1)} collective-permute-done((bf16[1152,256]{1,0:T(8,128)(2,1)S(1)}, bf16[1152,256]{1,0:T(8,128)(2,1)S(1)}, u32[]{:S(2)}, u32[]{:S(2)}) %collective-permute-start.7) | collective-permute-done | bytes 589856 | tf_op jit(solution)/shard_map/ppermute | solution.py:286
  87.1 0.6 project.1
  87.7 7.2 %collective-permute-start.10 = (bf16[128,256]{1,0:T(8,128)(2,1)S(1)}, bf16[128,256]{1,0:T(8,128)(2,1)S(1)}, u32[]{:S(2)}, u32[]{:S(2)}) collective-permute-start(bf16[128,256]{1,0:T(8,128)(2,1)S(1)} %get-tuple-element.32), channel_id=1, source_target_pairs={{0,64},{4,68},{8,72},{12,76},{16,80},{20,84},{24,88},{28,92},{32,9... | collective-permute-start | bytes 196616 | tf_op jit(solution)/shard_map/ppermute | solution.py:282
  94.9 3.9 %collective-permute-start.9 = (bf16[128,256]{1,0:T(8,128)(2,1)S(1)}, bf16[128,256]{1,0:T(8,128)(2,1)S(1)}, u32[]{:S(2)}, u32[]{:S(2)}) collective-permute-start(bf16[128,256]{1,0:T(8,128)(2,1)S(1)} %get-tuple-element.32), channel_id=1, source_target_pairs={{0,32},{4,36},{8,40},{12,44},{16,48},{20,52},{24,56},{28,60},{32,6... | collective-permute-start | bytes 196616 | tf_op jit(solution)/shard_map/ppermute | solution.py:282
  98.9 11.9 %collective-permute-done.9 = bf16[128,256]{1,0:T(8,128)(2,1)S(1)} collective-permute-done((bf16[128,256]{1,0:T(8,128)(2,1)S(1)}, bf16[128,256]{1,0:T(8,128)(2,1)S(1)}, u32[]{:S(2)}, u32[]{:S(2)}) %collective-permute-start.9) | collective-permute-done | bytes 65568 | tf_op jit(solution)/shard_map/ppermute | solution.py:282
  110.8 2.9 %collective-permute-start.11 = (bf16[256,256]{1,0:T(8,128)(2,1)S(1)}, bf16[256,256]{1,0:T(8,128)(2,1)S(1)}, u32[]{:S(2)}, u32[]{:S(2)}) collective-permute-start(bf16[256,256]{1,0:T(8,128)(2,1)S(1)} %get-tuple-element.48), channel_id=1, source_target_pairs={{0,16},{4,20},{8,24},{12,28},{16,32},{20,36},{24,40},{28,44},{32,4... | collective-permute-start | bytes 393224 | tf_op jit(solution)/shard_map/ppermute | solution.py:282
  113.7 4.5 %collective-permute-start.12 = (bf16[256,256]{1,0:T(8,128)(2,1)S(1)}, bf16[256,256]{1,0:T(8,128)(2,1)S(1)}, u32[]{:S(2)}, u32[]{:S(2)}) collective-permute-start(bf16[256,256]{1,0:T(8,128)(2,1)S(1)} %get-tuple-element.48), channel_id=1, source_target_pairs={{0,8},{4,12},{8,16},{12,20},{16,24},{20,28},{24,32},{28,36},{32,40... | collective-permute-start | bytes 393224 | tf_op jit(solution)/shard_map/ppermute | solution.py:282
  118.2 0.0 collective-permute-done.10
  118.2 2.6 %collective-permute-start.13 = (bf16[256,256]{1,0:T(8,128)(2,1)S(1)}, bf16[256,256]{1,0:T(8,128)(2,1)S(1)}, u32[]{:S(2)}, u32[]{:S(2)}) collective-permute-start(bf16[256,256]{1,0:T(8,128)(2,1)S(1)} %pad_maximum_fusion.3), channel_id=1, source_target_pairs={{0,120},{4,124},{8,0},{12,4},{16,8},{20,12},{24,16},{28,20},{32,24... | collective-permute-start | bytes 393224 | tf_op jit(solution)/shard_map/ppermute | solution.py:282
  120.8 0.0 collective-permute-done.11
  120.9 4.3 %collective-permute-done.12 = bf16[256,256]{1,0:T(8,128)(2,1)S(1)} collective-permute-done((bf16[256,256]{1,0:T(8,128)(2,1)S(1)}, bf16[256,256]{1,0:T(8,128)(2,1)S(1)}, u32[]{:S(2)}, u32[]{:S(2)}) %collective-permute-start.12) | collective-permute-done | bytes 131104 | tf_op jit(solution)/shard_map/ppermute | solution.py:282
  125.2 0.0 collective-permute-done.13
  125.2 1.9 %collective-permute-start.14 = (bf16[1152,256]{1,0:T(8,128)(2,1)S(1)}, bf16[1152,256]{1,0:T(8,128)(2,1)S(1)}, u32[]{:S(2)}, u32[]{:S(2)}) collective-permute-start(bf16[1152,256]{1,0:T(8,128)(2,1)S(1)} %constant_dynamic-update-slice_fusion.11.own), channel_id=1, source_target_pairs={{0,4},{4,0},{8,12},{12,8},{16,20},{20,16},{24,28},{28,24},{32,36},... | collective-permute-start | bytes 1769480 | tf_op jit(solution)/shard_map/ppermute | solution.py:286
  127.2 0.0 all-gather.3.cloned.1.call-done
  127.2 1.2 copy-done.5
  128.4 0.6 query.1.refs_2_
  129.0 0.0 copy-start
  129.1 0.1 collective-permute-done.14.sib
  129.1 0.9 assemble.1
  130.1 1.4 finish_low.1
  131.5 3.5 %collective-permute-start.15 = (bf16[128,768]{1,0:T(8,128)(2,1)S(1)}, bf16[128,768]{1,0:T(8,128)(2,1)S(1)}, u32[]{:S(2)}, u32[]{:S(2)}) collective-permute-start(bf16[128,768]{1,0:T(8,128)(2,1)S(1)} %finish_low.1), channel_id=1, source_target_pairs={{0,128},{128,256},{256,384},{1,129},{129,257},{257,385},{2,130},{1... | collective-permute-start | bytes 589832 | tf_op jit(solution)/shard_map/ppermute | solution.py:403
  135.0 1.0 finish_high.1
  136.0 9.1 %collective-permute-start.16 = (bf16[128,256]{1,0:T(8,128)(2,1)S(1)}, bf16[128,256]{1,0:T(8,128)(2,1)S(1)}, u32[]{:S(2)}, u32[]{:S(2)}) collective-permute-start(bf16[128,256]{1,0:T(8,128)(2,1)S(1)} %finish_high.1), channel_id=1, source_target_pairs={{0,128},{128,256},{256,384},{1,129},{129,257},{257,385},{2,130},{1... | collective-permute-start | bytes 196616 | tf_op jit(solution)/shard_map/ppermute | solution.py:403
  145.1 0.7 maximum_bitcast_fusion
  145.8 1.2 collective-permute-done.16
  146.9 0.0 collective-permute-done.15
  146.9 0.7 maximum_bitcast_fusion.1
  (34 shorter events, 0.2 us)
Async XLA Ops:
  7.2 32.8 %copy-start.9 = (bf16[1,128,128]{2,1,0:T(8,128)(2,1)S(1)}, bf16[1,128,128]{2,1,0:T(8,128)(2,1)}, u32[]{:S(2)}) copy-start(bf16[1,128,128]{2,1,0:T(8,128)(2,1)} %param.17) | copy-start | bytes 98308
  7.2 32.8 %copy-start.8 = (bf16[1,128,128]{2,1,0:T(8,128)(2,1)S(1)}, bf16[1,128,128]{2,1,0:T(8,128)(2,1)}, u32[]{:S(2)}) copy-start(bf16[1,128,128]{2,1,0:T(8,128)(2,1)} %param.18) | copy-start | bytes 98308
  7.2 120.0 %all-gather.3.cloned.1.call-start = ((), (), s32[]{:S(2)}) async-start(), calls=%async_computation.1 | async-start | bytes 8650752 | tf_op jit(solution)/shard_map/all_gather | solution.py:310
  9.4 30.5 %collective-permute-start = (bf16[144,256]{1,0:T(8,128)(2,1)S(1)}, bf16[144,256]{1,0:T(8,128)(2,1)S(1)}, u32[]{:S(2)}, u32[]{:S(2)}) collective-permute-start(bf16[144,256]{1,0:T(8,128)(2,1)S(1)} %pad_maximum_fusion.4), channel_id=1, source_target_pairs={{0,32},{4,36},{8,40},{12,44},{16,48},{20,52},{24,56},{28,60},{32,6... | collective-permute-start | bytes 221192 | tf_op jit(solution)/shard_map/ppermute | solution.py:282
  18.5 21.5 %collective-permute-start.1 = (bf16[144,256]{1,0:T(8,128)(2,1)S(1)}, bf16[144,256]{1,0:T(8,128)(2,1)S(1)}, u32[]{:S(2)}, u32[]{:S(2)}) collective-permute-start(bf16[144,256]{1,0:T(8,128)(2,1)S(1)} %pad_maximum_fusion.4), channel_id=1, source_target_pairs={{0,96},{4,100},{8,104},{12,108},{16,112},{20,116},{24,120},{28,124... | collective-permute-start | bytes 221192 | tf_op jit(solution)/shard_map/ppermute | solution.py:282
  24.0 16.0 %collective-permute-start.2 = (bf16[144,256]{1,0:T(8,128)(2,1)S(1)}, bf16[144,256]{1,0:T(8,128)(2,1)S(1)}, u32[]{:S(2)}, u32[]{:S(2)}) collective-permute-start(bf16[144,256]{1,0:T(8,128)(2,1)S(1)} %pad_maximum_fusion.4), channel_id=1, source_target_pairs={{0,64},{4,68},{8,72},{12,76},{16,80},{20,84},{24,88},{28,92},{32,9... | collective-permute-start | bytes 221192 | tf_op jit(solution)/shard_map/ppermute | solution.py:282
  39.9 35.8 %copy-start.1 = (f32[1,16]{1,0:T(1,128)S(1)}, f32[1,16]{1,0:T(1,128)}, u32[]{:S(2)}) copy-start(f32[1,16]{1,0:T(1,128)} %bias.1) | copy-start | bytes 196
  39.9 35.8 %copy-start.2 = (f32[1,16]{1,0:T(1,128)S(1)}, f32[1,16]{1,0:T(1,128)}, u32[]{:S(2)}) copy-start(f32[1,16]{1,0:T(1,128)} %rate.1) | copy-start | bytes 196
  39.9 35.8 %copy-start.3 = (f32[1,16]{1,0:T(1,128)S(1)}, f32[1,16]{1,0:T(1,128)}, u32[]{:S(2)}) copy-start(f32[1,16]{1,0:T(1,128)} %skip.1) | copy-start | bytes 196
  40.0 35.6 %copy-start.6 = (bf16[576,256]{1,0:T(8,128)(2,1)}, bf16[576,256]{1,0:T(8,128)(2,1)S(1)}, u32[]{:S(2)}) copy-start(bf16[576,256]{1,0:T(8,128)(2,1)S(1)} %constant_dynamic-update-slice_fusion) | copy-start | bytes 884740
  40.8 34.8 %all-to-all-start = ((bf16[4,192,1024]{2,1,0:T(8,128)(2,1)}), bf16[4,192,1024]{2,1,0:T(8,128)(2,1)S(1)}, u32[]{:S(2)}, u32[]{:S(2)}) async-start(bf16[4,192,1024]{2,1,0:T(8,128)(2,1)} %pad_maximum_fusion), calls=%async_computation | async-start | bytes 3145728 | tf_op jit(solution)/shard_map/all_to_all | solution.py:333
  45.6 25.9 %collective-permute-start.5 = (bf16[576,256]{1,0:T(8,128)(2,1)S(1)}, bf16[576,256]{1,0:T(8,128)(2,1)S(1)}, u32[]{:S(2)}, u32[]{:S(2)}) collective-permute-start(bf16[576,256]{1,0:T(8,128)(2,1)S(1)} %constant_dynamic-update-slice_fusion), channel_id=1, source_target_pairs={{0,8},{4,12},{8,16},{12,20},{16,24},{20,28},{24,32},{28,36},{32,40... | collective-permute-start | bytes 884744 | tf_op jit(solution)/shard_map/ppermute | solution.py:282
  54.8 18.9 %collective-permute-start.6 = (bf16[576,256]{1,0:T(8,128)(2,1)S(1)}, bf16[576,256]{1,0:T(8,128)(2,1)S(1)}, u32[]{:S(2)}, u32[]{:S(2)}) collective-permute-start(bf16[576,256]{1,0:T(8,128)(2,1)S(1)} %constant_dynamic-update-slice_fusion), channel_id=1, source_target_pairs={{0,120},{4,124},{8,0},{12,4},{16,8},{20,12},{24,16},{28,20},{32,24... | collective-permute-start | bytes 884744 | tf_op jit(solution)/shard_map/ppermute | solution.py:282
  60.0 21.3 %collective-permute-start.3 = (bf16[288,256]{1,0:T(8,128)(2,1)}, bf16[288,256]{1,0:T(8,128)(2,1)}, u32[]{:S(2)}, u32[]{:S(2)}) collective-permute-start(bf16[288,256]{1,0:T(8,128)(2,1)} %get-tuple-element.29), channel_id=1, source_target_pairs={{0,16},{4,20},{8,24},{12,28},{16,32},{20,36},{24,40},{28,44},{32,4... | collective-permute-start | bytes 442376 | tf_op jit(solution)/shard_map/ppermute | solution.py:282
  62.0 20.3 %collective-permute-start.4 = (bf16[288,256]{1,0:T(8,128)(2,1)}, bf16[288,256]{1,0:T(8,128)(2,1)}, u32[]{:S(2)}, u32[]{:S(2)}) collective-permute-start(bf16[288,256]{1,0:T(8,128)(2,1)} %get-tuple-element.30), channel_id=1, source_target_pairs={{0,112},{4,116},{8,120},{12,124},{16,0},{20,4},{24,8},{28,12},{32,... | collective-permute-start | bytes 442376 | tf_op jit(solution)/shard_map/ppermute | solution.py:282
  73.7 11.4 %collective-permute-start.8 = (bf16[1152,256]{1,0:T(8,128)(2,1)S(1)}, bf16[1152,256]{1,0:T(8,128)(2,1)S(1)}, u32[]{:S(2)}, u32[]{:S(2)}) collective-permute-start(bf16[1152,256]{1,0:T(8,128)(2,1)S(1)} %constant_dynamic-update-slice_fusion.7.own_b), channel_id=1, source_target_pairs={{0,4},{4,0},{8,12},{12,8},{16,20},{20,16},{24,28},{28,24},{32,36},... | collective-permute-start | bytes 1769480 | tf_op jit(solution)/shard_map/ppermute | solution.py:286
  75.7 4.1 %copy-start.7 = (bf16[576,256]{1,0:T(8,128)(2,1)S(1)}, bf16[576,256]{1,0:T(8,128)(2,1)}, u32[]{:S(2)}) copy-start(bf16[576,256]{1,0:T(8,128)(2,1)} %copy-done.6) | copy-start | bytes 884740
  79.8 7.9 %copy-start.4 = (bf16[128,4096]{1,0:T(8,128)(2,1)}, bf16[128,4096]{1,0:T(8,128)(2,1)S(1)}, u32[]{:S(2)}) copy-start(bf16[128,4096]{1,0:T(8,128)(2,1)S(1)} %get-tuple-element.27.xn) | copy-start | bytes 3145732
  83.2 3.9 %collective-permute-start.7 = (bf16[1152,256]{1,0:T(8,128)(2,1)S(1)}, bf16[1152,256]{1,0:T(8,128)(2,1)S(1)}, u32[]{:S(2)}, u32[]{:S(2)}) collective-permute-start(bf16[1152,256]{1,0:T(8,128)(2,1)S(1)} %constant_dynamic-update-slice_fusion.4.own_a), channel_id=1, source_target_pairs={{0,4},{4,0},{8,12},{12,8},{16,20},{20,16},{24,28},{28,24},{32,36},... | collective-permute-start | bytes 1769480 | tf_op jit(solution)/shard_map/ppermute | solution.py:286
  87.7 30.5 %collective-permute-start.10 = (bf16[128,256]{1,0:T(8,128)(2,1)S(1)}, bf16[128,256]{1,0:T(8,128)(2,1)S(1)}, u32[]{:S(2)}, u32[]{:S(2)}) collective-permute-start(bf16[128,256]{1,0:T(8,128)(2,1)S(1)} %get-tuple-element.32), channel_id=1, source_target_pairs={{0,64},{4,68},{8,72},{12,76},{16,80},{20,84},{24,88},{28,92},{32,9... | collective-permute-start | bytes 196616 | tf_op jit(solution)/shard_map/ppermute | solution.py:282
  94.9 15.9 %collective-permute-start.9 = (bf16[128,256]{1,0:T(8,128)(2,1)S(1)}, bf16[128,256]{1,0:T(8,128)(2,1)S(1)}, u32[]{:S(2)}, u32[]{:S(2)}) collective-permute-start(bf16[128,256]{1,0:T(8,128)(2,1)S(1)} %get-tuple-element.32), channel_id=1, source_target_pairs={{0,32},{4,36},{8,40},{12,44},{16,48},{20,52},{24,56},{28,60},{32,6... | collective-permute-start | bytes 196616 | tf_op jit(solution)/shard_map/ppermute | solution.py:282
  110.8 10.0 %collective-permute-start.11 = (bf16[256,256]{1,0:T(8,128)(2,1)S(1)}, bf16[256,256]{1,0:T(8,128)(2,1)S(1)}, u32[]{:S(2)}, u32[]{:S(2)}) collective-permute-start(bf16[256,256]{1,0:T(8,128)(2,1)S(1)} %get-tuple-element.48), channel_id=1, source_target_pairs={{0,16},{4,20},{8,24},{12,28},{16,32},{20,36},{24,40},{28,44},{32,4... | collective-permute-start | bytes 393224 | tf_op jit(solution)/shard_map/ppermute | solution.py:282
  113.7 11.5 %collective-permute-start.12 = (bf16[256,256]{1,0:T(8,128)(2,1)S(1)}, bf16[256,256]{1,0:T(8,128)(2,1)S(1)}, u32[]{:S(2)}, u32[]{:S(2)}) collective-permute-start(bf16[256,256]{1,0:T(8,128)(2,1)S(1)} %get-tuple-element.48), channel_id=1, source_target_pairs={{0,8},{4,12},{8,16},{12,20},{16,24},{20,28},{24,32},{28,36},{32,40... | collective-permute-start | bytes 393224 | tf_op jit(solution)/shard_map/ppermute | solution.py:282
  118.2 7.0 %collective-permute-start.13 = (bf16[256,256]{1,0:T(8,128)(2,1)S(1)}, bf16[256,256]{1,0:T(8,128)(2,1)S(1)}, u32[]{:S(2)}, u32[]{:S(2)}) collective-permute-start(bf16[256,256]{1,0:T(8,128)(2,1)S(1)} %pad_maximum_fusion.3), channel_id=1, source_target_pairs={{0,120},{4,124},{8,0},{12,4},{16,8},{20,12},{24,16},{28,20},{32,24... | collective-permute-start | bytes 393224 | tf_op jit(solution)/shard_map/ppermute | solution.py:282
  125.2 3.9 %collective-permute-start.14 = (bf16[1152,256]{1,0:T(8,128)(2,1)S(1)}, bf16[1152,256]{1,0:T(8,128)(2,1)S(1)}, u32[]{:S(2)}, u32[]{:S(2)}) collective-permute-start(bf16[1152,256]{1,0:T(8,128)(2,1)S(1)} %constant_dynamic-update-slice_fusion.11.own), channel_id=1, source_target_pairs={{0,4},{4,0},{8,12},{12,8},{16,20},{20,16},{24,28},{28,24},{32,36},... | collective-permute-start | bytes 1769480 | tf_op jit(solution)/shard_map/ppermute | solution.py:286
  127.2 1.2 copy-start.5
  129.0 1.0 copy-start
  131.5 15.4 %collective-permute-start.15 = (bf16[128,768]{1,0:T(8,128)(2,1)S(1)}, bf16[128,768]{1,0:T(8,128)(2,1)S(1)}, u32[]{:S(2)}, u32[]{:S(2)}) collective-permute-start(bf16[128,768]{1,0:T(8,128)(2,1)S(1)} %finish_low.1), channel_id=1, source_target_pairs={{0,128},{128,256},{256,384},{1,129},{129,257},{257,385},{2,130},{1... | collective-permute-start | bytes 589832 | tf_op jit(solution)/shard_map/ppermute | solution.py:403
  136.0 11.0 %collective-permute-start.16 = (bf16[128,256]{1,0:T(8,128)(2,1)S(1)}, bf16[128,256]{1,0:T(8,128)(2,1)S(1)}, u32[]{:S(2)}, u32[]{:S(2)}) collective-permute-start(bf16[128,256]{1,0:T(8,128)(2,1)S(1)} %finish_high.1), channel_id=1, source_target_pairs={{0,128},{128,256},{256,384},{1,129},{129,257},{257,385},{2,130},{1... | collective-permute-start | bytes 196616 | tf_op jit(solution)/shard_map/ppermute | solution.py:403
Sparse Core Ops, SparseCore 0:
  10.1 105.6 all-gather.2
